TPU v7x, 32 devices: a whole 2x2x4 slice. The times are simulated.
32 devices in a mesh: dp: 4 (over y, x), expert: 8 (over z, core).
Axes of the slice: x: 2, y: 2, z: 4, core: 2. Of those that a mesh axis runs over, the one named last changes fastest.
Arguments:
- tokens: bfloat16 [4096, 1024], P(('dp', 'expert')), may hold values from -6 to 6
- cotangent: bfloat16 [4096, 1024], P(('dp', 'expert')), may hold values from -6 to 6
- seq_lengths: int32 [32, 2], P(('dp', 'expert')), may hold values from 0 to 128, as said below
- routes: int32 [4096, 16], P(('dp', 'expert')), may hold values from 0 to 47, all different within a row; in each aligned block of 128 rows (0 to 127, 128 to 255, ...) at most 64 rows name the same one
- head_experts: int32 [4096, 4, 2], P(('dp', 'expert')), may hold values from 0 to 4, all different within a row
- norm_gain: float32 [1024], replicated, may hold values from 0.25 to 1.75
- w_query: bfloat16 [1024, 512], replicated, may hold values from -0.1875 to 0.1875
- w_key: bfloat16 [1024, 512], replicated, may hold values from -0.1875 to 0.1875
- w_value: bfloat16 [1024, 2560], replicated, may hold values from -0.1875 to 0.1875
- w_output: bfloat16 [1024, 2560], replicated, may hold values from -2 to 2
- w_value_gate: bfloat16 [1024, 20], replicated, may hold values from -0.125 to 0.125
- w_output_gate: bfloat16 [1024, 20], replicated, may hold values from -0.125 to 0.125
- w_router: bfloat16 [1024, 48], replicated, may hold values from -0.0625 to 0.0625
- w_up: bfloat16 [48, 1024, 128], P('expert'), may hold values from -0.1875 to 0.1875
- w_down: bfloat16 [48, 1024, 128], P('expert'), may hold values from -0.5 to 0.5
Outputs:
- mixed: bfloat16 [4096, 1024], P(('dp', 'expert'))
- grad_tokens: float32 [4096, 1024], P(('dp', 'expert'))
- grad_gain: float32 [1024], P(('dp', 'expert'))
- grad_query: float32 [1024, 512], P(('dp', 'expert'))
- grad_key: float32 [1024, 512], P(('dp', 'expert'))
- grad_value: float32 [1024, 2560], P(('dp', 'expert'))
- grad_output: float32 [1024, 2560], P(('dp', 'expert'))
- grad_value_gate: float32 [1024, 20], P(('dp', 'expert'))
- grad_output_gate: float32 [1024, 20], P(('dp', 'expert'))
- grad_router: float32 [1024, 48], P(('dp', 'expert'))
- grad_up: float32 [48, 1024, 128], P('expert', 'dp')
- grad_down: float32 [48, 1024, 128], P('expert', 'dp')
Inputs may be any that keep to these rules, and one draw needn't show every extreme that they name: `seq_lengths`: row r lists the lengths of the one or two sequences packed from the start of device block r; each row sums to at most 128, rows past the sum are padding, and in every draw some block holds one sequence of exactly 128 rows. The 16 experts of a token differ. Within the rows of one device block no expert is named by more than 64 routes, and in every draw some expert is named by exactly 64 routes of some block. `head_experts`: the two experts of a token and head differ.
All inputs are finite; a program needn't handle non-finite values.
Results may differ from a plain program's by a relative error of at most 0.013.
Values may be sent and summed in bfloat16 or wider, within the bound.
A program may use at most 192 MiB of HBM per device.

v0:
```python
import jax
import jax.numpy as jnp
from jax import lax
from jax.sharding import PartitionSpec as P

D = 1024
H = 4
DH = 128
EA = 5
TOPK = 16


norm_eps = 1e-05
rope_base = 10000.0
masked_score = -1e30


def sequence_layout(lengths, count):
    bounds = jnp.cumsum(lengths)
    starts = bounds - lengths
    places = jnp.arange(count, dtype=jnp.int32)
    seq_ids = jnp.sum((places[:, None] >= bounds[None, :]).astype(jnp.int32), axis=1)
    live = places < bounds[-1]
    slot_ids = jnp.arange(lengths.shape[0], dtype=jnp.int32)
    first = jnp.sum(jnp.where(seq_ids[:, None] == slot_ids[None, :], starts[None, :], 0), axis=1)
    positions = jnp.where(live, places - first, 0)
    return (seq_ids, live, positions)


def rope_tables(positions, width):
    half = width // 2
    freq = rope_base ** (-(jnp.arange(half, dtype=jnp.float32) * 2.0 / width))
    angles = positions.astype(jnp.float32)[:, None] * freq[None, :]
    return (jnp.cos(angles), jnp.sin(angles))


def rotate(field, cosine, sine):
    half = field.shape[-1] // 2
    first, second = (field[..., :half], field[..., half:])
    cos_h, sin_h = (cosine[:, None, :], sine[:, None, :])
    return jnp.concatenate(
        [first * cos_h - second * sin_h, second * cos_h + first * sin_h], axis=-1
    )


def rotate_back(field, cosine, sine):
    half = field.shape[-1] // 2
    first, second = (field[..., :half], field[..., half:])
    cos_h, sin_h = (cosine[:, None, :], sine[:, None, :])
    return jnp.concatenate(
        [first * cos_h + second * sin_h, second * cos_h - first * sin_h], axis=-1
    )


def slot_tables(routes, experts, most):
    count = routes.shape[0] * routes.shape[1]
    flat = routes.reshape(count)
    order = jnp.argsort(flat, stable=True)
    ordered = flat[order]
    firsts = jnp.searchsorted(ordered, jnp.arange(experts, dtype=jnp.int32))
    ranks = jnp.arange(count, dtype=jnp.int32) - firsts[ordered]
    sorted_slots = ordered * most + ranks
    slot_of_row = jnp.zeros((count,), jnp.int32).at[order].set(sorted_slots)
    row_of_slot = jnp.full((experts * most,), count, jnp.int32).at[sorted_slots].set(order)
    return (slot_of_row, row_of_slot)


def per_device(
    tokens,
    cotangent,
    seq_lengths,
    routes,
    head_experts,
    norm_gain,
    w_query,
    w_key,
    w_value,
    w_output,
    w_value_gate,
    w_output_gate,
    w_router,
    w_up,
    w_down,
):
    f32 = jnp.float32
    bf16 = jnp.bfloat16
    count = tokens.shape[0]
    experts = w_router.shape[1]
    local_experts = w_up.shape[0]
    owners = lax.axis_size("expert")
    most = 3 * count * TOPK // (2 * experts)
    routed = count * TOPK
    block = min(512, count)
    block_starts = jnp.arange(count // block, dtype=jnp.int32) * block
    scale = DH ** (-0.5)
    contract_last = (((1,), (1,)), ((), ()))
    contract_first = (((0,), (0,)), ((), ()))
    seq_ids, live, positions = sequence_layout(seq_lengths[0], count)
    cosine, sine = rope_tables(positions, DH)
    inputs = tokens.astype(f32)
    centred = inputs - jnp.mean(inputs, axis=-1, keepdims=True)
    inverse = lax.rsqrt(jnp.mean(centred * centred, axis=-1, keepdims=True) + norm_eps)
    standard = centred * inverse
    normed = (standard * norm_gain).astype(bf16)
    query_proj = jnp.dot(normed, w_query, preferred_element_type=f32).reshape(count, H, DH)
    key_proj = jnp.dot(normed, w_key, preferred_element_type=f32).reshape(count, H, DH)
    query_rot = (rotate(query_proj, cosine, sine) * scale).astype(bf16)
    key_rot = rotate(key_proj, cosine, sine).astype(bf16)
    chosen = jnp.any(
        head_experts[:, None, :, :] == jnp.arange(EA, dtype=jnp.int32)[None, :, None, None], axis=-1
    )
    value_gates = jnp.where(
        chosen,
        jax.nn.sigmoid(
            jnp.dot(tokens, w_value_gate, preferred_element_type=f32).reshape(count, EA, H)
        ),
        0.0,
    )
    output_gates = jnp.where(
        chosen,
        jax.nn.sigmoid(
            jnp.dot(tokens, w_output_gate, preferred_element_type=f32).reshape(count, EA, H)
        ),
        0.0,
    )
    value_all = jnp.dot(tokens, w_value, preferred_element_type=f32).reshape(count, EA, H, DH)
    values = jnp.sum(value_gates[..., None] * value_all, axis=1).astype(bf16)

    def allowed_at(start):
        queries = start + jnp.arange(block, dtype=jnp.int32)
        keys = jnp.arange(count, dtype=jnp.int32)
        same = (
            (seq_ids[:, None] == seq_ids[None, :])
            & (keys[None, :] <= queries[:, None])
            & live[None, :]
        )
        return same | (keys[None, :] == queries[:, None])

    def scores_at(start):
        scores = jnp.einsum("qhd,khd->hqk", query_rot, key_rot, preferred_element_type=f32)
        return (query_rot, jnp.where(allowed_at(start)[None], scores, masked_score))

    def attend(start):
        query_block, scores = scores_at(start)
        highest = jnp.max(scores, axis=-1, keepdims=True)
        shifted = jnp.exp(scores - highest)
        totals = jnp.sum(shifted, axis=-1, keepdims=True)
        shares = (shifted / totals).astype(bf16)
        result = jnp.einsum("hqk,khd->qhd", shares, values, preferred_element_type=f32)
        return (result, (highest + jnp.log(totals))[..., 0])

    attended, log_totals = lax.map(attend, block_starts)
    attended = attended.reshape(count, H, DH)
    log_totals = jnp.transpose(log_totals, (1, 0, 2)).reshape(H, count)
    heads_mixed = (
        (output_gates[..., None] * attended[:, None]).astype(bf16).reshape(count, EA * H * DH)
    )
    hidden = inputs + lax.dot_general(
        heads_mixed, w_output, contract_last, preferred_element_type=f32
    )
    hidden_low = hidden.astype(bf16)
    logits = jnp.dot(hidden_low, w_router, preferred_element_type=f32)
    gates = jax.nn.sigmoid(jnp.take_along_axis(logits, routes, axis=1))
    slot_of_row, row_of_slot = slot_tables(routes, experts, most)
    valid = row_of_slot < routed
    safe_row = jnp.minimum(row_of_slot, routed - 1)
    source = safe_row // TOPK
    outgoing = jnp.where(valid[:, None], hidden_low[source], jnp.zeros((), bf16)).reshape(
        owners, local_experts, most, D
    )

    def expert_apply(items):
        raised = jnp.einsum("nemd,edf->nemf", items, w_up, preferred_element_type=f32)
        active = jax.nn.silu(raised).astype(bf16)
        lowered = jnp.einsum("nemf,edf->nemd", active, w_down, preferred_element_type=f32).astype(
            bf16
        )
        return (lowered, raised)

    lowered, raised = expert_apply(
        lax.all_to_all(outgoing, "expert", split_axis=0, concat_axis=0, tiled=True)
    )
    returned = lax.all_to_all(lowered, "expert", split_axis=0, concat_axis=0, tiled=True).reshape(
        experts * most, D
    )
    expert_rows = returned[slot_of_row].reshape(count, TOPK, D)
    output = hidden + jnp.sum(gates[..., None] * expert_rows, axis=1)
    mixed = output.astype(bf16)
    grad_out = cotangent.astype(f32) * live[:, None].astype(f32)
    grad_gates = jnp.sum(grad_out[:, None, :] * expert_rows, axis=2)
    gate_flat = gates.reshape(routed)
    grad_outgoing = (
        jnp.where(valid[:, None], gate_flat[safe_row][:, None] * grad_out[source], 0.0)
        .astype(bf16)
        .reshape(owners, local_experts, most, D)
    )
    grad_lowered = lax.all_to_all(grad_outgoing, "expert", split_axis=0, concat_axis=0, tiled=True)
    items = lax.all_to_all(outgoing, "expert", split_axis=0, concat_axis=0, tiled=True)
    raised = expert_apply(items)[1]
    grad_active = jnp.einsum("nemd,edf->nemf", grad_lowered, w_down, preferred_element_type=f32)
    sigmoid_raised = jax.nn.sigmoid(raised)
    grad_raised = (grad_active * sigmoid_raised * (1.0 + raised * (1.0 - sigmoid_raised))).astype(
        bf16
    )
    grad_items = jnp.einsum("nemf,edf->nemd", grad_raised, w_up, preferred_element_type=f32).astype(
        bf16
    )
    active = jax.nn.silu(raised).astype(bf16)
    grad_items, grad_raised, active = (grad_items, grad_raised, active)
    grad_items, grad_raised, active, grad_arrived, arrived = (
        grad_items,
        grad_raised,
        active,
        grad_lowered,
        items,
    )
    grad_up_local = jnp.einsum("nemd,nemf->edf", arrived, grad_raised, preferred_element_type=f32)
    grad_down_local = jnp.einsum("nemd,nemf->edf", grad_arrived, active, preferred_element_type=f32)
    grad_up, grad_down = (
        lax.psum_scatter(
            grad_up_local.astype(jnp.bfloat16), "dp", scatter_dimension=1, tiled=True
        ).astype(jnp.float32),
        lax.psum_scatter(
            grad_down_local.astype(jnp.bfloat16), "dp", scatter_dimension=1, tiled=True
        ).astype(jnp.float32),
    )
    grad_back = lax.all_to_all(
        grad_items, "expert", split_axis=0, concat_axis=0, tiled=True
    ).reshape(experts * most, D)
    grad_hidden = grad_out + jnp.sum(
        grad_back[slot_of_row].reshape(count, TOPK, D), axis=1, dtype=f32
    )
    grad_picked = grad_gates * gates * (1.0 - gates)
    expert_ids = jnp.arange(experts, dtype=jnp.int32)
    grad_logits = jnp.sum(
        jnp.where(routes[:, :, None] == expert_ids[None, None, :], grad_picked[..., None], 0.0),
        axis=1,
    ).astype(bf16)
    grad_router = lax.dot_general(
        hidden_low, grad_logits, contract_first, preferred_element_type=f32
    )
    grad_hidden = grad_hidden + lax.dot_general(
        grad_logits, w_router, contract_last, preferred_element_type=f32
    )
    grad_hidden_low = grad_hidden.astype(bf16)
    grad_output = lax.dot_general(
        grad_hidden_low, heads_mixed, contract_first, preferred_element_type=f32
    )
    grad_mixed = jnp.dot(grad_hidden_low, w_output, preferred_element_type=f32).reshape(
        count, EA, H, DH
    )
    grad_attended = jnp.sum(output_gates[..., None] * grad_mixed, axis=1).astype(bf16)
    grad_out_gates = jnp.sum(grad_mixed * attended[:, None], axis=-1)
    grad_out_logits = (
        jnp.where(chosen, grad_out_gates * output_gates * (1.0 - output_gates), 0.0)
        .astype(bf16)
        .reshape(count, EA * H)
    )

    def attend_back(carry, start):
        grad_keys, grad_vals = carry
        query_block, scores = scores_at(start)
        shares = jnp.exp(scores - log_totals[..., None])
        grad_shares = jnp.einsum("qhd,khd->hqk", grad_attended, values, preferred_element_type=f32)
        centre = jnp.sum(shares * grad_shares, axis=-1, keepdims=True)
        grad_scores = (shares * (grad_shares - centre)).astype(bf16)
        grad_query_block = jnp.einsum(
            "hqk,khd->qhd", grad_scores, key_rot, preferred_element_type=f32
        )
        grad_keys = grad_keys + jnp.einsum(
            "hqk,qhd->khd", grad_scores, query_block, preferred_element_type=f32
        )
        grad_vals = grad_vals + jnp.einsum(
            "hqk,qhd->khd", shares.astype(bf16), grad_attended, preferred_element_type=f32
        )
        return ((grad_keys, grad_vals), grad_query_block)

    zero_heads = jnp.zeros((count, H, DH), f32)
    (grad_keys, grad_vals), grad_queries = lax.scan(
        attend_back, (zero_heads, zero_heads), block_starts
    )
    grad_queries = grad_queries.reshape(count, H, DH)
    grad_query_proj = (
        rotate_back(grad_queries * scale, cosine, sine).astype(bf16).reshape(count, H * DH)
    )
    grad_key_proj = rotate_back(grad_keys, cosine, sine).astype(bf16).reshape(count, H * DH)
    grad_value_all = (
        (value_gates[..., None] * grad_vals[:, None]).astype(bf16).reshape(count, EA * H * DH)
    )
    grad_value_gates = jnp.sum(grad_vals[:, None] * value_all, axis=-1)
    grad_value_logits = (
        jnp.where(chosen, grad_value_gates * value_gates * (1.0 - value_gates), 0.0)
        .astype(bf16)
        .reshape(count, EA * H)
    )
    grad_query = lax.dot_general(
        normed, grad_query_proj, contract_first, preferred_element_type=f32
    )
    grad_key = lax.dot_general(normed, grad_key_proj, contract_first, preferred_element_type=f32)
    grad_value = lax.dot_general(tokens, grad_value_all, contract_first, preferred_element_type=f32)
    grad_value_gate = lax.dot_general(
        tokens, grad_value_logits, contract_first, preferred_element_type=f32
    )
    grad_output_gate = lax.dot_general(
        tokens, grad_out_logits, contract_first, preferred_element_type=f32
    )
    grad_normed = lax.dot_general(
        grad_query_proj, w_query, contract_last, preferred_element_type=f32
    ) + lax.dot_general(grad_key_proj, w_key, contract_last, preferred_element_type=f32)
    grad_gain = jnp.sum(grad_normed * standard, axis=0)
    grad_standard = grad_normed * norm_gain
    grad_tokens = grad_hidden + inverse * (
        grad_standard
        - jnp.mean(grad_standard, axis=-1, keepdims=True)
        - standard * jnp.mean(grad_standard * standard, axis=-1, keepdims=True)
    )
    grad_tokens = (
        grad_tokens
        + lax.dot_general(grad_value_all, w_value, contract_last, preferred_element_type=f32)
        + lax.dot_general(
            grad_value_logits, w_value_gate, contract_last, preferred_element_type=f32
        )
        + lax.dot_general(grad_out_logits, w_output_gate, contract_last, preferred_element_type=f32)
    )
    summed = (
        lax.psum_scatter(grad_gain, ("dp", "expert"), scatter_dimension=0, tiled=True),
        lax.psum_scatter(grad_query, ("dp", "expert"), scatter_dimension=0, tiled=True),
        lax.psum_scatter(grad_key, ("dp", "expert"), scatter_dimension=0, tiled=True),
        lax.psum_scatter(grad_value, ("dp", "expert"), scatter_dimension=0, tiled=True),
        lax.psum_scatter(grad_output, ("dp", "expert"), scatter_dimension=0, tiled=True),
        lax.psum_scatter(grad_value_gate, ("dp", "expert"), scatter_dimension=0, tiled=True),
        lax.psum_scatter(grad_output_gate, ("dp", "expert"), scatter_dimension=0, tiled=True),
        lax.psum_scatter(grad_router, ("dp", "expert"), scatter_dimension=0, tiled=True),
    )
    return (
        mixed,
        grad_tokens,
        summed[0],
        summed[1],
        summed[2],
        summed[3],
        summed[4],
        summed[5],
        summed[6],
        summed[7],
        grad_up,
        grad_down,
    )


def solution(mesh):
    return jax.shard_map(
        per_device,
        mesh=mesh,
        in_specs=(
            P(("dp", "expert"), None),
            P(("dp", "expert"), None),
            P(("dp", "expert"), None),
            P(("dp", "expert"), None),
            P(("dp", "expert"), None, None),
            P(),
            P(),
            P(),
            P(),
            P(),
            P(),
            P(),
            P(),
            P("expert", None, None),
            P("expert", None, None),
        ),
        out_specs=(
            P(("dp", "expert"), None),
            P(("dp", "expert"), None),
            P(("dp", "expert")),
            P(("dp", "expert"), None),
            P(("dp", "expert"), None),
            P(("dp", "expert"), None),
            P(("dp", "expert"), None),
            P(("dp", "expert"), None),
            P(("dp", "expert"), None),
            P(("dp", "expert"), None),
            P("expert", "dp", None),
            P("expert", "dp", None),
        ),
        check_vma=False,
    )
```

profile of v0, /device:TPU:0, one launch (start us, length us, event | category | flops | bytes accessed | tf_op | source)
XLA Modules:
  0.0 1796.3 jit_solution(17162618374152852253)
XLA Ops:
  15.4 11.8 gather_fusion.1
  27.2 9.9 while.35
  44.7 25.7 %subtract_add_fusion = (s32[2048]{0:T(1024)S(1)}, s32[2048]{0:T(1024)S(1)}) fusion(s32[2048]{0:T(1024)S(1)} %get-tuple-element.434, pred[2048]{0:T(1024)(128)(4,1)S(1)} %get-tuple-element.271, pred[2048]{0:T(1024)(128)(4,1)S(1)} %get-tuple-element.270, pred[2048]{0:T(1024)(128)(4,1)S(1)} %get-tuple-element.269, pred[2048]{0:T(1024)(128)(4,1)S(1)} %get-tuple-element.268, ...), kind=kLoop, calls=%fused_computation.207 | loop fusion | flops 90112 | bytes 116900 | tf_op jit(solution)/shard_map/add | solution.py:62
  70.5 8.1 scatter_custom_fusion
  106.3 14.0 gather_fusion.2
  124.1 145.7 %all_to_all.21 = bf16[8,6,64,1024]{3,2,1,0:T(8,128)(2,1)S(1)} all-to-all(bf16[8,6,64,1024]{3,2,1,0:T(8,128)(2,1)S(1)} %broadcast_select_fusion.2), channel_id=1, replica_groups=mesh['dp'=4,'expert'=8] {'expert'}, dimensions={0} | all-to-all | bytes 12582912 | tf_op jit(solution)/shard_map/all_to_all | solution.py:181
  284.4 13.5 gather_fusion.7
  298.8 14.2 gather_fusion.5
  313.1 8.0 scatter_custom_fusion.1
  321.1 101.7 %all-to-all-done.1 = bf16[8,6,64,1024]{3,2,1,0:T(8,128)(2,1)} async-done(((bf16[8,6,64,1024]{3,2,1,0:T(8,128)(2,1)}), bf16[8,6,64,1024]{3,2,1,0:T(8,128)(2,1)}, u32[]{:S(2)}, u32[]{:S(2)}) %all-to-all-start.1) | async-done | bytes 6291488 | tf_op jit(solution)/shard_map/all_to_all | solution.py:183
  422.9 14.6 gather_fusion.3
  440.9 17.4 gather_fusion.4
  464.0 142.1 %all_to_all.22 = bf16[8,6,64,1024]{3,2,1,0:T(8,128)(2,1)S(1)} all-to-all(bf16[8,6,64,1024]{3,2,1,0:T(8,128)(2,1)S(1)} %select_convert_fusion), channel_id=1, replica_groups=mesh['dp'=4,'expert'=8] {'expert'}, dimensions={0} | all-to-all | bytes 12582912 | tf_op jit(solution)/shard_map/all_to_all | solution.py:197
  633.1 125.3 %all-to-all-done.3 = bf16[8,6,64,1024]{3,2,1,0:T(8,128)(2,1)} async-done(((bf16[8,6,64,1024]{3,2,1,0:T(8,128)(2,1)}), bf16[8,6,64,1024]{3,2,1,0:T(8,128)(2,1)}, u32[]{:S(2)}, u32[]{:S(2)}) %all-to-all-start.3) | async-done | bytes 6291488 | tf_op jit(solution)/shard_map/all_to_all | solution.py:227
  758.4 14.6 gather_fusion.6
  827.1 11.5 copy.248
  851.8 38.1 %all-reduce = f32[1024]{0:T(1024)} all-reduce(f32[1024]{0:T(1024)} %get-tuple-element.228), channel_id=2, replica_groups=mesh['dp'=4,'expert'=8] {'dp','expert'}, use_global_device_ids=true, to_apply=%region_25.26.clone | all-reduce | flops 1024 | bytes 8192
  898.9 37.8 %reduce-scatter.30.cloned.1.call-done = f32[32,20]{1,0:T(8,128)} async-done(((f32[1024,20]{1,0:T(8,128)}), f32[32,20]{1,0:T(8,128)}) %reduce-scatter.30.cloned.1.call-update) | async-done | bytes 2576
  938.1 130.7 %reduce-scatter.32.cloned.1.call-done = f32[32,20]{1,0:T(8,128)} async-done(((f32[1024,20]{1,0:T(8,128)}), f32[32,20]{1,0:T(8,128)}) %reduce-scatter.32.cloned.1.call-update) | async-done | bytes 2576
  1070.2 131.5 %reduce-scatter.22.cloned.1.call-done = f32[32,48]{1,0:T(8,128)} async-done(((f32[1024,48]{1,0:T(8,128)}), f32[32,48]{1,0:T(8,128)}) %reduce-scatter.22.cloned.1.call-update) | async-done | bytes 6160 | tf_op jit(solution)/shard_map/reduce_scatter | solution.py:333
  1201.7 136.4 %reduce-scatter.18.cloned.1.call-done = f32[32,512]{1,0:T(8,128)} async-done(((f32[1024,512]{1,0:T(8,128)}), f32[32,512]{1,0:T(8,128)}) %reduce-scatter.18.cloned.1.call-update) | async-done | bytes 65552 | tf_op jit(solution)/shard_map/reduce_scatter | solution.py:328
  1338.1 136.0 %reduce-scatter.16.cloned.1.call-done = f32[32,512]{1,0:T(8,128)} async-done(((f32[1024,512]{1,0:T(8,128)}), f32[32,512]{1,0:T(8,128)}) %reduce-scatter.16.cloned.1.call-update) | async-done | bytes 65552 | tf_op jit(solution)/shard_map/reduce_scatter | solution.py:327
  1474.1 157.2 %reduce-scatter.20.cloned.1.call-done = f32[32,2560]{1,0:T(8,128)} async-done(((f32[1024,2560]{1,0:T(8,128)}), f32[32,2560]{1,0:T(8,128)}) %reduce-scatter.20.cloned.1.call-update) | async-done | bytes 327696 | tf_op jit(solution)/shard_map/reduce_scatter | solution.py:330
  1631.4 158.0 %reduce-scatter.28.cloned.1.call-done = f32[32,2560]{1,0:T(8,128)} async-done(((f32[1024,2560]{1,0:T(8,128)}), f32[32,2560]{1,0:T(8,128)}) %reduce-scatter.28.cloned.1.call-update) | async-done | bytes 327696
  (312 shorter events, 186.6 us)
Async XLA Ops:
  7.2 262.6 %copy-start = (bf16[6,1024,128]{2,1,0:T(8,128)(2,1)S(1)}, bf16[6,1024,128]{2,1,0:T(8,128)(2,1)}, u32[]{:S(2)}) copy-start(bf16[6,1024,128]{2,1,0:T(8,128)(2,1)} %param.30) | copy-start | bytes 4718596
  15.3 64.8 %copy-start.1 = (bf16[128,1024]{1,0:T(8,128)(2,1)S(1)}, bf16[128,1024]{1,0:T(8,128)(2,1)}, u32[]{:S(2)}) copy-start(bf16[128,1024]{1,0:T(8,128)(2,1)} %param.17) | copy-start | bytes 786436
  15.3 65.1 %copy-start.53 = (s32[128,4,2]{0,2,1:T(2,128)S(1)}, s32[128,4,2]{0,2,1:T(2,128)}, u32[]{:S(2)}) copy-start(s32[128,4,2]{0,2,1:T(2,128)} %param.21) | copy-start | bytes 12292
  15.3 65.2 %copy-start.37 = (bf16[1024,20]{0,1:T(8,128)(2,1)S(1)}, bf16[1024,20]{0,1:T(8,128)(2,1)}, u32[]{:S(2)}) copy-start(bf16[1024,20]{0,1:T(8,128)(2,1)} %param.27) | copy-start | bytes 122884
  27.1 53.6 %copy-start.39 = (bf16[1024,20]{0,1:T(8,128)(2,1)S(1)}, bf16[1024,20]{0,1:T(8,128)(2,1)}, u32[]{:S(2)}) copy-start(bf16[1024,20]{0,1:T(8,128)(2,1)} %param.28) | copy-start | bytes 122884
  27.2 54.5 %copy-start.14 = (bf16[1024,512]{1,0:T(8,128)(2,1)S(1)}, bf16[1024,512]{1,0:T(8,128)(2,1)}, u32[]{:S(2)}) copy-start(bf16[1024,512]{1,0:T(8,128)(2,1)} %param.24) | copy-start | bytes 3145732
  27.2 54.5 %copy-start.41 = (f32[1024]{0:T(1024)S(1)}, f32[1024]{0:T(1024)}, u32[]{:S(2)}) copy-start(f32[1024]{0:T(1024)} %param.22) | copy-start | bytes 12292
  101.0 19.3 %copy-start.11 = (bf16[128,2560]{1,0:T(8,128)(2,1)}, bf16[128,2560]{1,0:T(8,128)(2,1)S(1)}, u32[]{:S(2)}) copy-start(bf16[128,2560]{1,0:T(8,128)(2,1)S(1)} %convert_element_type.163) | copy-start | bytes 1966084
  279.0 143.9 %all-to-all-start.1 = ((bf16[8,6,64,1024]{3,2,1,0:T(8,128)(2,1)}), bf16[8,6,64,1024]{3,2,1,0:T(8,128)(2,1)}, u32[]{:S(2)}, u32[]{:S(2)}) async-start(bf16[8,6,64,1024]{3,2,1,0:T(8,128)(2,1)} %copy.215), calls=%async_computation.1 | async-start | bytes 12582912 | tf_op jit(solution)/shard_map/all_to_all | solution.py:183
  440.8 17.5 copy-start.29
  463.9 142.1 %copy-start.17 = (bf16[6,1024,128]{2,1,0:T(8,128)(2,1)S(1)}, bf16[6,1024,128]{2,1,0:T(8,128)(2,1)}, u32[]{:S(2)}) copy-start(bf16[6,1024,128]{2,1,0:T(8,128)(2,1)} %param.31) | copy-start | bytes 4718596
  464.0 142.1 %copy-start.54 = (f32[6,8,64,128]{3,2,1,0:T(8,128)S(1)}, f32[6,8,64,128]{3,2,1,0:T(8,128)}, u32[]{:S(2)}) copy-start(f32[6,8,64,128]{3,2,1,0:T(8,128)} %get-tuple-element.369) | copy-start | bytes 4718596
  614.7 143.7 %all-to-all-start.3 = ((bf16[8,6,64,1024]{3,2,1,0:T(8,128)(2,1)}), bf16[8,6,64,1024]{3,2,1,0:T(8,128)(2,1)}, u32[]{:S(2)}, u32[]{:S(2)}) async-start(bf16[8,6,64,1024]{3,2,1,0:T(8,128)(2,1)} %copy.218), calls=%async_computation.3 | async-start | bytes 12582912 | tf_op jit(solution)/shard_map/all_to_all | solution.py:227
  619.4 224.3 %reduce-scatter.26.cloned.1.call-start = ((), (), s32[]{:S(2)}) async-start(), calls=%async_computation.18 | async-start | bytes 1966080 | tf_op jit(solution)/shard_map/reduce_scatter | solution.py:223
  625.7 219.9 %reduce-scatter.24.cloned.1.call-start = ((), (), s32[]{:S(2)}) async-start(), calls=%async_computation.17 | async-start | bytes 1966080 | tf_op jit(solution)/shard_map/reduce_scatter | solution.py:220
  632.1 304.6 %reduce-scatter.30.cloned.1.call-start = ((), (), s32[]{:S(2)}) async-start(), calls=%async_computation.20 | async-start | bytes 540672
  633.0 159.1 %copy-start.48 = (f32[4,128]{1,0:T(4,128)}, f32[4,128]{1,0:T(4,128)S(1)}, u32[]{:S(2)}) copy-start(f32[4,128]{1,0:T(4,128)S(1)} %log_add_fusion) | copy-start | bytes 6148
  633.0 144.2 %copy-start.46 = (bf16[128,48]{0,1:T(8,128)(2,1)}, bf16[128,48]{0,1:T(8,128)(2,1)S(1)}, u32[]{:S(2)}) copy-start(bf16[128,48]{0,1:T(8,128)(2,1)S(1)} %select_reduce_fusion) | copy-start | bytes 36868
  803.5 265.2 %reduce-scatter.32.cloned.1.call-start = ((), (), s32[]{:S(2)}) async-start(), calls=%async_computation.21 | async-start | bytes 540672
  804.8 396.9 %reduce-scatter.22.cloned.1.call-start = ((), (), s32[]{:S(2)}) async-start(), calls=%async_computation.16 | async-start | bytes 540672 | tf_op jit(solution)/shard_map/reduce_scatter | solution.py:333
  806.6 531.5 %reduce-scatter.18.cloned.1.call-start = ((), (), s32[]{:S(2)}) async-start(), calls=%async_computation.14 | async-start | bytes 2162688 | tf_op jit(solution)/shard_map/reduce_scatter | solution.py:328
  811.1 663.0 %reduce-scatter.16.cloned.1.call-start = ((), (), s32[]{:S(2)}) async-start(), calls=%async_computation.13 | async-start | bytes 2162688 | tf_op jit(solution)/shard_map/reduce_scatter | solution.py:327
  814.0 817.3 %reduce-scatter.20.cloned.1.call-start = ((), (), s32[]{:S(2)}) async-start(), calls=%async_computation.15 | async-start | bytes 10813440 | tf_op jit(solution)/shard_map/reduce_scatter | solution.py:330
  819.7 969.7 %reduce-scatter.28.cloned.1.call-start = ((), (), s32[]{:S(2)}) async-start(), calls=%async_computation.19 | async-start | bytes 10813440
  (42 other events, 209.7 us)
Sparse Core Ops, SparseCore 0:
  625.9 32.2 reduce-scatter.25
  661.1 30.8 reduce-scatter.23
  803.7 133.0 reduce-scatter.29
  938.9 129.8 reduce-scatter.31
  1071.4 130.2 reduce-scatter.21
  1204.5 133.6 reduce-scatter.17
  1341.0 133.1 reduce-scatter.15
  1477.1 154.2 reduce-scatter.19
  1634.4 154.9 reduce-scatter.27
where the time goes:
time: 1810 us; the launch traced here: 1800 us
  waiting for transfers between devices  1110 us (61%)
  blocking collectives  326 us (18%)
  local copies, waits for them, and re-layouts  179 us (10%)
  other arithmetic  80.7 us (4%)
  matrix products  69.7 us (4%)
    unnamed x12, waiting for transfers between devices  327 us
    reduce_scatter x1, waiting for transfers between devices, per_device(): lax.psum_scatter(grad_output, ('dp', 'expert'), scatter_dimension=0, tile...  157 us
    all_to_all x1, blocking collectives, per_device(): lax.all_to_all(outgoing, 'expert', split_axis=0, concat_axis=0, tiled=True)  146 us
    all_to_all x1, blocking collectives, per_device(): lax.all_to_all(grad_outgoing, 'expert', split_axis=0, concat_axis=0, tile...  142 us
    reduce_scatter x1, waiting for transfers between devices, per_device(): lax.psum_scatter(grad_key, ('dp', 'expert'), scatter_dimension=0, tiled=T...  136 us
    reduce_scatter x1, waiting for transfers between devices, per_device(): lax.psum_scatter(grad_query, ('dp', 'expert'), scatter_dimension=0, tiled...  136 us
    reduce_scatter x1, waiting for transfers between devices, per_device(): lax.psum_scatter(grad_router, ('dp', 'expert'), scatter_dimension=0, tile...  132 us
    all_to_all x1, waiting for transfers between devices, per_device(): lax.all_to_all(grad_items, 'expert', split_axis=0, concat_axis=0, tiled=T...  125 us
  transfers between devices with their start and end apart: 11, of which 9 were waited for; matrix products, arithmetic and copies ran while one was open for 8% of the time, Pallas kernels for 0%

commit v1 on v0

--- a/solution.py
+++ b/solution.py
@@ -1,6 +1,11 @@
+import functools
+import math
+
 import jax
 import jax.numpy as jnp
 from jax import lax
+from jax.experimental import pallas as pl
+from jax.experimental.pallas import tpu as pltpu
 from jax.sharding import PartitionSpec as P
 
 D = 1024
@@ -65,7 +70,7 @@
     return (slot_of_row, row_of_slot)
 
 
-def per_device(
+def routed_layer(
     tokens,
     cotangent,
     seq_lengths,
@@ -348,9 +353,908 @@
     )
 
 
+F32 = jnp.float32
+BF16 = jnp.bfloat16
+MESH = pl.DeviceIdType.MESH
+LANES = 128
+
+
+def mm(a, b):
+    return lax.dot_general(a, b, (((1,), (0,)), ((), ())), preferred_element_type=F32)
+
+
+def mm_t(a, b):
+    return lax.dot_general(a, b, (((1,), (1,)), ((), ())), preferred_element_type=F32)
+
+
+def tmm(a, b):
+    return lax.dot_general(a, b, (((0,), (0,)), ((), ())), preferred_element_type=F32)
+
+
+def iota(shape, axis):
+    return lax.broadcasted_iota(jnp.int32, shape, axis)
+
+
+def column(x, j, width=LANES):
+    return jnp.broadcast_to(x[:, j : j + 1], (x.shape[0], width))
+
+
+def sigmoid(x):
+    return 1.0 / (1.0 + jnp.exp(-x))
+
+
+class Scratch:
+    def __init__(self):
+        self.names, self.shapes = [], []
+
+    def add(self, name, shape):
+        self.names.append(name)
+        self.shapes.append(shape)
+
+    def vmem(self, name, shape, dtype):
+        self.add(name, pltpu.VMEM(shape, dtype))
+
+    def sems(self, name, *shape):
+        self.add(name, pltpu.SemaphoreType.DMA(shape))
+
+
+INPUTS = ("tokens", "cot", "lens", "rt", "het", "gain", "wvg", "wog", "wr", "wq", "wk", "wv", "wo", "wu", "wd")
+OUTPUTS = ("mixed", "gtok", "ggain", "gq", "gk", "gv", "go", "gvg", "gog", "gr", "gup", "gdn")
+
+
+def layer_kernel(names, nd, nz, local, *refs):
+    r = dict(zip(names, refs))
+    R = type("R", (), r)
+    C = R.tokens.shape[0]
+    own_e = 2 * local
+    pad_e = R.maskb.shape[1]
+    EF = own_e * DH
+    HF = local * DH
+    HD = H * DH
+    EV = EA * HD
+    S = D // (nd * nz * 2)
+    SL = S * nz
+    GATE = EA * H
+    p = lax.axis_index("dp")
+    e = lax.axis_index("expert")
+    z = e // 2
+    c = e % 2
+    sib = 1 - c
+
+    def dev(p_, z_, c_):
+        return (p_, z_ * 2 + c_)
+
+    def times(i, n):
+        return pl.multiple_of(i * n, n)
+
+    def remote(src, dst, ss, rs, to):
+        return pltpu.make_async_remote_copy(
+            src_ref=src, dst_ref=dst, send_sem=ss, recv_sem=rs, device_id=to, device_id_type=MESH
+        )
+
+    def arrived(dst, rs):
+        remote(dst, dst, rs, rs, dev(p, z, sib)).wait_recv()
+
+    def sent(src, ss):
+        remote(src, src, ss, ss, dev(p, z, sib)).wait_send()
+
+    def plane(k):
+        return lax.rem(p + k, nd)
+
+    def line(k):
+        return lax.rem(z + k, nz)
+
+    loads = {}
+
+    def load(name, src, dst, sem):
+        cp = pltpu.make_async_copy(src, dst, sem)
+        cp.start()
+        loads.setdefault(name, []).append(cp)
+
+    def loaded(name):
+        for cp in loads.pop(name):
+            cp.wait()
+
+    load("qk", R.wq, R.wqk_b.at[:, 0:HD], R.ld.at[0])
+    load("qk", R.wk, R.wqk_b.at[:, HD : 2 * HD], R.ld.at[1])
+    load("v", R.wv, R.wv_b, R.ld.at[2])
+    for i in range(local):
+        col = times(c * local + i, DH)
+        load("up", R.wu.at[i], R.wup_b.at[:, pl.ds(col, DH)], R.ld.at[4 + i])
+        load("dn", R.wd.at[i], R.wdn_b.at[:, pl.ds(col, DH)], R.ld.at[4 + local + i])
+    load("o", R.wo, R.wo_b, R.ld.at[3])
+
+    barrier = pltpu.get_barrier_semaphore()
+    partners = [dev(p, z, sib)]
+    partners += [dev(p, line(k), c) for k in range(1, nz)]
+    for k in range(1, nd):
+        partners += [dev(plane(k), z, c), dev(plane(k), z, sib)]
+    for to in partners:
+        pl.semaphore_signal(barrier, inc=1, device_id=to, device_id_type=MESH)
+
+    l0 = R.lens[0, 0]
+    b1 = l0 + R.lens[0, 1]
+    row = iota((C, LANES), 0)
+    lane = iota((C, LANES), 1)
+    seq_r = (row >= l0).astype(jnp.int32) + (row >= b1).astype(jnp.int32)
+    seq_c = (lane >= l0).astype(jnp.int32) + (lane >= b1).astype(jnp.int32)
+    live = row < b1
+    allowed = ((seq_r == seq_c) & (lane <= row) & (lane < b1)) | (row == lane)
+    live_f = jnp.where(live, 1.0, 0.0).astype(F32)
+    start = jnp.where(seq_r == 0, 0, l0)
+    position = jnp.where(live, row - start, 0).astype(F32)
+
+    for b in range(D // LANES):
+        cols = slice(b * LANES, (b + 1) * LANES)
+        R.cotb[pl.ds(times(z, C), C), cols] = (R.cot[:, cols].astype(F32) * live_f).astype(BF16)
+    ids = iota((pad_e, C), 0)
+    for zz in range(nz):
+        named = jnp.zeros((pad_e, C), F32)
+        for k in range(TOPK):
+            hit = jnp.broadcast_to(R.rt[k : k + 1, :], (pad_e, C)) == ids + zz * own_e
+            named = jnp.where(hit & (ids < own_e), 1.0, named)
+        R.mask_s[zz] = named.astype(BF16)
+    R.maskb[z] = R.mask_s[z]
+
+    pl.semaphore_wait(barrier, len(partners))
+
+    def block(buf, o):
+        return buf.at[pl.ds(times(o, C), C), :]
+
+    def pass_on(buf, ss, rs, o, right, left):
+        @pl.when(right)
+        def _():
+            remote(block(buf, o), block(buf, o), ss.at[0, o], rs.at[o], dev(p, z + 1, c)).start()
+
+        @pl.when(left)
+        def _():
+            remote(block(buf, o), block(buf, o), ss.at[1, o], rs.at[o], dev(p, z - 1, c)).start()
+
+    def passed(buf, ss, o, right, left):
+        @pl.when(right)
+        def _():
+            sent(block(buf, o), ss.at[0, o])
+
+        @pl.when(left)
+        def _():
+            sent(block(buf, o), ss.at[1, o])
+
+    def gather_own(buf, ss, rs):
+        pass_on(buf, ss, rs, z, z < nz - 1, z > 0)
+
+    def gather_on(buf, ss, rs, o):
+        arrived(block(buf, o), rs.at[o])
+        pass_on(buf, ss, rs, o, (o < z) & (z < nz - 1), (o > z) & (z > 0))
+
+    def gather_step(buf, ss, rs, k):
+        @pl.when(z >= k)
+        def _():
+            gather_on(buf, ss, rs, z - k)
+
+        @pl.when(z + k < nz)
+        def _():
+            gather_on(buf, ss, rs, z + k)
+
+    def gather_end(buf, ss):
+        passed(buf, ss, z, z < nz - 1, z > 0)
+        for k in range(1, nz):
+
+            @pl.when(z >= k)
+            def _():
+                passed(buf, ss, z - k, z < nz - 1, False)
+
+            @pl.when(z + k < nz)
+            def _():
+                passed(buf, ss, z + k, False, z > 0)
+
+    gather_own(R.cotb, R.cot_ss, R.cot_rs)
+    masks = []
+    for k in range(1, nz):
+        o = line(k)
+        cp = remote(R.mask_s.at[o], R.maskb.at[z], R.mask_ss.at[k], R.mask_rs.at[z], dev(p, o, c))
+        cp.start()
+        masks.append(cp)
+
+    s_row, s_col = iota((GATE, LANES), 0), iota((GATE, LANES), 1)
+    to_v = jnp.where(s_row == s_col, 1.0, 0.0).astype(BF16)
+    to_o = jnp.where(s_row + GATE == s_col, 1.0, 0.0).astype(BF16)
+    R.wg_b[...] = (mm(R.wvg[...], to_v) + mm(R.wog[...], to_o)).astype(BF16)
+    experts = R.wr.shape[1]
+    r_row, r_col = iota((experts, LANES), 0), iota((experts, LANES), 1)
+    to_r = jnp.where((r_row == r_col + z * own_e) & (r_col < own_e), 1.0, 0.0).astype(BF16)
+    R.wrl_b[...] = mm(R.wr[...], to_r).astype(BF16)
+
+    half = lax.rem(lane, DH // 2).astype(F32)
+    angle = position * jnp.exp(half * (-2.0 / DH * math.log(rope_base)))
+    cosine = jnp.cos(angle)
+    sine = jnp.where(lane < DH // 2, -jnp.sin(angle), jnp.sin(angle))
+
+    def rot(v):
+        return v * cosine + pltpu.roll(v, DH // 2, 1) * sine
+
+    def rot_back(v):
+        return v * cosine - pltpu.roll(v, DH // 2, 1) * sine
+
+    inputs = R.tokens[...].astype(F32)
+    centred = inputs - jnp.mean(inputs, axis=-1, keepdims=True)
+    inverse = lax.rsqrt(jnp.mean(centred * centred, axis=-1, keepdims=True) + norm_eps)
+    standard = centred * inverse
+    R.std_b[...] = standard
+    R.normed_b[...] = (standard * R.gain[...]).astype(BF16)
+
+    loaded("qk")
+    scale = DH ** (-0.5)
+    qk = mm(R.normed_b[...], R.wqk_b[:, 0:HD])
+    for h in range(H):
+        hs = slice(h * DH, (h + 1) * DH)
+        R.q_b[:, hs] = (rot(qk[:, hs]) * scale).astype(BF16)
+    qk = mm(R.normed_b[...], R.wqk_b[:, HD : 2 * HD])
+    for h in range(H):
+        hs = slice(h * DH, (h + 1) * DH)
+        R.k_b[:, hs] = rot(qk[:, hs]).astype(BF16)
+
+    hit = []
+    for j in range(GATE):
+        x, h = divmod(j, H)
+        one = (R.het[2 * h : 2 * h + 1, :] == x) | (R.het[2 * h + 1 : 2 * h + 2, :] == x)
+        hit.append(jnp.where(one, 1.0, 0.0).astype(F32))
+    hit = jnp.concatenate(hit + hit + [jnp.zeros((LANES - 2 * GATE, C), F32)], axis=0)
+    R.gate_b[...] = sigmoid(mm(R.tokens[...], R.wg_b[...])) * hit.T
+
+    loaded("up")
+    loaded("dn")
+    wx = []
+    for i, buf in enumerate((R.wup_b, R.wdn_b)):
+        part = buf.at[:, pl.ds(times(c, HF), HF)]
+        cp = remote(part, part, R.w_ss.at[i], R.w_rs.at[i], dev(p, z, sib))
+        cp.start()
+        wx.append(cp)
+
+    loaded("v")
+    gates = R.gate_b[...]
+    total = [None] * H
+    for x in range(EA):
+        R.val_b[:, x * HD : (x + 1) * HD] = mm(R.tokens[...], R.wv_b[:, x * HD : (x + 1) * HD])
+        for h in range(H):
+            lo = x * HD + h * DH
+            term = column(gates, x * H + h) * R.val_b[:, lo : lo + DH]
+            total[h] = term if x == 0 else total[h] + term
+    for h in range(H):
+        R.v_b[:, h * DH : (h + 1) * DH] = total[h].astype(BF16)
+
+    for h in range(H):
+        hs = slice(h * DH, (h + 1) * DH)
+        scores = jnp.where(allowed, mm_t(R.q_b[:, hs], R.k_b[:, hs]), masked_score)
+        shifted = jnp.exp(scores - jnp.max(scores, axis=-1, keepdims=True))
+        shares = shifted / jnp.sum(shifted, axis=-1, keepdims=True)
+        R.prob_b[h] = shares
+        R.att_b[:, hs] = mm(shares.astype(BF16), R.v_b[:, hs])
+
+    for k in range(1, 2):
+        gather_step(R.cotb, R.cot_ss, R.cot_rs, k)
+
+    for x in range(EA):
+        for h in range(H):
+            lo = x * HD + h * DH
+            R.mix_b[:, lo : lo + DH] = (
+                column(gates, GATE + x * H + h) * R.att_b[:, h * DH : (h + 1) * DH]
+            ).astype(BF16)
+    loaded("o")
+    half_d = D // 2
+    for b in range(2):
+        cols = slice(b * half_d, (b + 1) * half_d)
+        hidden = R.tokens[:, cols].astype(F32) + mm_t(R.mix_b[...], R.wo_b[cols, :])
+        R.hid_f[:, cols] = hidden
+        R.hidb[pl.ds(times(z, C), C), cols] = hidden.astype(BF16)
+    gather_own(R.hidb, R.hid_ss, R.hid_rs)
+
+    def put_turned(x, w):
+        for b in range(D // LANES):
+            t = x[:, b * LANES : (b + 1) * LANES].astype(F32).T.astype(BF16)
+            for q in range(LANES // S):
+                i = (b * LANES) // S + q
+                pp, zz, cc = i // (2 * nz), (i % (2 * nz)) // 2, i % 2
+                at = (pp * 2 + cc) * SL + zz * S
+                R.lt[at : at + S, w * LANES : (w + 1) * LANES] = t[q * S : (q + 1) * S, :]
+
+    plane_all = [(k, dc) for k in range(nd) for dc in range(2) if k or dc]
+
+    def side(dc):
+        return sib if dc else c
+
+    def send_turned(w0, w1, ss, rs):
+        out = []
+        lanes = slice(w0 * LANES, w1 * LANES)
+        for k, dc in plane_all:
+            to = plane(k)
+            slot = 2 * k + dc
+            at = times(to * 2 + side(dc), SL)
+            cp = remote(
+                R.lt.at[pl.ds(at, SL), lanes],
+                R.ltr.at[slot, :, lanes],
+                ss.at[slot],
+                rs.at[slot],
+                dev(to, z, side(dc)),
+            )
+            cp.start()
+            out.append(cp)
+        R.ltr[0, :, lanes] = R.lt[pl.ds(times(p * 2 + c, SL), SL), lanes]
+        return out
+
+    def send_rows(buf, lanes, ss, rs):
+        out = []
+        for k in range(1, nd):
+            cp = remote(
+                buf.at[0:C, lanes],
+                buf.at[2 * k * C : (2 * k + 1) * C, lanes],
+                ss.at[k],
+                rs.at[2 * k],
+                dev(plane(k), z, c),
+            )
+            cp.start()
+            out.append(cp)
+        return out + [hand_over(buf, lanes, ss, rs, 0)]
+
+    def hand_over(buf, lanes, ss, rs, k):
+        cp = remote(
+            buf.at[2 * k * C : (2 * k + 1) * C, lanes],
+            buf.at[(2 * k + 1) * C : (2 * k + 2) * C, lanes],
+            ss.at[nd + k],
+            rs.at[2 * k + 1],
+            dev(p, z, sib),
+        )
+        cp.start()
+        return cp
+
+    def hand_all(buf, lanes, ss, rs, out):
+        for k in range(1, nd):
+            out[k - 1].wait_recv()
+            out.append(hand_over(buf, lanes, ss, rs, k))
+
+    def rows_here(buf, lanes, rs):
+        for k in range(nd):
+            arrived(buf.at[(2 * k + 1) * C : (2 * k + 2) * C, lanes], rs.at[2 * k + 1])
+
+    put_turned(R.tokens[...], 0)
+    put_turned(R.normed_b[...], 1)
+    put_turned(R.hid_f[...], 2)
+    turned = send_turned(0, 3, R.lt_ss, R.lt_rs)
+    R.ra[0:C, 0:HD] = R.att_b[...].astype(BF16)
+    R.ra[0:C, HD : HD + LANES] = gates.astype(BF16)
+    RA = slice(0, HD + LANES)
+    ra_out = send_rows(R.ra, RA, R.ra_ss, R.ra_rs)
+
+    for k in range(2, nz - 1):
+        gather_step(R.cotb, R.cot_ss, R.cot_rs, k)
+
+    for cp in wx:
+        cp.wait()
+
+    least = jnp.minimum(z, nz - 1 - z)
+
+    def origin(k):
+        paired = k <= 2 * least
+        dist = jnp.where(paired, (k + 1) // 2, k - least)
+        left = jnp.where(paired, lax.rem(k, 2) == 1, z > nz - 1 - z)
+        return jnp.where(k == 0, z, jnp.where(left, z - dist, z + dist))
+
+    def expert_block(k, carry):
+        o = origin(k)
+        rows = pl.ds(times(o, C), C)
+
+        @pl.when(k > 0)
+        def _():
+            gather_on(R.hidb, R.hid_ss, R.hid_rs, o)
+
+            @pl.when((o == z - nz + 1) | (o == z + nz - 1))
+            def _():
+                arrived(block(R.cotb, o), R.cot_rs.at[o])
+
+            arrived(R.maskb.at[o], R.mask_rs.at[o])
+
+        hb = R.hidb[rows, :]
+        cb = R.cotb[rows, :]
+        named = R.maskb[o].astype(F32)
+        named = jnp.concatenate([named, jnp.zeros((LANES - pad_e, C), F32)], axis=0).T
+        g = sigmoid(mm(hb, R.wrl_b[...])) * named
+        glog = jnp.zeros((C, LANES), F32)
+        for q in range(own_e // 4):
+            cols = slice(q * 4 * DH, (q + 1) * 4 * DH)
+            raised = mm(hb, R.wup_b[:, cols])
+            back = mm(cb, R.wdn_b[:, cols])
+            for i in range(4):
+                j = q * 4 + i
+                u = raised[:, i * DH : (i + 1) * DH]
+                a = back[:, i * DH : (i + 1) * DH]
+                gj = column(g, j)
+                s = sigmoid(u)
+                act = u * s
+                lo = j * DH
+                R.gact[rows, lo : lo + DH] = (gj * act).astype(BF16)
+                R.gra[rows, lo : lo + DH] = (gj * a * (s * (1.0 + u * (1.0 - s)))).astype(BF16)
+                gg = jnp.sum(a * act, axis=1, keepdims=True)
+                glog = jnp.where(lane == j, jnp.broadcast_to(gg, (C, LANES)), glog)
+        glog = glog * g * (1.0 - g)
+        low = glog.astype(BF16)
+        R.glog_s[o] = glog.T[0:pad_e, :].astype(BF16)
+        for b in range(2):
+            cols = slice(b * half_d, (b + 1) * half_d)
+            gh = mm_t(R.gra[rows, :], R.wup_b[cols, :]) + mm_t(low, R.wrl_b[cols, :])
+            R.gh_s[o, :, cols] = gh.astype(BF16)
+
+        @pl.when(k > 0)
+        def _():
+            remote(R.gh_s.at[o], R.gh_r.at[z], R.gh_ss.at[o], R.gh_rs.at[z], dev(p, o, c)).start()
+            remote(
+                R.glog_s.at[o], R.glog_r.at[z], R.gl_ss.at[o], R.gl_rs.at[z], dev(p, o, c)
+            ).start()
+
+        return carry
+
+    lax.fori_loop(0, nz, expert_block, 0)
+
+    def out_tile(t, carry):
+        rows = pl.ds(times(t, 256), 256)
+        got = mm_t(R.gact[...], R.wdn_b[rows, :]).astype(BF16)
+        for o in range(nz):
+            R.out_s[o, :, rows] = got[o * C : (o + 1) * C, :]
+        return carry
+
+    lax.fori_loop(0, D // 256, out_tile, 0)
+    for k in range(1, nz):
+        o = line(k)
+        remote(R.out_s.at[o], R.out_r.at[z], R.out_ss.at[o], R.out_rs.at[z], dev(p, o, c)).start()
+
+    pairs = []
+    for i, (left_of, right_of, buf) in enumerate(
+        ((R.cotb, R.gact, R.wdn_b), (R.hidb, R.gra, R.wup_b))
+    ):
+
+        def grad_tile(t, carry, base):
+            cols = pl.ds(pl.multiple_of(base + t * 256, 256), 256)
+            buf[:, cols] = tmm(left_of[...], right_of[:, cols]).astype(BF16)
+            return carry
+
+        lax.fori_loop(0, HF // 256, functools.partial(grad_tile, base=sib * HF), 0)
+        cp = remote(
+            buf.at[:, pl.ds(times(sib, HF), HF)],
+            R.pair_r.at[i],
+            R.pair_ss.at[i],
+            R.pair_rs.at[i],
+            dev(p, z, sib),
+        )
+        cp.start()
+        pairs.append(cp)
+        lax.fori_loop(0, HF // 256, functools.partial(grad_tile, base=c * HF), 0)
+
+    hand_all(R.ra, RA, R.ra_ss, R.ra_rs, ra_out)
+
+    ghid = R.cotb[pl.ds(times(z, C), C), :].astype(F32) + R.gh_s[z].astype(F32)
+    for k in range(1, nz):
+        o = line(k)
+        arrived(R.gh_r.at[o], R.gh_rs.at[o])
+        arrived(R.glog_r.at[o], R.gl_rs.at[o])
+        ghid = ghid + R.gh_r[o].astype(F32)
+    R.glog_r[z] = R.glog_s[z]
+    R.ghid_f[...] = ghid
+    R.ghid_b[...] = ghid.astype(BF16)
+    put_turned(R.ghid_f[...], 3)
+    turned_late = send_turned(3, 4, R.ltl_ss, R.ltl_rs)
+
+    gates = R.gate_b[...]
+    small = jnp.zeros((C, LANES), F32)
+    gatt = [None] * H
+    for x in range(EA):
+        gmix = mm(R.ghid_b[...], R.wo_b[:, x * HD : (x + 1) * HD])
+        for h in range(H):
+            hs = slice(h * DH, (h + 1) * DH)
+            j = GATE + x * H + h
+            term = column(gates, j) * gmix[:, hs]
+            gatt[h] = term if x == 0 else gatt[h] + term
+            gg = jnp.sum(gmix[:, hs] * R.att_b[:, hs], axis=1, keepdims=True)
+            small = jnp.where(lane == j, jnp.broadcast_to(gg, (C, LANES)), small)
+    for h in range(H):
+        hs = slice(h * DH, (h + 1) * DH)
+        low = gatt[h].astype(BF16)
+        R.gatt_b[:, hs] = low
+        gval = tmm(R.prob_b[h].astype(BF16), low)
+        R.gval_f[:, hs] = gval
+        R.rb[0:C, hs] = gval.astype(BF16)
+        for x in range(EA):
+            lo = x * HD + h * DH
+            j = x * H + h
+            gg = jnp.sum(gval * R.val_b[:, lo : lo + DH], axis=1, keepdims=True)
+            small = jnp.where(lane == j, jnp.broadcast_to(gg, (C, LANES)), small)
+    small = small * gates * (1.0 - gates)
+    glog = jnp.concatenate(
+        [jnp.zeros((2 * GATE, C), F32)]
+        + [R.glog_r[o].astype(F32) for o in range(nz)]
+        + [jnp.zeros((LANES - 2 * GATE - nz * pad_e, C), F32)],
+        axis=0,
+    )
+    R.small_b[...] = small.astype(BF16)
+    R.rb[0:C, HD : HD + LANES] = (small + glog.T).astype(BF16)
+    RV = slice(0, HD + LANES)
+    rv_out = send_rows(R.rb, RV, R.rv_ss, R.rv_rs)
+
+    q0 = HD + LANES
+    for h in range(H):
+        hs = slice(h * DH, (h + 1) * DH)
+        low = R.gatt_b[:, hs]
+        gsh = mm_t(low, R.v_b[:, hs])
+        prob = R.prob_b[h]
+        centre = jnp.sum(prob * gsh, axis=-1, keepdims=True)
+        gs = (prob * (gsh - centre)).astype(BF16)
+        R.rb[0:C, q0 + h * DH : q0 + (h + 1) * DH] = rot_back(
+            mm(gs, R.k_b[:, hs]) * scale
+        ).astype(BF16)
+        R.rb[0:C, q0 + HD + h * DH : q0 + HD + (h + 1) * DH] = rot_back(
+            tmm(gs, R.q_b[:, hs])
+        ).astype(BF16)
+    RQ = slice(q0, q0 + 2 * HD)
+    rq_out = send_rows(R.rb, RQ, R.rq_ss, R.rq_rs)
+
+    for cp in turned:
+        cp.wait()
+    rows_here(R.ra, RA, R.ra_rs)
+    for cp in turned_late:
+        cp.wait()
+
+    def turned_of(w):
+        return jnp.concatenate(
+            [R.ltr[s, :, w * LANES : (w + 1) * LANES] for s in range(2 * nd)], axis=1
+        )
+
+    def send_part(part, lanes):
+        for k in range(1, nz):
+            o = line(k)
+            remote(
+                R.pb.at[pl.ds(times(o, S), S), lanes],
+                R.pr.at[z, :, lanes],
+                R.p_ss.at[part, o],
+                R.p_rs.at[part, z],
+                dev(p, o, c),
+            ).start()
+
+    def gated_grad(w, rows_of, g0, at):
+        left = turned_of(w)
+        for x in range(EA):
+            right = []
+            for h in range(H):
+                gx = column(R.ra[:, HD : HD + LANES], g0 + x * H + h).astype(F32)
+                right.append((gx * rows_of[:, h * DH : (h + 1) * DH].astype(F32)).astype(BF16))
+            right = jnp.concatenate(right, axis=1)
+            R.pb[:, at + x * HD : at + (x + 1) * HD] = mm(left, right).astype(BF16)
+
+    PO, PV, PQ, PS = (
+        slice(0, EV),
+        slice(EV, 2 * EV),
+        slice(2 * EV, 2 * EV + 2 * HD),
+        slice(2 * EV + 2 * HD, 2 * EV + 2 * HD + LANES),
+    )
+    gated_grad(3, R.ra, GATE, 0)
+    send_part(0, PO)
+
+    gproj = mm_t(R.rb[0:C, RQ], R.wqk_b[...])
+    standard = R.std_b[...]
+    column_sum = jnp.sum(gproj * standard, axis=0, keepdims=True)
+    for b in range(D // LANES):
+        R.gp[0, b : b + 1, :] = column_sum[:, b * LANES : (b + 1) * LANES]
+    gain_out = []
+    for k, dc in plane_all:
+        slot = 2 * k + dc
+        cp = remote(
+            R.gp.at[0], R.gp.at[slot], R.gp_ss.at[slot], R.gp_rs.at[slot], dev(plane(k), z, side(dc))
+        )
+        cp.start()
+        gain_out.append(cp)
+
+    hand_all(R.rb, RV, R.rv_ss, R.rv_rs, rv_out)
+
+    inputs = R.tokens[...].astype(F32)
+    centred = inputs - jnp.mean(inputs, axis=-1, keepdims=True)
+    inverse = lax.rsqrt(jnp.mean(centred * centred, axis=-1, keepdims=True) + norm_eps)
+    gs = gproj * R.gain[...]
+    gtok = R.ghid_f[...] + inverse * (
+        gs
+        - jnp.mean(gs, axis=-1, keepdims=True)
+        - standard * jnp.mean(gs * standard, axis=-1, keepdims=True)
+    )
+    R.gtok[...] = gtok
+    for x in range(EA):
+        for h in range(H):
+            lo = x * HD + h * DH
+            R.mix_b[:, lo : lo + DH] = (
+                column(gates, x * H + h) * R.gval_f[:, h * DH : (h + 1) * DH]
+            ).astype(BF16)
+    for b in range(2):
+        cols = slice(b * half_d, (b + 1) * half_d)
+        R.gtok[:, cols] += mm_t(R.mix_b[...], R.wv_b[cols, :]) + mm_t(
+            R.small_b[...], R.wg_b[cols, :]
+        )
+
+    rows_here(R.rb, RV, R.rv_rs)
+    gated_grad(0, R.rb, 0, EV)
+    send_part(1, PV)
+    hand_all(R.rb, RQ, R.rq_ss, R.rq_rs, rq_out)
+    lane_s = iota((SL, LANES), 1)
+    small_t = mm(turned_of(0), R.rb[:, HD : HD + LANES])
+    small_h = mm(turned_of(2), R.rb[:, HD : HD + LANES])
+    R.pb[:, PS] = jnp.where(lane_s < 2 * GATE, small_t, small_h).astype(BF16)
+    send_part(3, PS)
+    rows_here(R.rb, RQ, R.rq_rs)
+    left = turned_of(1)
+    for b in range(2):
+        lo = q0 + b * HD
+        R.pb[:, 2 * EV + b * HD : 2 * EV + (b + 1) * HD] = mm(left, R.rb[:, lo : lo + HD]).astype(
+            BF16
+        )
+    send_part(2, PQ)
+
+    own_cols = pl.ds(times(c, HF), HF)
+    rows_d = D // nd
+    plane_out = []
+    for i, buf in enumerate((R.wdn_b, R.wup_b)):
+        pairs[i].wait()
+
+        def pair_tile(t, carry):
+            rows = pl.ds(times(t, 128), 128)
+            buf[rows, own_cols] = (
+                buf[rows, own_cols].astype(F32) + R.pair_r[i, rows, :].astype(F32)
+            ).astype(BF16)
+            return carry
+
+        lax.fori_loop(0, D // 128, pair_tile, 0)
+        for k in range(1, nd):
+            to = plane(k)
+            cp = remote(
+                buf.at[pl.ds(times(to, rows_d), rows_d), own_cols],
+                R.eg_r.at[k - 1, i],
+                R.eg_ss.at[k - 1, i],
+                R.eg_rs.at[k - 1, i],
+                dev(to, z, c),
+            )
+            cp.start()
+            plane_out.append(cp)
+
+    total = R.gp[0]
+    for cp, (k, dc) in zip(gain_out, plane_all):
+        cp.wait()
+        total = total + R.gp[2 * k + dc]
+    R.gz_s[...] = total
+    for k in range(1, nz):
+        o = line(k)
+        remote(R.gz_s, R.gz.at[z], R.gz_ss.at[o], R.gz_rs.at[z], dev(p, o, c)).start()
+
+    out = R.hid_f[...] + R.out_s[z].astype(F32)
+    for k in range(1, nz):
+        o = line(k)
+        arrived(R.out_r.at[o], R.out_rs.at[o])
+        out = out + R.out_r[o].astype(F32)
+    R.mixed[...] = out.astype(BF16)
+
+    for k in range(1, nz):
+        o = line(k)
+        arrived(R.gz.at[o], R.gz_rs.at[o])
+        total = total + R.gz[o]
+    first = (p * 2 * nz + z * 2 + c) * S
+    pick_row = iota((D // LANES, LANES), 0) == first // LANES
+    line_sum = jnp.sum(jnp.where(pick_row, total, 0.0), axis=0, keepdims=True)
+    shift = lax.rem(LANES - lax.rem(first, LANES), LANES)
+    line_sum = pltpu.roll(jnp.broadcast_to(line_sum, (8, LANES)), shift, 1)
+    R.ggain[...] = line_sum[0:1, 0:S]
+
+    own_rows = pl.ds(times(z, S), S)
+
+    def line_total(part, lanes):
+        got = R.pb[own_rows, lanes].astype(F32)
+        for k in range(1, nz):
+            o = line(k)
+            arrived(R.pr.at[o, :, lanes], R.p_rs.at[part, o])
+            got = got + R.pr[o, :, lanes].astype(F32)
+        return got
+
+    R.go[...] = line_total(0, PO)
+    R.gv[...] = line_total(1, PV)
+    got = line_total(3, PS)
+
+    def pick(width, source):
+        a, b = iota((LANES, width), 0), iota((LANES, width), 1)
+        sel = jnp.where(a == source(b), 1.0, 0.0).astype(F32)
+        return lax.dot_general(
+            got,
+            sel,
+            (((1,), (0,)), ((), ())),
+            preferred_element_type=F32,
+            precision=lax.Precision.HIGHEST,
+        )
+
+    def router_lane(b):
+        at = jnp.zeros_like(b)
+        for o in range(nz):
+            at = jnp.where(b >= o * own_e, 2 * GATE + o * pad_e + b - o * own_e, at)
+        return at
+
+    R.gvg[...] = pick(GATE, lambda b: b)
+    R.gog[...] = pick(GATE, lambda b: b + GATE)
+    R.gr[...] = pick(experts, router_lane)
+    got = line_total(2, PQ)
+    R.gq[...] = got[:, 0:HD]
+    R.gk[...] = got[:, HD : 2 * HD]
+
+    for i, (buf, dst) in enumerate(((R.wdn_b, R.gdn), (R.wup_b, R.gup))):
+        for k in range(1, nd):
+            plane_out[i * (nd - 1) + k - 1].wait_recv()
+        rows = pl.ds(times(p, rows_d), rows_d)
+        for x in range(local):
+            got = buf[rows, pl.ds(times(c * local + x, DH), DH)].astype(F32)
+            for k in range(1, nd):
+                got = got + R.eg_r[k - 1, i, :, x * DH : (x + 1) * DH].astype(F32)
+            dst[x] = got
+
+    gather_end(R.cotb, R.cot_ss)
+    gather_end(R.hidb, R.hid_ss)
+    for cp in masks + ra_out + rv_out + rq_out + plane_out:
+        cp.wait_send()
+    for k in range(1, nz):
+        o = line(k)
+        sent(R.gh_s.at[o], R.gh_ss.at[o])
+        sent(R.glog_s.at[o], R.gl_ss.at[o])
+        sent(R.out_s.at[o], R.out_ss.at[o])
+        sent(R.gz_s, R.gz_ss.at[o])
+        for part, lanes in enumerate((PO, PV, PQ, PS)):
+            sent(R.pb.at[pl.ds(times(o, S), S), lanes], R.p_ss.at[part, o])
+
+
+def fused_layer(nd, nz, *args):
+    (tokens, cotangent, seq_lengths, routes, head_experts, norm_gain) = args[:6]
+    (w_query, w_key, w_value, w_output, w_value_gate, w_output_gate, w_router) = args[6:13]
+    w_up, w_down = args[13:]
+    C = tokens.shape[0]
+    local = w_up.shape[0]
+    experts = w_router.shape[1]
+    own_e = 2 * local
+    pad_e = -(-own_e // 16) * 16
+    EF, HF, HD = own_e * DH, local * DH, H * DH
+    EV = EA * HD
+    S = D // (nd * nz * 2)
+    SL = S * nz
+    PW = 2 * EV + 2 * HD + LANES
+    s = Scratch()
+    s.vmem("wqk_b", (D, 2 * HD), BF16)
+    s.vmem("wv_b", (D, EV), BF16)
+    s.vmem("wo_b", (D, EV), BF16)
+    s.vmem("wup_b", (D, EF), BF16)
+    s.vmem("wdn_b", (D, EF), BF16)
+    s.vmem("wg_b", (D, LANES), BF16)
+    s.vmem("wrl_b", (D, LANES), BF16)
+    s.vmem("cotb", (nz * C, D), BF16)
+    s.vmem("hidb", (nz * C, D), BF16)
+    s.vmem("mask_s", (nz, pad_e, C), BF16)
+    s.vmem("maskb", (nz, pad_e, C), BF16)
+    s.vmem("std_b", (C, D), F32)
+    s.vmem("normed_b", (C, D), BF16)
+    s.vmem("q_b", (C, HD), BF16)
+    s.vmem("k_b", (C, HD), BF16)
+    s.vmem("v_b", (C, HD), BF16)
+    s.vmem("gate_b", (C, LANES), F32)
+    s.vmem("val_b", (C, EV), F32)
+    s.vmem("prob_b", (H, C, C), F32)
+    s.vmem("att_b", (C, HD), F32)
+    s.vmem("mix_b", (C, EV), BF16)
+    s.vmem("hid_f", (C, D), F32)
+    s.vmem("lt", (D, 4 * LANES), BF16)
+    s.vmem("ltr", (2 * nd, SL, 4 * LANES), BF16)
+    s.vmem("ra", (2 * nd * C, HD + LANES), BF16)
+    s.vmem("rb", (2 * nd * C, 3 * HD + LANES), BF16)
+    s.vmem("gact", (nz * C, EF), BF16)
+    s.vmem("gra", (nz * C, EF), BF16)
+    for name in ("gh_s", "gh_r", "out_s", "out_r"):
+        s.vmem(name, (nz, C, D), BF16)
+    for name in ("glog_s", "glog_r"):
+        s.vmem(name, (nz, pad_e, C), BF16)
+    s.vmem("pair_r", (2, D, HF), BF16)
+    s.vmem("eg_r", (nd - 1, 2, D // nd, HF), BF16)
+    s.vmem("ghid_f", (C, D), F32)
+    s.vmem("ghid_b", (C, D), BF16)
+    s.vmem("gatt_b", (C, HD), BF16)
+    s.vmem("gval_f", (C, HD), F32)
+    s.vmem("small_b", (C, LANES), BF16)
+    s.vmem("pb", (SL, PW), BF16)
+    s.vmem("pr", (nz, S, PW), BF16)
+    s.vmem("gp", (2 * nd, D // LANES, LANES), F32)
+    s.vmem("gz_s", (D // LANES, LANES), F32)
+    s.vmem("gz", (nz, D // LANES, LANES), F32)
+    s.sems("ld", 4 + 2 * local)
+    for name in ("cot_ss", "hid_ss"):
+        s.sems(name, 2, nz)
+    for name in ("cot_rs", "hid_rs", "mask_ss", "mask_rs", "gh_ss", "gh_rs", "gl_ss", "gl_rs", "out_ss", "out_rs", "gz_ss", "gz_rs"):
+        s.sems(name, nz)
+    for name in "w_ss w_rs pair_ss pair_rs".split():
+        s.sems(name, 2)
+    for name in ("lt_ss", "lt_rs", "ltl_ss", "ltl_rs", "gp_ss", "gp_rs", "ra_ss", "ra_rs", "rv_ss", "rv_rs", "rq_ss", "rq_rs"):
+        s.sems(name, 2 * nd)
+    for name in ("eg_ss", "eg_rs"):
+        s.sems(name, nd - 1, 2)
+    for name in ("p_ss", "p_rs"):
+        s.sems(name, 4, nz)
+
+    def out(*shape, dtype=F32):
+        return jax.ShapeDtypeStruct(shape, dtype)
+
+    vmem = pl.BlockSpec(memory_space=pltpu.VMEM)
+    smem = pl.BlockSpec(memory_space=pltpu.SMEM)
+    hbm = pl.BlockSpec(memory_space=pl.ANY)
+    outs = pl.pallas_call(
+        functools.partial(layer_kernel, INPUTS + OUTPUTS + tuple(s.names), nd, nz, local),
+        out_shape=(
+            out(C, D, dtype=BF16),
+            out(C, D),
+            out(1, S),
+            out(S, HD),
+            out(S, HD),
+            out(S, EV),
+            out(S, EV),
+            out(S, EA * H),
+            out(S, EA * H),
+            out(S, experts),
+            out(local, D // nd, DH),
+            out(local, D // nd, DH),
+        ),
+        in_specs=[vmem, vmem, smem] + [vmem] * 6 + [hbm] * 6,
+        out_specs=[vmem] * 12,
+        scratch_shapes=s.shapes,
+        compiler_params=pltpu.CompilerParams(
+            collective_id=0, has_side_effects=True, vmem_limit_bytes=VMEM_LIMIT
+        ),
+    )(
+        tokens,
+        cotangent,
+        seq_lengths,
+        routes.T,
+        head_experts.reshape(C, 2 * H).T,
+        norm_gain.reshape(1, D),
+        w_value_gate,
+        w_output_gate,
+        w_router,
+        w_query,
+        w_key,
+        w_value,
+        w_output,
+        w_up,
+        w_down,
+    )
+    outs = list(outs)
+    outs[2] = outs[2].reshape(S)
+    return tuple(outs)
+
+
+VMEM_LIMIT = 62 * 1024 * 1024
+
+
+def fits(nd, nz, count, experts):
+    own_e = experts // nz
+    pad_e = -(-own_e // 16) * 16
+    return (
+        count == LANES
+        and nz * count <= 512
+        and own_e % 4 == 0
+        and D % (nd * nz * 2 * 16) == 0
+        and LANES % (D // (nd * nz * 2)) == 0
+        and 2 * EA * H + nz * pad_e <= LANES
+    )
+
+
+def per_device(nd, ne, *args):
+    count, experts = args[0].shape[0], args[12].shape[1]
+    if ne % 2 == 0 and fits(nd, ne // 2, count, experts):
+        return fused_layer(nd, ne // 2, *args)
+    return routed_layer(*args)
+
+
 def solution(mesh):
     return jax.shard_map(
-        per_device,
+        functools.partial(per_device, mesh.shape["dp"], mesh.shape["expert"]),
         mesh=mesh,
         in_specs=(
             P(("dp", "expert"), None),

time: 1810 us -> 166 us (0.09)
  waiting for transfers between devices: 1110 us -> 0 us
  blocking collectives: 326 us -> 0 us
  local copies, waits for them, and re-layouts: 179 us -> 23.3 us
  Pallas kernels: 0 us -> 142 us
  other arithmetic: 80.7 us -> 0 us
  matrix products: 69.7 us -> 0 us
    reduce_scatter x6 -> x0, waiting for transfers between devices: 561 us -> none  [the longest x1 157 us: per_device(): lax.psum_scatter(grad_output, ('dp', 'expert'), scatter_dimension=0, tile...]
    unnamed x12 -> x0, waiting for transfers between devices: 327 us -> none
    all_to_all x2 -> x0, blocking collectives: 288 us -> none  [the longest x1 146 us: per_device(): lax.all_to_all(outgoing, 'expert', split_axis=0, concat_axis=0, tiled=True)]
    all_to_all x2 -> x0, waiting for transfers between devices: 227 us -> none  [the longest x1 125 us: per_device(): lax.all_to_all(grad_items, 'expert', split_axis=0, concat_axis=0, tiled=T...]
    pallas_call x0 -> x1, Pallas kernels: none -> 142 us  [fused_layer(): pl.pallas_call(functools.partial(layer_kernel, INPUTS + OUTPUTS + tuple(s...]
    gather x26 -> x0, local copies, waits for them, and re-layouts: 112 us -> none  [the longest x1 17.4 us: per_device(): gate_flat[safe_row][:, None] * grad_out[source]]
    dot_general x33 -> x0, matrix products: 69.7 us -> none  [the longest x1 6.3 us: per_device(): jnp.einsum('nemd,nemf->edf', arrived, grad_raised, preferred_element_type...]
    unnamed x1 -> x0, blocking collectives: 38.1 us -> none
  transfers between devices with their start and end apart: 11 -> 0, of which waited for: 9 -> 0; matrix products, arithmetic and copies ran while one was open for 8% -> 0% of each run, Pallas kernels for 0% -> 0%
where the time goes in v1:
time: 166 us; the launch traced here: 165 us
  Pallas kernels  142 us (86%)
  local copies, waits for them, and re-layouts  23.3 us (14%)
    pallas_call x1, Pallas kernels, fused_layer(): pl.pallas_call(functools.partial(layer_kernel, INPUTS + OUTPUTS + tuple(s...  142 us
    unnamed x17, local copies, waits for them, and re-layouts  23.3 us

profile of v1, /device:TPU:0, one launch (start us, length us, event | category | flops | bytes accessed | tf_op | source)
XLA Modules:
  0.0 165.5 jit_solution(6991931521204009990)
XLA Ops:
  0.6 1.7 %copy.27.refs_6_ = bf16[1024,20]{1,0:T(8,128)(2,1)} copy(bf16[1024,20]{0,1:T(8,128)(2,1)} %param.25) | data formatting | bytes 81920 | tf_op args[10]
  2.3 1.7 %copy.28.refs_7_ = bf16[1024,20]{1,0:T(8,128)(2,1)} copy(bf16[1024,20]{0,1:T(8,128)(2,1)} %param.26) | data formatting | bytes 81920 | tf_op args[11]
  4.0 1.7 %copy.29.refs_8_ = bf16[1024,48]{1,0:T(8,128)(2,1)} copy(bf16[1024,48]{0,1:T(8,128)(2,1)} %param.27) | data formatting | bytes 196608 | tf_op args[12]
  5.7 141.5 %shard_map.238 = (bf16[128,1024]{1,0:T(8,128)(2,1)}, f32[128,1024]{1,0:T(8,128)}, f32[1,32]{1,0:T(1,128)}, f32[32,512]{1,0:T(8,128)}, f32[32,512]{1,0:T(8,128)},...) custom-call(bf16[128,1024]{1,0:T(8,128)(2,1)} %refs_0_.1, ...), custom_call_target="tpu_custom_call" | custom-call | tf_op jit(solution)/shard_map/pallas_call | solution.py:1188
  147.3 0.0 copy-start
  147.3 1.5 copy.30
  148.7 1.4 copy.31
  150.1 1.7 %copy.42 = bf16[128,1024]{1,0:T(8,128)(2,1)} copy(bf16[128,1024]{1,0:T(8,128)(2,1)} %get-tuple-element.60) | data formatting | bytes 524288
  151.8 1.9 %copy.43 = f32[128,1024]{1,0:T(8,128)} copy(f32[128,1024]{1,0:T(8,128)} %get-tuple-element.61) | data formatting | bytes 1048576
  153.7 1.2 copy.44
  154.8 1.5 copy.45
  156.3 1.5 copy.46
  157.8 1.7 %copy.47 = f32[32,2560]{1,0:T(8,128)} copy(f32[32,2560]{1,0:T(8,128)} %get-tuple-element.65) | data formatting | bytes 655360
  159.5 1.7 %copy.48 = f32[32,2560]{1,0:T(8,128)} copy(f32[32,2560]{1,0:T(8,128)} %get-tuple-element.66) | data formatting | bytes 655360
  161.2 1.3 copy.49
  162.6 2.1 %copy.50 = f32[6,256,128]{2,1,0:T(8,128)} copy(f32[6,256,128]{2,1,0:T(8,128)} %get-tuple-element.70) | data formatting | bytes 1572864
  164.6 0.0 copy-done
  164.6 0.9 copy.51
Async XLA Ops:
  147.3 17.4 %copy-start = (f32[6,256,128]{2,1,0:T(8,128)S(1)}, f32[6,256,128]{2,1,0:T(8,128)}, u32[]{:S(2)}) copy-start(f32[6,256,128]{2,1,0:T(8,128)} %get-tuple-element.71) | copy-start | bytes 2359300

commit v2 on v1

--- a/solution.py
+++ b/solution.py
@@ -558,11 +558,11 @@
     s_row, s_col = iota((GATE, LANES), 0), iota((GATE, LANES), 1)
     to_v = jnp.where(s_row == s_col, 1.0, 0.0).astype(BF16)
     to_o = jnp.where(s_row + GATE == s_col, 1.0, 0.0).astype(BF16)
-    R.wg_b[...] = (mm(R.wvg[...], to_v) + mm(R.wog[...], to_o)).astype(BF16)
-    experts = R.wr.shape[1]
+    R.wg_b[...] = (tmm(R.wvg[...], to_v) + tmm(R.wog[...], to_o)).astype(BF16)
+    experts = R.wr.shape[0]
     r_row, r_col = iota((experts, LANES), 0), iota((experts, LANES), 1)
     to_r = jnp.where((r_row == r_col + z * own_e) & (r_col < own_e), 1.0, 0.0).astype(BF16)
-    R.wrl_b[...] = mm(R.wr[...], to_r).astype(BF16)
+    R.wrl_b[...] = tmm(R.wr[...], to_r).astype(BF16)
 
     half = lax.rem(lane, DH // 2).astype(F32)
     angle = position * jnp.exp(half * (-2.0 / DH * math.log(rope_base)))
@@ -1059,12 +1059,12 @@
     got = line_total(3, PS)
 
     def pick(width, source):
-        a, b = iota((LANES, width), 0), iota((LANES, width), 1)
+        a, b = iota((width, LANES), 1), iota((width, LANES), 0)
         sel = jnp.where(a == source(b), 1.0, 0.0).astype(F32)
         return lax.dot_general(
+            sel,
             got,
-            sel,
-            (((1,), (0,)), ((), ())),
+            (((1,), (1,)), ((), ())),
             preferred_element_type=F32,
             precision=lax.Precision.HIGHEST,
         )
@@ -1104,6 +1104,12 @@
         sent(R.gz_s, R.gz_ss.at[o])
         for part, lanes in enumerate((PO, PV, PQ, PS)):
             sent(R.pb.at[pl.ds(times(o, S), S), lanes], R.p_ss.at[part, o])
+
+
+def settle_kernel(*refs):
+    n = len(refs) // 2
+    for src, dst in zip(refs[:n], refs[n:]):
+        dst[...] = src[...]
 
 
 def fused_layer(nd, nz, *args):
@@ -1195,9 +1201,9 @@
             out(S, HD),
             out(S, EV),
             out(S, EV),
-            out(S, EA * H),
-            out(S, EA * H),
-            out(S, experts),
+            out(EA * H, S),
+            out(EA * H, S),
+            out(experts, S),
             out(local, D // nd, DH),
             out(local, D // nd, DH),
         ),
@@ -1214,9 +1220,9 @@
         routes.T,
         head_experts.reshape(C, 2 * H).T,
         norm_gain.reshape(1, D),
-        w_value_gate,
-        w_output_gate,
-        w_router,
+        w_value_gate.T,
+        w_output_gate.T,
+        w_router.T,
         w_query,
         w_key,
         w_value,
@@ -1224,8 +1230,18 @@
         w_up,
         w_down,
     )
-    outs = list(outs)
+    outs = list(
+        pl.pallas_call(
+            settle_kernel,
+            out_shape=[out(*x.shape, dtype=x.dtype) for x in outs],
+            in_specs=[vmem] * 12,
+            out_specs=[vmem] * 12,
+            compiler_params=pltpu.CompilerParams(vmem_limit_bytes=VMEM_LIMIT),
+        )(*outs)
+    )
     outs[2] = outs[2].reshape(S)
+    for i in (7, 8, 9):
+        outs[i] = outs[i].T
     return tuple(outs)
 
 

time: 166 us -> 147 us (0.89)
  local copies, waits for them, and re-layouts: 23.3 us -> 1.42 us
  Pallas kernels: 142 us -> 145 us
    unnamed x17 -> x1, local copies, waits for them, and re-layouts: 23.3 us -> 1.42 us
    pallas_call x0 -> x1, Pallas kernels: none -> 3.62 us  [fused_layer(): pl.pallas_call(settle_kernel, out_shape=[out(*x.shape, dtype=x.dtype) for...]
where the time goes in v2:
time: 147 us
  Pallas kernels  145 us (99%)
    pallas_call x1, Pallas kernels, fused_layer(): pl.pallas_call(functools.partial(layer_kernel, INPUTS + OUTPUTS + tuple(s...  141 us
    pallas_call x1, Pallas kernels, fused_layer(): pl.pallas_call(settle_kernel, out_shape=[out(*x.shape, dtype=x.dtype) for...  3.62 us

profile of v2, /device:TPU:0, one launch (start us, length us, event | category | flops | bytes accessed | tf_op | source)
XLA Modules:
  0.0 147.1 jit_solution(425589893950166784)
XLA Ops:
  0.7 141.4 %shard_map.238 = (bf16[128,1024]{1,0:T(8,128)(2,1)}, f32[128,1024]{1,0:T(8,128)}, f32[1,32]{1,0:T(1,128)}, f32[32,512]{1,0:T(8,128)}, f32[32,512]{1,0:T(8,128)},...) custom-call(bf16[128,1024]{1,0:T(8,128)(2,1)} %refs_0_.1, ...), custom_call_target="tpu_custom_call" | custom-call | tf_op jit(solution)/shard_map/pallas_call | solution.py:1194
  142.1 3.6 %shard_map.239 = (bf16[128,1024]{1,0:T(8,128)(2,1)}, f32[128,1024]{1,0:T(8,128)}, f32[1,32]{1,0:T(1,128)}, f32[32,512]{1,0:T(8,128)}, f32[32,512]{1,0:T(8,128)},...) custom-call(bf16[128,1024]{1,0:T(8,128)(2,1)} %get-tuple-element.36., ...), custom_call_target="tpu_custom_call" | custom-call | tf_op jit(solution)/shard_map/pallas_call | solution.py:1234
  145.7 1.4 copy.27

commit v3 on v2

--- a/solution.py
+++ b/solution.py
@@ -438,8 +438,12 @@
     def sent(src, ss):
         remote(src, src, ss, ss, dev(p, z, sib)).wait_send()
 
+    beside = p + 1 - 2 * lax.rem(p, 2)
+    across = lax.rem(p + 2, nd)
+    diagonal = lax.rem(beside + 2, nd)
+
     def plane(k):
-        return lax.rem(p + k, nd)
+        return (p, beside, across, diagonal)[k]
 
     def line(k):
         return lax.rem(z + k, nz)
@@ -629,9 +633,6 @@
         shares = shifted / jnp.sum(shifted, axis=-1, keepdims=True)
         R.prob_b[h] = shares
         R.att_b[:, hs] = mm(shares.astype(BF16), R.v_b[:, hs])
-
-    for k in range(1, 2):
-        gather_step(R.cotb, R.cot_ss, R.cot_rs, k)
 
     for x in range(EA):
         for h in range(H):
@@ -647,6 +648,7 @@
         R.hid_f[:, cols] = hidden
         R.hidb[pl.ds(times(z, C), C), cols] = hidden.astype(BF16)
     gather_own(R.hidb, R.hid_ss, R.hid_rs)
+    gather_step(R.cotb, R.cot_ss, R.cot_rs, 1)
 
     def put_turned(x, w):
         for b in range(D // LANES):
@@ -681,12 +683,15 @@
         R.ltr[0, :, lanes] = R.lt[pl.ds(times(p * 2 + c, SL), SL), lanes]
         return out
 
+    def rows_at(buf, lanes, slot):
+        return buf.at[slot * C : (slot + 1) * C, lanes]
+
     def send_rows(buf, lanes, ss, rs):
         out = []
-        for k in range(1, nd):
+        for k in (1, 2):
             cp = remote(
-                buf.at[0:C, lanes],
-                buf.at[2 * k * C : (2 * k + 1) * C, lanes],
+                rows_at(buf, lanes, 0),
+                rows_at(buf, lanes, 2 * k),
                 ss.at[k],
                 rs.at[2 * k],
                 dev(plane(k), z, c),
@@ -697,8 +702,8 @@
 
     def hand_over(buf, lanes, ss, rs, k):
         cp = remote(
-            buf.at[2 * k * C : (2 * k + 1) * C, lanes],
-            buf.at[(2 * k + 1) * C : (2 * k + 2) * C, lanes],
+            rows_at(buf, lanes, 2 * k),
+            rows_at(buf, lanes, 2 * k + 1),
             ss.at[nd + k],
             rs.at[2 * k + 1],
             dev(p, z, sib),
@@ -706,14 +711,28 @@
         cp.start()
         return cp
 
-    def hand_all(buf, lanes, ss, rs, out):
-        for k in range(1, nd):
-            out[k - 1].wait_recv()
+    def hand_near(buf, lanes, ss, rs, out, via):
+        for k in (via, 3 - via):
+            arrived(rows_at(buf, lanes, 2 * k), rs.at[2 * k])
+            if k == via:
+                cp = remote(
+                    rows_at(buf, lanes, 2 * k),
+                    rows_at(buf, lanes, 6),
+                    ss.at[3],
+                    rs.at[6],
+                    dev(plane(3 - via), z, c),
+                )
+                cp.start()
+                out.append(cp)
             out.append(hand_over(buf, lanes, ss, rs, k))
+
+    def hand_far(buf, lanes, ss, rs, out):
+        arrived(rows_at(buf, lanes, 6), rs.at[6])
+        out.append(hand_over(buf, lanes, ss, rs, 3))
 
     def rows_here(buf, lanes, rs):
         for k in range(nd):
-            arrived(buf.at[(2 * k + 1) * C : (2 * k + 2) * C, lanes], rs.at[2 * k + 1])
+            arrived(rows_at(buf, lanes, 2 * k + 1), rs.at[2 * k + 1])
 
     put_turned(R.tokens[...], 0)
     put_turned(R.normed_b[...], 1)
@@ -731,6 +750,11 @@
         cp.wait()
 
     least = jnp.minimum(z, nz - 1 - z)
+    inner = least > 0
+    left_half = z < nz // 2
+    near = jnp.where(inner, jnp.where(left_half, 0, nz - 1), jnp.where(left_half, 1, nz - 2))
+    fellow = jnp.where(left_half, nz // 2, nz // 2 - 1)
+    far = jnp.where(left_half, nz - 1, 0)
 
     def origin(k):
         paired = k <= 2 * least
@@ -742,10 +766,16 @@
         o = origin(k)
         rows = pl.ds(times(o, C), C)
 
+        @pl.when((k == 1) & inner)
+        def _():
+            gather_on(R.hidb, R.hid_ss, R.hid_rs, origin(1))
+
+        @pl.when((k > 0) & (k + inner.astype(jnp.int32) < nz))
+        def _():
+            gather_on(R.hidb, R.hid_ss, R.hid_rs, origin(k + inner.astype(jnp.int32)))
+
         @pl.when(k > 0)
         def _():
-            gather_on(R.hidb, R.hid_ss, R.hid_rs, o)
-
             @pl.when((o == z - nz + 1) | (o == z + nz - 1))
             def _():
                 arrived(block(R.cotb, o), R.cot_rs.at[o])
@@ -758,12 +788,12 @@
         named = jnp.concatenate([named, jnp.zeros((LANES - pad_e, C), F32)], axis=0).T
         g = sigmoid(mm(hb, R.wrl_b[...])) * named
         glog = jnp.zeros((C, LANES), F32)
-        for q in range(own_e // 4):
-            cols = slice(q * 4 * DH, (q + 1) * 4 * DH)
+        for q in range(2):
+            cols = slice(q * HF, (q + 1) * HF)
             raised = mm(hb, R.wup_b[:, cols])
             back = mm(cb, R.wdn_b[:, cols])
-            for i in range(4):
-                j = q * 4 + i
+            for i in range(local):
+                j = q * local + i
                 u = raised[:, i * DH : (i + 1) * DH]
                 a = back[:, i * DH : (i + 1) * DH]
                 gj = column(g, j)
@@ -784,14 +814,160 @@
 
         @pl.when(k > 0)
         def _():
-            remote(R.gh_s.at[o], R.gh_r.at[z], R.gh_ss.at[o], R.gh_rs.at[z], dev(p, o, c)).start()
             remote(
                 R.glog_s.at[o], R.glog_r.at[z], R.gl_ss.at[o], R.gl_rs.at[z], dev(p, o, c)
             ).start()
 
+        @pl.when((k > 0) & (least == 0) & (o != fellow))
+        def _():
+            send_back(o)
+
+        @pl.when((k > 0) & (least == 0) & (o == fellow))
+        def _():
+            send_by(o, near, 0)
+
+        @pl.when((k > 0) & inner & (o == far))
+        def _():
+            send_by(o, fellow, 1)
+
         return carry
 
+    def send_back(o):
+        remote(R.gh_s.at[o], R.gh_r.at[z], R.gh_ss.at[o], R.gh_rs.at[z], dev(p, o, c)).start()
+
+    def send_by(o, by, slot):
+        remote(
+            R.gh_s.at[o], R.gh_x.at[slot], R.gh_ss.at[o], R.gx_rs.at[slot], dev(p, by, c)
+        ).start()
+
+    def relay_back(o, slot):
+        arrived(R.gh_x.at[slot], R.gx_rs.at[slot])
+        R.gh_s[o] = (R.gh_s[o].astype(F32) + R.gh_x[slot].astype(F32)).astype(BF16)
+        send_back(o)
+
     lax.fori_loop(0, nz, expert_block, 0)
+
+    pairs = {}
+
+    def expert_grad(buf, left_of, right_of, whose):
+        cols = pl.ds(times(whose, HF), HF)
+        buf[:, cols] = tmm(left_of[...], right_of[:, cols]).astype(BF16)
+
+    def to_fellow_core(i, buf):
+        cp = remote(
+            buf.at[:, pl.ds(times(sib, HF), HF)],
+            R.pair_r.at[i],
+            R.pair_ss.at[i],
+            R.pair_rs.at[i],
+            dev(p, z, sib),
+        )
+        cp.start()
+        pairs[i] = cp
+
+    own_cols = pl.ds(times(c, HF), HF)
+    rows_d = D // nd
+    plane_out = []
+
+    def expert_grad_on(i, buf):
+        pairs[i].wait()
+
+        def pair_tile(t, carry):
+            rows = pl.ds(times(t, 128), 128)
+            buf[rows, own_cols] = (
+                buf[rows, own_cols].astype(F32) + R.pair_r[i, rows, :].astype(F32)
+            ).astype(BF16)
+            return carry
+
+        lax.fori_loop(0, D // 128, pair_tile, 0)
+        part_on(i, buf, diagonal, beside if i == 0 else across, 1)
+
+    def rows_of(at):
+        return pl.ds(times(at, rows_d), rows_d)
+
+    def part_on(i, buf, whose, to, slot):
+        cp = remote(
+            buf.at[rows_of(whose), own_cols],
+            R.eg_r.at[slot, i],
+            R.eg_ss.at[slot, i],
+            R.eg_rs.at[slot, i],
+            dev(to, z, c),
+        )
+        cp.start()
+        plane_out.append(cp)
+
+    def expert_grad_relay(i, buf):
+        first, to = (beside, across) if i == 0 else (across, beside)
+        part_on(i, buf, first, first, 0)
+        arrived(R.eg_r.at[1, i], R.eg_rs.at[1, i])
+        rows = rows_of(to)
+        buf[rows, own_cols] = (
+            buf[rows, own_cols].astype(F32) + R.eg_r[1, i].astype(F32)
+        ).astype(BF16)
+        part_on(i, buf, to, to, 2)
+
+    def to_place(own, got, ss, rs, o):
+        remote(own(o), got(z), ss.at[o], rs.at[z], dev(p, o, c)).start()
+
+    def sum_out(own, got, ss, rs, via, via_sem):
+        @pl.when(inner)
+        def _():
+            to_place(own, got, ss, rs, far)
+            to_place(own, got, ss, rs, near)
+
+        @pl.when(least == 0)
+        def _():
+            remote(own(fellow), via, ss.at[fellow], via_sem, dev(p, near, c)).start()
+            to_place(own, got, ss, rs, far)
+            to_place(own, got, ss, rs, near)
+
+    def sum_on(own, got, ss, rs, via, via_sem):
+        @pl.when(inner)
+        def _():
+            arrived(via, via_sem)
+            own(fellow)[...] = (own(fellow)[...].astype(F32) + via[...].astype(F32)).astype(BF16)
+            to_place(own, got, ss, rs, fellow)
+
+    def sum_in(total, got, rs):
+        def add(o):
+            arrived(got(o), rs.at[o])
+            total[...] += got(o)[...].astype(F32)
+
+        add(near)
+        add(fellow)
+
+        @pl.when(least == 0)
+        def _():
+            add(far)
+
+    def out_run(k, n):
+        def hand(d, slot, to):
+            if k > 1:
+                arrived(R.out_r.at[d], R.out_rs.at[d])
+                R.out_s[d] = (R.out_s[d].astype(F32) + R.out_r[d].astype(F32)).astype(BF16)
+            remote(
+                R.out_s.at[d], R.out_r.at[slot], R.out_ss.at[d], R.out_rs.at[slot], dev(p, to, c)
+            ).start()
+
+        @pl.when(z == k - 1)
+        def _():
+            hand(nz - 1 - n, nz - 1 - n, k)
+
+        @pl.when(z == nz - k)
+        def _():
+            hand(n, nz if n == nz - k - 1 else n, nz - k - 1)
+
+    def part_sum(i, lanes):
+        return (
+            lambda o: R.pb.at[pl.ds(times(o, S), S), lanes],
+            lambda o: R.pr.at[o, :, lanes],
+            R.p_ss.at[i],
+            R.p_rs.at[i],
+        )
+
+    hand_near(R.ra, RA, R.ra_ss, R.ra_rs, ra_out, 2)
+    expert_grad(R.wup_b, R.hidb, R.gra, sib)
+    to_fellow_core(1, R.wup_b)
+    expert_grad(R.wup_b, R.hidb, R.gra, c)
 
     def out_tile(t, carry):
         rows = pl.ds(times(t, 256), 256)
@@ -801,43 +977,37 @@
         return carry
 
     lax.fori_loop(0, D // 256, out_tile, 0)
+    out_run(1, 0)
+    expert_grad(R.wdn_b, R.cotb, R.gact, sib)
+    to_fellow_core(0, R.wdn_b)
+
+    @pl.when(inner)
+    def _():
+        relay_back(near, 1)
+        relay_back(fellow, 0)
+
+    expert_grad_on(1, R.wup_b)
+    expert_grad(R.wdn_b, R.cotb, R.gact, c)
+    expert_grad_on(0, R.wdn_b)
+    hand_far(R.ra, RA, R.ra_ss, R.ra_rs, ra_out)
+
+    out_run(1, 1)
+    out_run(2, 0)
+
+    R.ghid_f[...] = R.cotb[pl.ds(times(z, C), C), :].astype(F32) + R.gh_s[z].astype(F32)
+
+    def add_back(o):
+        arrived(R.gh_r.at[o], R.gh_rs.at[o])
+        R.ghid_f[...] += R.gh_r[o].astype(F32)
+
+    add_back(near)
+    add_back(jnp.where(inner, fellow, far))
+
     for k in range(1, nz):
         o = line(k)
-        remote(R.out_s.at[o], R.out_r.at[z], R.out_ss.at[o], R.out_rs.at[z], dev(p, o, c)).start()
-
-    pairs = []
-    for i, (left_of, right_of, buf) in enumerate(
-        ((R.cotb, R.gact, R.wdn_b), (R.hidb, R.gra, R.wup_b))
-    ):
-
-        def grad_tile(t, carry, base):
-            cols = pl.ds(pl.multiple_of(base + t * 256, 256), 256)
-            buf[:, cols] = tmm(left_of[...], right_of[:, cols]).astype(BF16)
-            return carry
-
-        lax.fori_loop(0, HF // 256, functools.partial(grad_tile, base=sib * HF), 0)
-        cp = remote(
-            buf.at[:, pl.ds(times(sib, HF), HF)],
-            R.pair_r.at[i],
-            R.pair_ss.at[i],
-            R.pair_rs.at[i],
-            dev(p, z, sib),
-        )
-        cp.start()
-        pairs.append(cp)
-        lax.fori_loop(0, HF // 256, functools.partial(grad_tile, base=c * HF), 0)
-
-    hand_all(R.ra, RA, R.ra_ss, R.ra_rs, ra_out)
-
-    ghid = R.cotb[pl.ds(times(z, C), C), :].astype(F32) + R.gh_s[z].astype(F32)
-    for k in range(1, nz):
-        o = line(k)
-        arrived(R.gh_r.at[o], R.gh_rs.at[o])
         arrived(R.glog_r.at[o], R.gl_rs.at[o])
-        ghid = ghid + R.gh_r[o].astype(F32)
     R.glog_r[z] = R.glog_s[z]
-    R.ghid_f[...] = ghid
-    R.ghid_b[...] = ghid.astype(BF16)
+    R.ghid_b[...] = R.ghid_f[...].astype(BF16)
     put_turned(R.ghid_f[...], 3)
     turned_late = send_turned(3, 4, R.ltl_ss, R.ltl_rs)
 
@@ -894,47 +1064,6 @@
     RQ = slice(q0, q0 + 2 * HD)
     rq_out = send_rows(R.rb, RQ, R.rq_ss, R.rq_rs)
 
-    for cp in turned:
-        cp.wait()
-    rows_here(R.ra, RA, R.ra_rs)
-    for cp in turned_late:
-        cp.wait()
-
-    def turned_of(w):
-        return jnp.concatenate(
-            [R.ltr[s, :, w * LANES : (w + 1) * LANES] for s in range(2 * nd)], axis=1
-        )
-
-    def send_part(part, lanes):
-        for k in range(1, nz):
-            o = line(k)
-            remote(
-                R.pb.at[pl.ds(times(o, S), S), lanes],
-                R.pr.at[z, :, lanes],
-                R.p_ss.at[part, o],
-                R.p_rs.at[part, z],
-                dev(p, o, c),
-            ).start()
-
-    def gated_grad(w, rows_of, g0, at):
-        left = turned_of(w)
-        for x in range(EA):
-            right = []
-            for h in range(H):
-                gx = column(R.ra[:, HD : HD + LANES], g0 + x * H + h).astype(F32)
-                right.append((gx * rows_of[:, h * DH : (h + 1) * DH].astype(F32)).astype(BF16))
-            right = jnp.concatenate(right, axis=1)
-            R.pb[:, at + x * HD : at + (x + 1) * HD] = mm(left, right).astype(BF16)
-
-    PO, PV, PQ, PS = (
-        slice(0, EV),
-        slice(EV, 2 * EV),
-        slice(2 * EV, 2 * EV + 2 * HD),
-        slice(2 * EV + 2 * HD, 2 * EV + 2 * HD + LANES),
-    )
-    gated_grad(3, R.ra, GATE, 0)
-    send_part(0, PO)
-
     gproj = mm_t(R.rb[0:C, RQ], R.wqk_b[...])
     standard = R.std_b[...]
     column_sum = jnp.sum(gproj * standard, axis=0, keepdims=True)
@@ -949,7 +1078,77 @@
         cp.start()
         gain_out.append(cp)
 
-    hand_all(R.rb, RV, R.rv_ss, R.rv_rs, rv_out)
+    out_run(1, 2)
+    out_run(2, 1)
+    out_run(3, 0)
+    for cp in turned:
+        cp.wait()
+    rows_here(R.ra, RA, R.ra_rs)
+    for cp in turned_late:
+        cp.wait()
+
+    def turned_of(w):
+        return jnp.concatenate(
+            [R.ltr[s, :, w * LANES : (w + 1) * LANES] for s in range(2 * nd)], axis=1
+        )
+
+    def send_part(part, lanes):
+        for o in (far, fellow, near):
+            to_place(*part_sum(part, lanes), o)
+
+    def gated_grad(w, rows_of, g0, at):
+        left = turned_of(w)
+        for x in range(EA):
+            right = []
+            for h in range(H):
+                gx = column(R.ra[:, HD : HD + LANES], g0 + x * H + h).astype(F32)
+                right.append((gx * rows_of[:, h * DH : (h + 1) * DH].astype(F32)).astype(BF16))
+            right = jnp.concatenate(right, axis=1)
+            R.pb[:, at + x * HD : at + (x + 1) * HD] = mm(left, right).astype(BF16)
+
+    PO, PV, PQ, PS = (
+        slice(0, EV),
+        slice(EV, 2 * EV),
+        slice(2 * EV, 2 * EV + 2 * HD),
+        slice(2 * EV + 2 * HD, 2 * EV + 2 * HD + LANES),
+    )
+    gated_grad(3, R.ra, GATE, 0)
+    sum_out(*part_sum(0, PO), R.px.at[0], R.px_rs.at[0])
+
+    hand_near(R.rb, RV, R.rv_ss, R.rv_rs, rv_out, 2)
+    hand_near(R.rb, RQ, R.rq_ss, R.rq_rs, rq_out, 1)
+    hand_far(R.rb, RV, R.rv_ss, R.rv_rs, rv_out)
+    expert_grad_relay(0, R.wdn_b)
+    expert_grad_relay(1, R.wup_b)
+    total = R.gp[0]
+    for cp, (k, dc) in zip(gain_out, plane_all):
+        cp.wait()
+        total = total + R.gp[2 * k + dc]
+    R.gz_s[...] = total
+    for k in range(1, nz):
+        o = line(k)
+        remote(R.gz_s, R.gz.at[z], R.gz_ss.at[o], R.gz_rs.at[z], dev(p, o, c)).start()
+
+    rows_here(R.rb, RV, R.rv_rs)
+    gated_grad(0, R.rb, 0, EV)
+    sum_out(*part_sum(1, PV), R.px.at[1], R.px_rs.at[1])
+    sum_on(*part_sum(0, PO), R.px.at[0], R.px_rs.at[0])
+    hand_far(R.rb, RQ, R.rq_ss, R.rq_rs, rq_out)
+    lane_s = iota((SL, LANES), 1)
+    small_t = mm(turned_of(0), R.rb[:, HD : HD + LANES])
+    small_h = mm(turned_of(2), R.rb[:, HD : HD + LANES])
+    R.pb[:, PS] = jnp.where(lane_s < 2 * GATE, small_t, small_h).astype(BF16)
+    send_part(3, PS)
+    rows_here(R.rb, RQ, R.rq_rs)
+    left = turned_of(1)
+    for b in range(2):
+        lo = q0 + b * HD
+        R.pb[:, 2 * EV + b * HD : 2 * EV + (b + 1) * HD] = mm(left, R.rb[:, lo : lo + HD]).astype(
+            BF16
+        )
+    send_part(2, PQ)
+    sum_on(*part_sum(1, PV), R.px.at[1], R.px_rs.at[1])
+
 
     inputs = R.tokens[...].astype(F32)
     centred = inputs - jnp.mean(inputs, axis=-1, keepdims=True)
@@ -973,65 +1172,19 @@
             R.small_b[...], R.wg_b[cols, :]
         )
 
-    rows_here(R.rb, RV, R.rv_rs)
-    gated_grad(0, R.rb, 0, EV)
-    send_part(1, PV)
-    hand_all(R.rb, RQ, R.rq_ss, R.rq_rs, rq_out)
-    lane_s = iota((SL, LANES), 1)
-    small_t = mm(turned_of(0), R.rb[:, HD : HD + LANES])
-    small_h = mm(turned_of(2), R.rb[:, HD : HD + LANES])
-    R.pb[:, PS] = jnp.where(lane_s < 2 * GATE, small_t, small_h).astype(BF16)
-    send_part(3, PS)
-    rows_here(R.rb, RQ, R.rq_rs)
-    left = turned_of(1)
-    for b in range(2):
-        lo = q0 + b * HD
-        R.pb[:, 2 * EV + b * HD : 2 * EV + (b + 1) * HD] = mm(left, R.rb[:, lo : lo + HD]).astype(
-            BF16
-        )
-    send_part(2, PQ)
-
-    own_cols = pl.ds(times(c, HF), HF)
-    rows_d = D // nd
-    plane_out = []
-    for i, buf in enumerate((R.wdn_b, R.wup_b)):
-        pairs[i].wait()
-
-        def pair_tile(t, carry):
-            rows = pl.ds(times(t, 128), 128)
-            buf[rows, own_cols] = (
-                buf[rows, own_cols].astype(F32) + R.pair_r[i, rows, :].astype(F32)
-            ).astype(BF16)
-            return carry
-
-        lax.fori_loop(0, D // 128, pair_tile, 0)
-        for k in range(1, nd):
-            to = plane(k)
-            cp = remote(
-                buf.at[pl.ds(times(to, rows_d), rows_d), own_cols],
-                R.eg_r.at[k - 1, i],
-                R.eg_ss.at[k - 1, i],
-                R.eg_rs.at[k - 1, i],
-                dev(to, z, c),
-            )
-            cp.start()
-            plane_out.append(cp)
-
-    total = R.gp[0]
-    for cp, (k, dc) in zip(gain_out, plane_all):
-        cp.wait()
-        total = total + R.gp[2 * k + dc]
-    R.gz_s[...] = total
-    for k in range(1, nz):
-        o = line(k)
-        remote(R.gz_s, R.gz.at[z], R.gz_ss.at[o], R.gz_rs.at[z], dev(p, o, c)).start()
-
-    out = R.hid_f[...] + R.out_s[z].astype(F32)
-    for k in range(1, nz):
-        o = line(k)
-        arrived(R.out_r.at[o], R.out_rs.at[o])
-        out = out + R.out_r[o].astype(F32)
-    R.mixed[...] = out.astype(BF16)
+    R.hid_f[...] += R.out_s[z].astype(F32)
+
+    @pl.when(z > 0)
+    def _():
+        arrived(R.out_r.at[z], R.out_rs.at[z])
+        R.hid_f[...] += R.out_r[z].astype(F32)
+
+    @pl.when(z < nz - 1)
+    def _():
+        arrived(R.out_r.at[nz], R.out_rs.at[nz])
+        R.hid_f[...] += R.out_r[nz].astype(F32)
+
+    R.mixed[...] = R.hid_f[...].astype(BF16)
 
     for k in range(1, nz):
         o = line(k)
@@ -1054,16 +1207,19 @@
             got = got + R.pr[o, :, lanes].astype(F32)
         return got
 
-    R.go[...] = line_total(0, PO)
-    R.gv[...] = line_total(1, PV)
+    for i, (dst, lanes) in enumerate(((R.go, PO), (R.gv, PV))):
+        dst[...] = R.pb[own_rows, lanes].astype(F32)
+        sum_in(dst, part_sum(i, lanes)[1], R.p_rs.at[i])
     got = line_total(3, PS)
 
     def pick(width, source):
         a, b = iota((width, LANES), 1), iota((width, LANES), 0)
-        sel = jnp.where(a == source(b), 1.0, 0.0).astype(F32)
+        return jnp.where(a == source(b), 1.0, 0.0).astype(F32)
+
+    def picked(left, right):
         return lax.dot_general(
-            sel,
-            got,
+            left,
+            right,
             (((1,), (1,)), ((), ())),
             preferred_element_type=F32,
             precision=lax.Precision.HIGHEST,
@@ -1075,21 +1231,21 @@
             at = jnp.where(b >= o * own_e, 2 * GATE + o * pad_e + b - o * own_e, at)
         return at
 
-    R.gvg[...] = pick(GATE, lambda b: b)
-    R.gog[...] = pick(GATE, lambda b: b + GATE)
-    R.gr[...] = pick(experts, router_lane)
+    R.gvg[...] = picked(pick(GATE, lambda b: b), got)
+    R.gog[...] = picked(pick(GATE, lambda b: b + GATE), got)
+    R.gr[...] = picked(got, pick(experts, router_lane))
     got = line_total(2, PQ)
     R.gq[...] = got[:, 0:HD]
     R.gk[...] = got[:, HD : 2 * HD]
 
     for i, (buf, dst) in enumerate(((R.wdn_b, R.gdn), (R.wup_b, R.gup))):
-        for k in range(1, nd):
-            plane_out[i * (nd - 1) + k - 1].wait_recv()
-        rows = pl.ds(times(p, rows_d), rows_d)
+        for slot in (0, 2):
+            arrived(R.eg_r.at[slot, i], R.eg_rs.at[slot, i])
+        rows = rows_of(p)
         for x in range(local):
             got = buf[rows, pl.ds(times(c * local + x, DH), DH)].astype(F32)
-            for k in range(1, nd):
-                got = got + R.eg_r[k - 1, i, :, x * DH : (x + 1) * DH].astype(F32)
+            for slot in (0, 2):
+                got = got + R.eg_r[slot, i, :, x * DH : (x + 1) * DH].astype(F32)
             dst[x] = got
 
     gather_end(R.cotb, R.cot_ss)
@@ -1155,8 +1311,10 @@
     s.vmem("rb", (2 * nd * C, 3 * HD + LANES), BF16)
     s.vmem("gact", (nz * C, EF), BF16)
     s.vmem("gra", (nz * C, EF), BF16)
-    for name in ("gh_s", "gh_r", "out_s", "out_r"):
+    for name in ("gh_s", "gh_r", "out_s"):
         s.vmem(name, (nz, C, D), BF16)
+    s.vmem("out_r", (nz + 1, C, D), BF16)
+    s.vmem("gh_x", (2, C, D), BF16)
     for name in ("glog_s", "glog_r"):
         s.vmem(name, (nz, pad_e, C), BF16)
     s.vmem("pair_r", (2, D, HF), BF16)
@@ -1168,13 +1326,17 @@
     s.vmem("small_b", (C, LANES), BF16)
     s.vmem("pb", (SL, PW), BF16)
     s.vmem("pr", (nz, S, PW), BF16)
+    s.vmem("px", (2, S, EV), BF16)
     s.vmem("gp", (2 * nd, D // LANES, LANES), F32)
     s.vmem("gz_s", (D // LANES, LANES), F32)
     s.vmem("gz", (nz, D // LANES, LANES), F32)
     s.sems("ld", 4 + 2 * local)
+    s.sems("gx_rs", 2)
+    s.sems("out_rs", nz + 1)
+    s.sems("px_rs", 2)
     for name in ("cot_ss", "hid_ss"):
         s.sems(name, 2, nz)
-    for name in ("cot_rs", "hid_rs", "mask_ss", "mask_rs", "gh_ss", "gh_rs", "gl_ss", "gl_rs", "out_ss", "out_rs", "gz_ss", "gz_rs"):
+    for name in ("cot_rs", "hid_rs", "mask_ss", "mask_rs", "gh_ss", "gh_rs", "gl_ss", "gl_rs", "out_ss", "gz_ss", "gz_rs"):
         s.sems(name, nz)
     for name in "w_ss w_rs pair_ss pair_rs".split():
         s.sems(name, 2)
@@ -1203,7 +1365,7 @@
             out(S, EV),
             out(EA * H, S),
             out(EA * H, S),
-            out(experts, S),
+            out(S, experts),
             out(local, D // nd, DH),
             out(local, D // nd, DH),
         ),
@@ -1240,7 +1402,7 @@
         )(*outs)
     )
     outs[2] = outs[2].reshape(S)
-    for i in (7, 8, 9):
+    for i in (7, 8):
         outs[i] = outs[i].T
     return tuple(outs)
 
@@ -1253,7 +1415,8 @@
     pad_e = -(-own_e // 16) * 16
     return (
         count == LANES
-        and nz * count <= 512
+        and nz == 4
+        and nd == 4
         and own_e % 4 == 0
         and D % (nd * nz * 2 * 16) == 0
         and LANES % (D // (nd * nz * 2)) == 0

time: 147 us -> 111 us (0.76)
  Pallas kernels: 145 us -> 110 us
    pallas_call x1, Pallas kernels: 141 us -> 107 us  [fused_layer(): pl.pallas_call(functools.partial(layer_kernel, INPUTS + OUTPUTS + tuple(s...]
where the time goes in v3:
time: 111 us
  Pallas kernels  110 us (99%)
    pallas_call x1, Pallas kernels, fused_layer(): pl.pallas_call(functools.partial(layer_kernel, INPUTS + OUTPUTS + tuple(s...  107 us
    pallas_call x1, Pallas kernels, fused_layer(): pl.pallas_call(settle_kernel, out_shape=[out(*x.shape, dtype=x.dtype) for...  3.62 us

profile of v3, /device:TPU:0, one launch (start us, length us, event | category | flops | bytes accessed | tf_op | source)
XLA Modules:
  0.0 110.9 jit_solution(2077286003622440354)
XLA Ops:
  0.7 106.7 %shard_map.238 = (bf16[128,1024]{1,0:T(8,128)(2,1)}, f32[128,1024]{1,0:T(8,128)}, f32[1,32]{1,0:T(1,128)}, f32[32,512]{1,0:T(8,128)}, f32[32,512]{1,0:T(8,128)},...) custom-call(bf16[128,1024]{1,0:T(8,128)(2,1)} %refs_0_.1, ...), custom_call_target="tpu_custom_call" | custom-call | tf_op jit(solution)/shard_map/pallas_call | solution.py:1356
  107.3 3.6 %shard_map.239 = (bf16[128,1024]{1,0:T(8,128)(2,1)}, f32[128,1024]{1,0:T(8,128)}, f32[1,32]{1,0:T(1,128)}, f32[32,512]{1,0:T(8,128)}, f32[32,512]{1,0:T(8,128)},...) custom-call(bf16[128,1024]{1,0:T(8,128)(2,1)} %get-tuple-element.36., ...), custom_call_target="tpu_custom_call" | custom-call | tf_op jit(solution)/shard_map/pallas_call | solution.py:1396

commit v4 on v3

--- a/solution.py
+++ b/solution.py
@@ -686,9 +686,9 @@
     def rows_at(buf, lanes, slot):
         return buf.at[slot * C : (slot + 1) * C, lanes]
 
-    def send_rows(buf, lanes, ss, rs):
+    def send_rows(buf, lanes, ss, rs, ways=(1, 2)):
         out = []
-        for k in (1, 2):
+        for k in ways:
             cp = remote(
                 rows_at(buf, lanes, 0),
                 rows_at(buf, lanes, 2 * k),
@@ -712,7 +712,7 @@
         return cp
 
     def hand_near(buf, lanes, ss, rs, out, via):
-        for k in (via, 3 - via):
+        for k in (via, 3 - via) if via else (1, 2):
             arrived(rows_at(buf, lanes, 2 * k), rs.at[2 * k])
             if k == via:
                 cp = remote(
@@ -743,9 +743,6 @@
     RA = slice(0, HD + LANES)
     ra_out = send_rows(R.ra, RA, R.ra_ss, R.ra_rs)
 
-    for k in range(2, nz - 1):
-        gather_step(R.cotb, R.cot_ss, R.cot_rs, k)
-
     for cp in wx:
         cp.wait()
 
@@ -773,6 +770,11 @@
         @pl.when((k > 0) & (k + inner.astype(jnp.int32) < nz))
         def _():
             gather_on(R.hidb, R.hid_ss, R.hid_rs, origin(k + inner.astype(jnp.int32)))
+
+        @pl.when(k == 1)
+        def _():
+            for far_step in range(2, nz - 1):
+                gather_step(R.cotb, R.cot_ss, R.cot_rs, far_step)
 
         @pl.when(k > 0)
         def _():
@@ -830,6 +832,21 @@
         def _():
             send_by(o, fellow, 1)
 
+        @pl.when((k == 2) & (least == 0))
+        def _():
+            there = pl.ds(times(near, C), C)
+            for b in range(2):
+                cols = slice(b * half_d, (b + 1) * half_d)
+                R.out_s[near, :, cols] = mm_t(R.gact[there, :], R.wdn_b[cols, :]).astype(BF16)
+            slot = jnp.where(z == 0, near, nz)
+            remote(
+                R.out_s.at[near],
+                R.out_r.at[slot],
+                R.out_ss.at[near],
+                R.out_rs.at[slot],
+                dev(p, near, c),
+            ).start()
+
         return carry
 
     def send_back(o):
@@ -849,104 +866,69 @@
 
     pairs = {}
 
-    def expert_grad(buf, left_of, right_of, whose):
-        cols = pl.ds(times(whose, HF), HF)
-        buf[:, cols] = tmm(left_of[...], right_of[:, cols]).astype(BF16)
-
-    def to_fellow_core(i, buf):
-        cp = remote(
-            buf.at[:, pl.ds(times(sib, HF), HF)],
-            R.pair_r.at[i],
-            R.pair_ss.at[i],
-            R.pair_rs.at[i],
-            dev(p, z, sib),
-        )
-        cp.start()
-        pairs[i] = cp
-
-    own_cols = pl.ds(times(c, HF), HF)
+    def rows_of(at):
+        return pl.ds(times(at, rows_d), rows_d)
+
+
     rows_d = D // nd
     plane_out = []
 
-    def expert_grad_on(i, buf):
-        pairs[i].wait()
-
-        def pair_tile(t, carry):
-            rows = pl.ds(times(t, 128), 128)
-            buf[rows, own_cols] = (
-                buf[rows, own_cols].astype(F32) + R.pair_r[i, rows, :].astype(F32)
-            ).astype(BF16)
-            return carry
-
-        lax.fori_loop(0, D // 128, pair_tile, 0)
-        part_on(i, buf, diagonal, beside if i == 0 else across, 1)
-
-    def rows_of(at):
-        return pl.ds(times(at, rows_d), rows_d)
-
-    def part_on(i, buf, whose, to, slot):
+    def half(cc):
+        return pl.ds(times(cc, HF), HF)
+
+    def grad_at(i, k, cc):
+        if i == 0 and k == 3:
+            return R.dg.at[:, half(cc)]
+        return (R.wdn_b, R.wup_b)[i].at[rows_of(plane(k)), half(cc)]
+
+    def expert_grad(i, k):
+        left, right = ((R.cotb, R.gact), (R.hidb, R.gra))[i]
+        for cc in (sib, c):
+            grad_at(i, k, cc)[...] = tmm(left[:, rows_of(plane(k))], right[:, half(cc)]).astype(BF16)
+            if cc is sib:
+                cp = remote(
+                    grad_at(i, k, sib),
+                    R.pair_r.at[i, k],
+                    R.pair_ss.at[i, k],
+                    R.pair_rs.at[i, k],
+                    dev(p, z, sib),
+                )
+                cp.start()
+                pairs[i, k] = cp
+
+    def pair_sum(i, k):
+        pairs[i, k].wait()
+        own = grad_at(i, k, c)
+        own[...] = (own[...].astype(F32) + R.pair_r[i, k].astype(F32)).astype(BF16)
+
+    def part_on(i, k, to, slot):
         cp = remote(
-            buf.at[rows_of(whose), own_cols],
+            grad_at(i, k, c),
             R.eg_r.at[slot, i],
             R.eg_ss.at[slot, i],
             R.eg_rs.at[slot, i],
-            dev(to, z, c),
+            dev(plane(to), z, c),
         )
         cp.start()
         plane_out.append(cp)
 
-    def expert_grad_relay(i, buf):
-        first, to = (beside, across) if i == 0 else (across, beside)
-        part_on(i, buf, first, first, 0)
+    def expert_grad_relay(i):
+        first, second = (1, 2) if i == 0 else (2, 1)
+        part_on(i, first, first, 0)
         arrived(R.eg_r.at[1, i], R.eg_rs.at[1, i])
-        rows = rows_of(to)
-        buf[rows, own_cols] = (
-            buf[rows, own_cols].astype(F32) + R.eg_r[1, i].astype(F32)
-        ).astype(BF16)
-        part_on(i, buf, to, to, 2)
+        own = grad_at(i, second, c)
+        own[...] = (own[...].astype(F32) + R.eg_r[1, i].astype(F32)).astype(BF16)
+        part_on(i, second, second, 2)
 
     def to_place(own, got, ss, rs, o):
         remote(own(o), got(z), ss.at[o], rs.at[z], dev(p, o, c)).start()
 
-    def sum_out(own, got, ss, rs, via, via_sem):
-        @pl.when(inner)
-        def _():
-            to_place(own, got, ss, rs, far)
-            to_place(own, got, ss, rs, near)
-
-        @pl.when(least == 0)
-        def _():
-            remote(own(fellow), via, ss.at[fellow], via_sem, dev(p, near, c)).start()
-            to_place(own, got, ss, rs, far)
-            to_place(own, got, ss, rs, near)
-
-    def sum_on(own, got, ss, rs, via, via_sem):
-        @pl.when(inner)
-        def _():
-            arrived(via, via_sem)
-            own(fellow)[...] = (own(fellow)[...].astype(F32) + via[...].astype(F32)).astype(BF16)
-            to_place(own, got, ss, rs, fellow)
-
-    def sum_in(total, got, rs):
-        def add(o):
-            arrived(got(o), rs.at[o])
-            total[...] += got(o)[...].astype(F32)
-
-        add(near)
-        add(fellow)
-
-        @pl.when(least == 0)
-        def _():
-            add(far)
-
-    def out_run(k, n):
+    def run(own, got, ss, rs, k, n):
         def hand(d, slot, to):
             if k > 1:
-                arrived(R.out_r.at[d], R.out_rs.at[d])
-                R.out_s[d] = (R.out_s[d].astype(F32) + R.out_r[d].astype(F32)).astype(BF16)
-            remote(
-                R.out_s.at[d], R.out_r.at[slot], R.out_ss.at[d], R.out_rs.at[slot], dev(p, to, c)
-            ).start()
+                arrived(got(d), rs.at[d])
+                own(d)[...] = (own(d)[...].astype(F32) + got(d)[...].astype(F32)).astype(BF16)
+            remote(own(d), got(slot), ss.at[d], rs.at[slot], dev(p, to, c)).start()
 
         @pl.when(z == k - 1)
         def _():
@@ -955,44 +937,67 @@
         @pl.when(z == nz - k)
         def _():
             hand(n, nz if n == nz - k - 1 else n, nz - k - 1)
+
+    def run_end(total, got, rs):
+        for there, slot in ((z > 0, z), (z < nz - 1, nz)):
+
+            @pl.when(there)
+            def _():
+                arrived(got(slot), rs.at[slot])
+                total[...] += got(slot)[...].astype(F32)
+
+    out_sum = (lambda d: R.out_s.at[d], lambda d: R.out_r.at[d], R.out_ss, R.out_rs)
+    out_run = functools.partial(run, *out_sum)
+
+    def grad_sum(i, lanes):
+        return (
+            lambda d: R.pb.at[d * S : (d + 1) * S, lanes],
+            lambda d: R.pn.at[i, d],
+            R.pn_ss.at[i],
+            R.pn_rs.at[i],
+        )
 
     def part_sum(i, lanes):
         return (
             lambda o: R.pb.at[pl.ds(times(o, S), S), lanes],
-            lambda o: R.pr.at[o, :, lanes],
+            lambda o: R.pr.at[o, :, slice(lanes.start - 2 * EV, lanes.stop - 2 * EV)],
             R.p_ss.at[i],
             R.p_rs.at[i],
         )
 
     hand_near(R.ra, RA, R.ra_ss, R.ra_rs, ra_out, 2)
-    expert_grad(R.wup_b, R.hidb, R.gra, sib)
-    to_fellow_core(1, R.wup_b)
-    expert_grad(R.wup_b, R.hidb, R.gra, c)
+    expert_grad(1, 3)
+    expert_grad(0, 3)
+    for i, to in ((1, 2), (0, 1)):
+        pair_sum(i, 3)
+        part_on(i, 3, to, 1)
 
     def out_tile(t, carry):
         rows = pl.ds(times(t, 256), 256)
         got = mm_t(R.gact[...], R.wdn_b[rows, :]).astype(BF16)
         for o in range(nz):
-            R.out_s[o, :, rows] = got[o * C : (o + 1) * C, :]
+
+            @pl.when(inner | (o != near))
+            def _():
+                R.out_s[o, :, rows] = got[o * C : (o + 1) * C, :]
+
         return carry
 
     lax.fori_loop(0, D // 256, out_tile, 0)
     out_run(1, 0)
-    expert_grad(R.wdn_b, R.cotb, R.gact, sib)
-    to_fellow_core(0, R.wdn_b)
 
     @pl.when(inner)
     def _():
         relay_back(near, 1)
         relay_back(fellow, 0)
 
-    expert_grad_on(1, R.wup_b)
-    expert_grad(R.wdn_b, R.cotb, R.gact, c)
-    expert_grad_on(0, R.wdn_b)
+    for k in (1, 2, 0):
+        expert_grad(1, k)
+        expert_grad(0, k)
+    for k in (1, 2, 0):
+        pair_sum(1, k)
+        pair_sum(0, k)
     hand_far(R.ra, RA, R.ra_ss, R.ra_rs, ra_out)
-
-    out_run(1, 1)
-    out_run(2, 0)
 
     R.ghid_f[...] = R.cotb[pl.ds(times(z, C), C), :].astype(F32) + R.gh_s[z].astype(F32)
 
@@ -1006,10 +1011,12 @@
     for k in range(1, nz):
         o = line(k)
         arrived(R.glog_r.at[o], R.gl_rs.at[o])
+    out_run(1, 1)
     R.glog_r[z] = R.glog_s[z]
     R.ghid_b[...] = R.ghid_f[...].astype(BF16)
     put_turned(R.ghid_f[...], 3)
     turned_late = send_turned(3, 4, R.ltl_ss, R.ltl_rs)
+    out_run(2, 0)
 
     gates = R.gate_b[...]
     small = jnp.zeros((C, LANES), F32)
@@ -1045,7 +1052,7 @@
     R.small_b[...] = small.astype(BF16)
     R.rb[0:C, HD : HD + LANES] = (small + glog.T).astype(BF16)
     RV = slice(0, HD + LANES)
-    rv_out = send_rows(R.rb, RV, R.rv_ss, R.rv_rs)
+    rv_out = send_rows(R.rb, RV, R.rv_ss, R.rv_rs, (1, 2, 3))
 
     q0 = HD + LANES
     for h in range(H):
@@ -1061,10 +1068,11 @@
         R.rb[0:C, q0 + HD + h * DH : q0 + HD + (h + 1) * DH] = rot_back(
             tmm(gs, R.q_b[:, hs])
         ).astype(BF16)
-    RQ = slice(q0, q0 + 2 * HD)
+    RQ, RK = slice(q0, q0 + HD), slice(q0 + HD, q0 + 2 * HD)
     rq_out = send_rows(R.rb, RQ, R.rq_ss, R.rq_rs)
-
-    gproj = mm_t(R.rb[0:C, RQ], R.wqk_b[...])
+    rk_out = send_rows(R.rb, RK, R.rk_ss, R.rk_rs)
+
+    gproj = mm_t(R.rb[0:C, q0 : q0 + 2 * HD], R.wqk_b[...])
     standard = R.std_b[...]
     column_sum = jnp.sum(gproj * standard, axis=0, keepdims=True)
     for b in range(D // LANES):
@@ -1078,9 +1086,7 @@
         cp.start()
         gain_out.append(cp)
 
-    out_run(1, 2)
     out_run(2, 1)
-    out_run(3, 0)
     for cp in turned:
         cp.wait()
     rows_here(R.ra, RA, R.ra_rs)
@@ -1113,13 +1119,25 @@
         slice(2 * EV + 2 * HD, 2 * EV + 2 * HD + LANES),
     )
     gated_grad(3, R.ra, GATE, 0)
-    sum_out(*part_sum(0, PO), R.px.at[0], R.px_rs.at[0])
-
-    hand_near(R.rb, RV, R.rv_ss, R.rv_rs, rv_out, 2)
+    o_run = functools.partial(run, *grad_sum(0, PO))
+    v_run = functools.partial(run, *grad_sum(1, PV))
+    for n in range(nz - 1):
+        o_run(1, n)
+
+    out_run(3, 0)
+    hand_near(R.rb, RV, R.rv_ss, R.rv_rs, rv_out, 0)
+    hand_far(R.rb, RV, R.rv_ss, R.rv_rs, rv_out)
+    o_run(2, 0)
+    rows_here(R.rb, RV, R.rv_rs)
+    gated_grad(0, R.rb, 0, EV)
+    for n in range(nz - 1):
+        v_run(1, n)
+    o_run(2, 1)
+    hand_near(R.rb, RK, R.rk_ss, R.rk_rs, rk_out, 2)
     hand_near(R.rb, RQ, R.rq_ss, R.rq_rs, rq_out, 1)
-    hand_far(R.rb, RV, R.rv_ss, R.rv_rs, rv_out)
-    expert_grad_relay(0, R.wdn_b)
-    expert_grad_relay(1, R.wup_b)
+    expert_grad_relay(0)
+    expert_grad_relay(1)
+    o_run(3, 0)
     total = R.gp[0]
     for cp, (k, dc) in zip(gain_out, plane_all):
         cp.wait()
@@ -1129,25 +1147,25 @@
         o = line(k)
         remote(R.gz_s, R.gz.at[z], R.gz_ss.at[o], R.gz_rs.at[z], dev(p, o, c)).start()
 
-    rows_here(R.rb, RV, R.rv_rs)
-    gated_grad(0, R.rb, 0, EV)
-    sum_out(*part_sum(1, PV), R.px.at[1], R.px_rs.at[1])
-    sum_on(*part_sum(0, PO), R.px.at[0], R.px_rs.at[0])
-    hand_far(R.rb, RQ, R.rq_ss, R.rq_rs, rq_out)
     lane_s = iota((SL, LANES), 1)
     small_t = mm(turned_of(0), R.rb[:, HD : HD + LANES])
     small_h = mm(turned_of(2), R.rb[:, HD : HD + LANES])
     R.pb[:, PS] = jnp.where(lane_s < 2 * GATE, small_t, small_h).astype(BF16)
-    send_part(3, PS)
+    send_part(1, PS)
+    hand_far(R.rb, RQ, R.rq_ss, R.rq_rs, rq_out)
+    hand_far(R.rb, RK, R.rk_ss, R.rk_rs, rk_out)
     rows_here(R.rb, RQ, R.rq_rs)
+    rows_here(R.rb, RK, R.rk_rs)
     left = turned_of(1)
     for b in range(2):
         lo = q0 + b * HD
         R.pb[:, 2 * EV + b * HD : 2 * EV + (b + 1) * HD] = mm(left, R.rb[:, lo : lo + HD]).astype(
             BF16
         )
-    send_part(2, PQ)
-    sum_on(*part_sum(1, PV), R.px.at[1], R.px_rs.at[1])
+    v_run(2, 0)
+    send_part(0, PQ)
+    v_run(2, 1)
+    v_run(3, 0)
 
 
     inputs = R.tokens[...].astype(F32)
@@ -1173,17 +1191,7 @@
         )
 
     R.hid_f[...] += R.out_s[z].astype(F32)
-
-    @pl.when(z > 0)
-    def _():
-        arrived(R.out_r.at[z], R.out_rs.at[z])
-        R.hid_f[...] += R.out_r[z].astype(F32)
-
-    @pl.when(z < nz - 1)
-    def _():
-        arrived(R.out_r.at[nz], R.out_rs.at[nz])
-        R.hid_f[...] += R.out_r[nz].astype(F32)
-
+    run_end(R.hid_f, out_sum[1], R.out_rs)
     R.mixed[...] = R.hid_f[...].astype(BF16)
 
     for k in range(1, nz):
@@ -1203,14 +1211,15 @@
         got = R.pb[own_rows, lanes].astype(F32)
         for k in range(1, nz):
             o = line(k)
-            arrived(R.pr.at[o, :, lanes], R.p_rs.at[part, o])
-            got = got + R.pr[o, :, lanes].astype(F32)
+            there = part_sum(part, lanes)[1](o)
+            arrived(there, R.p_rs.at[part, o])
+            got = got + there[...].astype(F32)
         return got
 
     for i, (dst, lanes) in enumerate(((R.go, PO), (R.gv, PV))):
         dst[...] = R.pb[own_rows, lanes].astype(F32)
-        sum_in(dst, part_sum(i, lanes)[1], R.p_rs.at[i])
-    got = line_total(3, PS)
+        run_end(dst, grad_sum(i, lanes)[1], R.pn_rs.at[i])
+    got = line_total(1, PS)
 
     def pick(width, source):
         a, b = iota((width, LANES), 1), iota((width, LANES), 0)
@@ -1234,7 +1243,7 @@
     R.gvg[...] = picked(pick(GATE, lambda b: b), got)
     R.gog[...] = picked(pick(GATE, lambda b: b + GATE), got)
     R.gr[...] = picked(got, pick(experts, router_lane))
-    got = line_total(2, PQ)
+    got = line_total(0, PQ)
     R.gq[...] = got[:, 0:HD]
     R.gk[...] = got[:, HD : 2 * HD]
 
@@ -1250,7 +1259,7 @@
 
     gather_end(R.cotb, R.cot_ss)
     gather_end(R.hidb, R.hid_ss)
-    for cp in masks + ra_out + rv_out + rq_out + plane_out:
+    for cp in masks + ra_out + rv_out + rq_out + rk_out + plane_out:
         cp.wait_send()
     for k in range(1, nz):
         o = line(k)
@@ -1258,8 +1267,13 @@
         sent(R.glog_s.at[o], R.gl_ss.at[o])
         sent(R.out_s.at[o], R.out_ss.at[o])
         sent(R.gz_s, R.gz_ss.at[o])
-        for part, lanes in enumerate((PO, PV, PQ, PS)):
-            sent(R.pb.at[pl.ds(times(o, S), S), lanes], R.p_ss.at[part, o])
+        for lanes, ss in (
+            (PO, R.pn_ss.at[0]),
+            (PV, R.pn_ss.at[1]),
+            (PQ, R.p_ss.at[0]),
+            (PS, R.p_ss.at[1]),
+        ):
+            sent(R.pb.at[pl.ds(times(o, S), S), lanes], ss.at[o])
 
 
 def settle_kernel(*refs):
@@ -1317,7 +1331,8 @@
     s.vmem("gh_x", (2, C, D), BF16)
     for name in ("glog_s", "glog_r"):
         s.vmem(name, (nz, pad_e, C), BF16)
-    s.vmem("pair_r", (2, D, HF), BF16)
+    s.vmem("dg", (D // nd, EF), BF16)
+    s.vmem("pair_r", (2, nd, D // nd, HF), BF16)
     s.vmem("eg_r", (nd - 1, 2, D // nd, HF), BF16)
     s.vmem("ghid_f", (C, D), F32)
     s.vmem("ghid_b", (C, D), BF16)
@@ -1325,27 +1340,29 @@
     s.vmem("gval_f", (C, HD), F32)
     s.vmem("small_b", (C, LANES), BF16)
     s.vmem("pb", (SL, PW), BF16)
-    s.vmem("pr", (nz, S, PW), BF16)
-    s.vmem("px", (2, S, EV), BF16)
+    s.vmem("pr", (nz, S, PW - 2 * EV), BF16)
+    s.vmem("pn", (2, nz + 1, S, EV), BF16)
     s.vmem("gp", (2 * nd, D // LANES, LANES), F32)
     s.vmem("gz_s", (D // LANES, LANES), F32)
     s.vmem("gz", (nz, D // LANES, LANES), F32)
     s.sems("ld", 4 + 2 * local)
     s.sems("gx_rs", 2)
     s.sems("out_rs", nz + 1)
-    s.sems("px_rs", 2)
     for name in ("cot_ss", "hid_ss"):
         s.sems(name, 2, nz)
     for name in ("cot_rs", "hid_rs", "mask_ss", "mask_rs", "gh_ss", "gh_rs", "gl_ss", "gl_rs", "out_ss", "gz_ss", "gz_rs"):
         s.sems(name, nz)
-    for name in "w_ss w_rs pair_ss pair_rs".split():
+    for name in ("w_ss", "w_rs"):
         s.sems(name, 2)
-    for name in ("lt_ss", "lt_rs", "ltl_ss", "ltl_rs", "gp_ss", "gp_rs", "ra_ss", "ra_rs", "rv_ss", "rv_rs", "rq_ss", "rq_rs"):
+    for name in ("pair_ss", "pair_rs"):
+        s.sems(name, 2, nd)
+    for name in ("lt_ss", "lt_rs", "ltl_ss", "ltl_rs", "gp_ss", "gp_rs", "ra_ss", "ra_rs", "rv_ss", "rv_rs", "rq_ss", "rq_rs", "rk_ss", "rk_rs"):
         s.sems(name, 2 * nd)
     for name in ("eg_ss", "eg_rs"):
         s.sems(name, nd - 1, 2)
-    for name in ("p_ss", "p_rs"):
-        s.sems(name, 4, nz)
+    for name in ("p_ss", "p_rs", "pn_ss"):
+        s.sems(name, 2, nz)
+    s.sems("pn_rs", 2, nz + 1)
 
     def out(*shape, dtype=F32):
         return jax.ShapeDtypeStruct(shape, dtype)

time: 111 us -> 104 us (0.937)
  Pallas kernels: 110 us -> 103 us
    pallas_call x1, Pallas kernels: 107 us -> 99.6 us  [fused_layer(): pl.pallas_call(functools.partial(layer_kernel, INPUTS + OUTPUTS + tuple(s...]
where the time goes in v4:
time: 104 us
  Pallas kernels  103 us (99%)
    pallas_call x1, Pallas kernels, fused_layer(): pl.pallas_call(functools.partial(layer_kernel, INPUTS + OUTPUTS + tuple(s...  99.6 us
    pallas_call x1, Pallas kernels, fused_layer(): pl.pallas_call(settle_kernel, out_shape=[out(*x.shape, dtype=x.dtype) for...  3.62 us

profile of v4, /device:TPU:0, one launch (start us, length us, event | category | flops | bytes accessed | tf_op | source)
XLA Modules:
  0.0 103.9 jit_solution(5596857828564572557)
XLA Ops:
  0.7 99.6 %shard_map.238 = (bf16[128,1024]{1,0:T(8,128)(2,1)}, f32[128,1024]{1,0:T(8,128)}, f32[1,32]{1,0:T(1,128)}, f32[32,512]{1,0:T(8,128)}, f32[32,512]{1,0:T(8,128)},...) custom-call(bf16[128,1024]{1,0:T(8,128)(2,1)} %refs_0_.1, ...), custom_call_target="tpu_custom_call" | custom-call | tf_op jit(solution)/shard_map/pallas_call | solution.py:1373
  100.3 3.6 %shard_map.239 = (bf16[128,1024]{1,0:T(8,128)(2,1)}, f32[128,1024]{1,0:T(8,128)}, f32[1,32]{1,0:T(1,128)}, f32[32,512]{1,0:T(8,128)}, f32[32,512]{1,0:T(8,128)},...) custom-call(bf16[128,1024]{1,0:T(8,128)(2,1)} %get-tuple-element.36., ...), custom_call_target="tpu_custom_call" | custom-call | tf_op jit(solution)/shard_map/pallas_call | solution.py:1413

commit v5 on v4

--- a/solution.py
+++ b/solution.py
@@ -398,8 +398,13 @@
         self.add(name, pltpu.SemaphoreType.DMA(shape))
 
 
-INPUTS = ("tokens", "cot", "lens", "rt", "het", "gain", "wvg", "wog", "wr", "wq", "wk", "wv", "wo", "wu", "wd")
+SMALL = ("tokens", "cot", "lens", "rt", "het", "gain", "wvg", "wog", "wr")
+WEIGHTS = ("wq", "wk", "wv", "wo", "wu", "wd")
 OUTPUTS = ("mixed", "gtok", "ggain", "gq", "gk", "gv", "go", "gvg", "gog", "gr", "gup", "gdn")
+
+
+def in_hbm(names):
+    return tuple(name + "_h" for name in names)
 
 
 def layer_kernel(names, nd, nz, local, *refs):
@@ -448,26 +453,6 @@
     def line(k):
         return lax.rem(z + k, nz)
 
-    loads = {}
-
-    def load(name, src, dst, sem):
-        cp = pltpu.make_async_copy(src, dst, sem)
-        cp.start()
-        loads.setdefault(name, []).append(cp)
-
-    def loaded(name):
-        for cp in loads.pop(name):
-            cp.wait()
-
-    load("qk", R.wq, R.wqk_b.at[:, 0:HD], R.ld.at[0])
-    load("qk", R.wk, R.wqk_b.at[:, HD : 2 * HD], R.ld.at[1])
-    load("v", R.wv, R.wv_b, R.ld.at[2])
-    for i in range(local):
-        col = times(c * local + i, DH)
-        load("up", R.wu.at[i], R.wup_b.at[:, pl.ds(col, DH)], R.ld.at[4 + i])
-        load("dn", R.wd.at[i], R.wdn_b.at[:, pl.ds(col, DH)], R.ld.at[4 + local + i])
-    load("o", R.wo, R.wo_b, R.ld.at[3])
-
     barrier = pltpu.get_barrier_semaphore()
     partners = [dev(p, z, sib)]
     partners += [dev(p, line(k), c) for k in range(1, nz)]
@@ -476,6 +461,28 @@
     for to in partners:
         pl.semaphore_signal(barrier, inc=1, device_id=to, device_id_type=MESH)
 
+    loads = {}
+
+    def load(name, src, dst, sem):
+        cp = pltpu.make_async_copy(src, dst, sem)
+        cp.start()
+        loads.setdefault(name, []).append(cp)
+
+    def loaded(name):
+        for cp in loads.pop(name):
+            cp.wait()
+
+    for i, name in enumerate(("cot", "lens", "rt", "tokens", "gain", "het", "wvg", "wog", "wr")):
+        load(name, r[name + "_h"], r[name], R.ld_in.at[i])
+    stores = []
+
+    def store(*names):
+        for name in names:
+            cp = pltpu.make_async_copy(r[name], r[name + "_h"], R.st.at[OUTPUTS.index(name)])
+            cp.start()
+            stores.append(cp)
+
+    loaded("lens")
     l0 = R.lens[0, 0]
     b1 = l0 + R.lens[0, 1]
     row = iota((C, LANES), 0)
@@ -488,9 +495,19 @@
     start = jnp.where(seq_r == 0, 0, l0)
     position = jnp.where(live, row - start, 0).astype(F32)
 
+    loaded("cot")
     for b in range(D // LANES):
         cols = slice(b * LANES, (b + 1) * LANES)
         R.cotb[pl.ds(times(z, C), C), cols] = (R.cot[:, cols].astype(F32) * live_f).astype(BF16)
+    load("qk", R.wq, R.wqk_b.at[:, 0:HD], R.ld.at[0])
+    load("qk", R.wk, R.wqk_b.at[:, HD : 2 * HD], R.ld.at[1])
+    load("v", R.wv, R.wv_b, R.ld.at[2])
+    for i in range(local):
+        col = times(c * local + i, DH)
+        load("up", R.wu.at[i], R.wup_b.at[:, pl.ds(col, DH)], R.ld.at[4 + i])
+        load("dn", R.wd.at[i], R.wdn_b.at[:, pl.ds(col, DH)], R.ld.at[4 + local + i])
+    load("o", R.wo, R.wo_b, R.ld.at[3])
+    loaded("rt")
     ids = iota((pad_e, C), 0)
     for zz in range(nz):
         named = jnp.zeros((pad_e, C), F32)
@@ -558,6 +575,9 @@
         cp = remote(R.mask_s.at[o], R.maskb.at[z], R.mask_ss.at[k], R.mask_rs.at[z], dev(p, o, c))
         cp.start()
         masks.append(cp)
+
+    for name in ("tokens", "gain", "het", "wvg", "wog", "wr"):
+        loaded(name)
 
     s_row, s_col = iota((GATE, LANES), 0), iota((GATE, LANES), 1)
     to_v = jnp.where(s_row == s_col, 1.0, 0.0).astype(BF16)
@@ -771,7 +791,7 @@
         def _():
             gather_on(R.hidb, R.hid_ss, R.hid_rs, origin(k + inner.astype(jnp.int32)))
 
-        @pl.when(k == 1)
+        @pl.when(k == jnp.where(inner, 1, 2))
         def _():
             for far_step in range(2, nz - 1):
                 gather_step(R.cotb, R.cot_ss, R.cot_rs, far_step)
@@ -832,6 +852,10 @@
         def _():
             send_by(o, fellow, 1)
 
+        @pl.when(k == 2)
+        def _():
+            hand_near(R.ra, RA, R.ra_ss, R.ra_rs, [], 2)
+
         @pl.when((k == 2) & (least == 0))
         def _():
             there = pl.ds(times(near, C), C)
@@ -912,9 +936,22 @@
         cp.start()
         plane_out.append(cp)
 
+    def first_half(i, n):
+        first = 1 if i == 0 else 2
+        rows = slice(n * rows_d // 2, (n + 1) * rows_d // 2)
+        cp = remote(
+            grad_at(i, first, c).at[rows],
+            R.eg_r.at[0, i, rows],
+            R.eg_ss.at[3 * n, i],
+            R.eg_rs.at[3 * n, i],
+            dev(plane(first), z, c),
+        )
+        cp.start()
+        plane_out.append(cp)
+
     def expert_grad_relay(i):
-        first, second = (1, 2) if i == 0 else (2, 1)
-        part_on(i, first, first, 0)
+        second = 2 if i == 0 else 1
+        first_half(i, 1)
         arrived(R.eg_r.at[1, i], R.eg_rs.at[1, i])
         own = grad_at(i, second, c)
         own[...] = (own[...].astype(F32) + R.eg_r[1, i].astype(F32)).astype(BF16)
@@ -965,7 +1002,6 @@
             R.p_rs.at[i],
         )
 
-    hand_near(R.ra, RA, R.ra_ss, R.ra_rs, ra_out, 2)
     expert_grad(1, 3)
     expert_grad(0, 3)
     for i, to in ((1, 2), (0, 1)):
@@ -994,11 +1030,6 @@
     for k in (1, 2, 0):
         expert_grad(1, k)
         expert_grad(0, k)
-    for k in (1, 2, 0):
-        pair_sum(1, k)
-        pair_sum(0, k)
-    hand_far(R.ra, RA, R.ra_ss, R.ra_rs, ra_out)
-
     R.ghid_f[...] = R.cotb[pl.ds(times(z, C), C), :].astype(F32) + R.gh_s[z].astype(F32)
 
     def add_back(o):
@@ -1087,11 +1118,15 @@
         gain_out.append(cp)
 
     out_run(2, 1)
+    for k in (1, 2, 0):
+        pair_sum(1, k)
+        pair_sum(0, k)
+    first_half(0, 0)
+    first_half(1, 0)
+    hand_far(R.ra, RA, R.ra_ss, R.ra_rs, ra_out)
     for cp in turned:
         cp.wait()
     rows_here(R.ra, RA, R.ra_rs)
-    for cp in turned_late:
-        cp.wait()
 
     def turned_of(w):
         return jnp.concatenate(
@@ -1102,15 +1137,21 @@
         for o in (far, fellow, near):
             to_place(*part_sum(part, lanes), o)
 
-    def gated_grad(w, rows_of, g0, at):
+    def gate_rows(dst, rows_of, g0, s0, s1):
+        rows = slice(s0 * C, s1 * C)
+        for x in range(EA):
+            for h in range(H):
+                lo = x * HD + h * DH
+                gx = column(R.ra[rows, HD : HD + LANES], g0 + x * H + h).astype(F32)
+                dst[rows, lo : lo + DH] = (
+                    gx * rows_of[rows, h * DH : (h + 1) * DH].astype(F32)
+                ).astype(BF16)
+
+    def gated_grad(w, gated, at):
         left = turned_of(w)
         for x in range(EA):
-            right = []
-            for h in range(H):
-                gx = column(R.ra[:, HD : HD + LANES], g0 + x * H + h).astype(F32)
-                right.append((gx * rows_of[:, h * DH : (h + 1) * DH].astype(F32)).astype(BF16))
-            right = jnp.concatenate(right, axis=1)
-            R.pb[:, at + x * HD : at + (x + 1) * HD] = mm(left, right).astype(BF16)
+            cols = slice(x * HD, (x + 1) * HD)
+            R.pb[:, at + x * HD : at + (x + 1) * HD] = mm(left, gated[:, cols]).astype(BF16)
 
     PO, PV, PQ, PS = (
         slice(0, EV),
@@ -1118,21 +1159,53 @@
         slice(2 * EV, 2 * EV + 2 * HD),
         slice(2 * EV + 2 * HD, 2 * EV + 2 * HD + LANES),
     )
-    gated_grad(3, R.ra, GATE, 0)
+    gate_rows(R.wo_b, R.ra, GATE, 0, 2 * nd)
+    for cp in turned_late:
+        cp.wait()
+    gated_grad(3, R.wo_b, 0)
     o_run = functools.partial(run, *grad_sum(0, PO))
     v_run = functools.partial(run, *grad_sum(1, PV))
-    for n in range(nz - 1):
-        o_run(1, n)
-
+    o_run(1, 0)
+    o_run(1, 1)
     out_run(3, 0)
     hand_near(R.rb, RV, R.rv_ss, R.rv_rs, rv_out, 0)
+
+    inputs = R.tokens[...].astype(F32)
+    centred = inputs - jnp.mean(inputs, axis=-1, keepdims=True)
+    inverse = lax.rsqrt(jnp.mean(centred * centred, axis=-1, keepdims=True) + norm_eps)
+    gs = gproj * R.gain[...]
+    gtok = R.ghid_f[...] + inverse * (
+        gs
+        - jnp.mean(gs, axis=-1, keepdims=True)
+        - standard * jnp.mean(gs * standard, axis=-1, keepdims=True)
+    )
+    R.gtok[...] = gtok
+    for x in range(EA):
+        for h in range(H):
+            lo = x * HD + h * DH
+            R.mix_b[:, lo : lo + DH] = (
+                column(gates, x * H + h) * R.gval_f[:, h * DH : (h + 1) * DH]
+            ).astype(BF16)
+    for b in range(2):
+        cols = slice(b * half_d, (b + 1) * half_d)
+        R.gtok[:, cols] += mm_t(R.mix_b[...], R.wv_b[cols, :]) + mm_t(
+            R.small_b[...], R.wg_b[cols, :]
+        )
+
+    store("gtok")
+
+    o_run(2, 0)
+    for k in range(3):
+        arrived(rows_at(R.rb, RV, 2 * k + 1), R.rv_rs.at[2 * k + 1])
+    gate_rows(R.wv_b, R.rb, 0, 0, 6)
+    o_run(2, 1)
     hand_far(R.rb, RV, R.rv_ss, R.rv_rs, rv_out)
-    o_run(2, 0)
-    rows_here(R.rb, RV, R.rv_rs)
-    gated_grad(0, R.rb, 0, EV)
-    for n in range(nz - 1):
-        v_run(1, n)
-    o_run(2, 1)
+    arrived(rows_at(R.rb, RV, 7), R.rv_rs.at[7])
+    gate_rows(R.wv_b, R.rb, 0, 6, 8)
+    gated_grad(0, R.wv_b, EV)
+    v_run(1, 0)
+    v_run(1, 1)
+    o_run(1, 2)
     hand_near(R.rb, RK, R.rk_ss, R.rk_rs, rk_out, 2)
     hand_near(R.rb, RQ, R.rq_ss, R.rq_rs, rq_out, 1)
     expert_grad_relay(0)
@@ -1152,6 +1225,8 @@
     small_h = mm(turned_of(2), R.rb[:, HD : HD + LANES])
     R.pb[:, PS] = jnp.where(lane_s < 2 * GATE, small_t, small_h).astype(BF16)
     send_part(1, PS)
+    v_run(2, 0)
+    v_run(2, 1)
     hand_far(R.rb, RQ, R.rq_ss, R.rq_rs, rq_out)
     hand_far(R.rb, RK, R.rk_ss, R.rk_rs, rk_out)
     rows_here(R.rb, RQ, R.rq_rs)
@@ -1162,37 +1237,14 @@
         R.pb[:, 2 * EV + b * HD : 2 * EV + (b + 1) * HD] = mm(left, R.rb[:, lo : lo + HD]).astype(
             BF16
         )
-    v_run(2, 0)
     send_part(0, PQ)
-    v_run(2, 1)
+    v_run(1, 2)
     v_run(3, 0)
-
-
-    inputs = R.tokens[...].astype(F32)
-    centred = inputs - jnp.mean(inputs, axis=-1, keepdims=True)
-    inverse = lax.rsqrt(jnp.mean(centred * centred, axis=-1, keepdims=True) + norm_eps)
-    gs = gproj * R.gain[...]
-    gtok = R.ghid_f[...] + inverse * (
-        gs
-        - jnp.mean(gs, axis=-1, keepdims=True)
-        - standard * jnp.mean(gs * standard, axis=-1, keepdims=True)
-    )
-    R.gtok[...] = gtok
-    for x in range(EA):
-        for h in range(H):
-            lo = x * HD + h * DH
-            R.mix_b[:, lo : lo + DH] = (
-                column(gates, x * H + h) * R.gval_f[:, h * DH : (h + 1) * DH]
-            ).astype(BF16)
-    for b in range(2):
-        cols = slice(b * half_d, (b + 1) * half_d)
-        R.gtok[:, cols] += mm_t(R.mix_b[...], R.wv_b[cols, :]) + mm_t(
-            R.small_b[...], R.wg_b[cols, :]
-        )
 
     R.hid_f[...] += R.out_s[z].astype(F32)
     run_end(R.hid_f, out_sum[1], R.out_rs)
     R.mixed[...] = R.hid_f[...].astype(BF16)
+    store("mixed")
 
     for k in range(1, nz):
         o = line(k)
@@ -1204,6 +1256,7 @@
     shift = lax.rem(LANES - lax.rem(first, LANES), LANES)
     line_sum = pltpu.roll(jnp.broadcast_to(line_sum, (8, LANES)), shift, 1)
     R.ggain[...] = line_sum[0:1, 0:S]
+    store("ggain")
 
     own_rows = pl.ds(times(z, S), S)
 
@@ -1219,6 +1272,7 @@
     for i, (dst, lanes) in enumerate(((R.go, PO), (R.gv, PV))):
         dst[...] = R.pb[own_rows, lanes].astype(F32)
         run_end(dst, grad_sum(i, lanes)[1], R.pn_rs.at[i])
+    store("go", "gv")
     got = line_total(1, PS)
 
     def pick(width, source):
@@ -1243,24 +1297,34 @@
     R.gvg[...] = picked(pick(GATE, lambda b: b), got)
     R.gog[...] = picked(pick(GATE, lambda b: b + GATE), got)
     R.gr[...] = picked(got, pick(experts, router_lane))
+    store("gvg", "gog", "gr")
     got = line_total(0, PQ)
     R.gq[...] = got[:, 0:HD]
     R.gk[...] = got[:, HD : 2 * HD]
+    store("gq", "gk")
 
     for i, (buf, dst) in enumerate(((R.wdn_b, R.gdn), (R.wup_b, R.gup))):
-        for slot in (0, 2):
-            arrived(R.eg_r.at[slot, i], R.eg_rs.at[slot, i])
+        for n in range(2):
+            rows = slice(n * rows_d // 2, (n + 1) * rows_d // 2)
+            arrived(R.eg_r.at[0, i, rows], R.eg_rs.at[3 * n, i])
+        arrived(R.eg_r.at[2, i], R.eg_rs.at[2, i])
         rows = rows_of(p)
         for x in range(local):
             got = buf[rows, pl.ds(times(c * local + x, DH), DH)].astype(F32)
             for slot in (0, 2):
                 got = got + R.eg_r[slot, i, :, x * DH : (x + 1) * DH].astype(F32)
             dst[x] = got
-
+        store(("gdn", "gup")[i])
+
+    for cp in stores:
+        cp.wait()
     gather_end(R.cotb, R.cot_ss)
     gather_end(R.hidb, R.hid_ss)
     for cp in masks + ra_out + rv_out + rq_out + rk_out + plane_out:
         cp.wait_send()
+    sent(rows_at(R.ra, RA, 4), R.ra_ss.at[3])
+    for k in (1, 2):
+        sent(rows_at(R.ra, RA, 2 * k), R.ra_ss.at[nd + k])
     for k in range(1, nz):
         o = line(k)
         sent(R.gh_s.at[o], R.gh_ss.at[o])
@@ -1276,10 +1340,17 @@
             sent(R.pb.at[pl.ds(times(o, S), S), lanes], ss.at[o])
 
 
-def settle_kernel(*refs):
-    n = len(refs) // 2
-    for src, dst in zip(refs[:n], refs[n:]):
-        dst[...] = src[...]
+def settle_kernel(n, *refs):
+    src, dst, held, sems = refs[:n], refs[n : 2 * n], refs[2 * n : 3 * n], refs[-1]
+    ins = [pltpu.make_async_copy(src[i], held[i], sems.at[0, i]) for i in range(n)]
+    outs = [pltpu.make_async_copy(held[i], dst[i], sems.at[1, i]) for i in range(n)]
+    for cp in ins:
+        cp.start()
+    for there, back in zip(ins, outs):
+        there.wait()
+        back.start()
+    for cp in outs:
+        cp.wait()
 
 
 def fused_layer(nd, nz, *args):
@@ -1359,7 +1430,7 @@
     for name in ("lt_ss", "lt_rs", "ltl_ss", "ltl_rs", "gp_ss", "gp_rs", "ra_ss", "ra_rs", "rv_ss", "rv_rs", "rq_ss", "rq_rs", "rk_ss", "rk_rs"):
         s.sems(name, 2 * nd)
     for name in ("eg_ss", "eg_rs"):
-        s.sems(name, nd - 1, 2)
+        s.sems(name, 4, 2)
     for name in ("p_ss", "p_rs", "pn_ss"):
         s.sems(name, 2, nz)
     s.sems("pn_rs", 2, nz + 1)
@@ -1367,27 +1438,40 @@
     def out(*shape, dtype=F32):
         return jax.ShapeDtypeStruct(shape, dtype)
 
-    vmem = pl.BlockSpec(memory_space=pltpu.VMEM)
-    smem = pl.BlockSpec(memory_space=pltpu.SMEM)
     hbm = pl.BlockSpec(memory_space=pl.ANY)
+    names = in_hbm(SMALL) + WEIGHTS + in_hbm(OUTPUTS)
+    results = (
+        out(C, D, dtype=BF16),
+        out(C, D),
+        out(1, S),
+        out(S, HD),
+        out(S, HD),
+        out(S, EV),
+        out(S, EV),
+        out(EA * H, S),
+        out(EA * H, S),
+        out(S, experts),
+        out(local, D // nd, DH),
+        out(local, D // nd, DH),
+    )
+    for name, x in zip(OUTPUTS, results):
+        s.vmem(name, x.shape, x.dtype)
+    s.vmem("tokens", (C, D), BF16)
+    s.vmem("cot", (C, D), BF16)
+    s.add("lens", pltpu.SMEM((1, 2), jnp.int32))
+    s.vmem("rt", (TOPK, C), jnp.int32)
+    s.vmem("het", (2 * H, C), jnp.int32)
+    s.vmem("gain", (1, D), F32)
+    s.vmem("wvg", (EA * H, D), BF16)
+    s.vmem("wog", (EA * H, D), BF16)
+    s.vmem("wr", (experts, D), BF16)
+    s.sems("ld_in", len(SMALL))
+    s.sems("st", len(OUTPUTS))
     outs = pl.pallas_call(
-        functools.partial(layer_kernel, INPUTS + OUTPUTS + tuple(s.names), nd, nz, local),
-        out_shape=(
-            out(C, D, dtype=BF16),
-            out(C, D),
-            out(1, S),
-            out(S, HD),
-            out(S, HD),
-            out(S, EV),
-            out(S, EV),
-            out(EA * H, S),
-            out(EA * H, S),
-            out(S, experts),
-            out(local, D // nd, DH),
-            out(local, D // nd, DH),
-        ),
-        in_specs=[vmem, vmem, smem] + [vmem] * 6 + [hbm] * 6,
-        out_specs=[vmem] * 12,
+        functools.partial(layer_kernel, names + tuple(s.names), nd, nz, local),
+        out_shape=results,
+        in_specs=[hbm] * 15,
+        out_specs=[hbm] * len(OUTPUTS),
         scratch_shapes=s.shapes,
         compiler_params=pltpu.CompilerParams(
             collective_id=0, has_side_effects=True, vmem_limit_bytes=VMEM_LIMIT
@@ -1411,10 +1495,12 @@
     )
     outs = list(
         pl.pallas_call(
-            settle_kernel,
-            out_shape=[out(*x.shape, dtype=x.dtype) for x in outs],
-            in_specs=[vmem] * 12,
-            out_specs=[vmem] * 12,
+            functools.partial(settle_kernel, len(outs)),
+            out_shape=results,
+            in_specs=[hbm] * len(outs),
+            out_specs=[hbm] * len(outs),
+            scratch_shapes=[pltpu.VMEM(x.shape, x.dtype) for x in outs]
+            + [pltpu.SemaphoreType.DMA((2, len(outs)))],
             compiler_params=pltpu.CompilerParams(vmem_limit_bytes=VMEM_LIMIT),
         )(*outs)
     )

time: 104 us -> 100 us (0.962)
  Pallas kernels: 103 us -> 99.4 us
    pallas_call x2, Pallas kernels: 103 us -> 99.4 us  [the longest x1 96.4 us: fused_layer(): pl.pallas_call(functools.partial(layer_kernel, names + tuple(s.names), nd...]
where the time goes in v5:
time: 100 us
  Pallas kernels  99.4 us (99%)
    pallas_call x1, Pallas kernels, fused_layer(): pl.pallas_call(functools.partial(layer_kernel, names + tuple(s.names), nd...  96.4 us
    pallas_call x1, Pallas kernels, fused_layer(): pl.pallas_call(functools.partial(settle_kernel, len(outs)), out_shape=res...  3.01 us

profile of v5, /device:TPU:0, one launch (start us, length us, event | category | flops | bytes accessed | tf_op | source)
XLA Modules:
  0.0 100.2 jit_solution(8955802357297158022)
XLA Ops:
  0.7 96.4 %shard_map.238 = (bf16[128,1024]{1,0:T(8,128)(2,1)}, f32[128,1024]{1,0:T(8,128)}, f32[1,32]{1,0:T(1,128)}, f32[32,512]{1,0:T(8,128)}, f32[32,512]{1,0:T(8,128)},...) custom-call(bf16[128,1024]{1,0:T(8,128)(2,1)} %refs_0_.1, ...), custom_call_target="tpu_custom_call" | custom-call | tf_op jit(solution)/shard_map/pallas_call | solution.py:1470
  97.1 3.0 %shard_map.239 = (bf16[128,1024]{1,0:T(8,128)(2,1)}, f32[128,1024]{1,0:T(8,128)}, f32[1,32]{1,0:T(1,128)}, f32[32,512]{1,0:T(8,128)}, f32[32,512]{1,0:T(8,128)},...) custom-call(bf16[128,1024]{1,0:T(8,128)(2,1)} %get-tuple-element.36., ...), custom_call_target="tpu_custom_call" | custom-call | tf_op jit(solution)/shard_map/pallas_call | solution.py:1497

commit v6 on v5

--- a/solution.py
+++ b/solution.py
@@ -447,6 +447,9 @@
     across = lax.rem(p + 2, nd)
     diagonal = lax.rem(beside + 2, nd)
 
+    def core_cols(cc):
+        return pl.ds(times(cc, HF), HF)
+
     def plane(k):
         return (p, beside, across, diagonal)[k]
 
@@ -466,11 +469,14 @@
     def load(name, src, dst, sem):
         cp = pltpu.make_async_copy(src, dst, sem)
         cp.start()
-        loads.setdefault(name, []).append(cp)
-
-    def loaded(name):
-        for cp in loads.pop(name):
-            cp.wait()
+        loads[name] = cp
+
+    def loaded(*names):
+        for name in names:
+            loads.pop(name).wait()
+
+    def landed(dst, sem):
+        pltpu.make_async_copy(dst, dst, sem).wait()
 
     for i, name in enumerate(("cot", "lens", "rt", "tokens", "gain", "het", "wvg", "wog", "wr")):
         load(name, r[name + "_h"], r[name], R.ld_in.at[i])
@@ -478,7 +484,7 @@
 
     def store(*names):
         for name in names:
-            cp = pltpu.make_async_copy(r[name], r[name + "_h"], R.st.at[OUTPUTS.index(name)])
+            cp = pltpu.make_async_copy(r[name], r[name + "_h"], R.ld_in.at[OUTPUTS.index(name)])
             cp.start()
             stores.append(cp)
 
@@ -500,13 +506,13 @@
         cols = slice(b * LANES, (b + 1) * LANES)
         R.cotb[pl.ds(times(z, C), C), cols] = (R.cot[:, cols].astype(F32) * live_f).astype(BF16)
     load("qk", R.wq, R.wqk_b.at[:, 0:HD], R.ld.at[0])
-    load("qk", R.wk, R.wqk_b.at[:, HD : 2 * HD], R.ld.at[1])
-    load("v", R.wv, R.wv_b, R.ld.at[2])
+    load("qk", R.wk, R.wqk_b.at[:, HD : 2 * HD], R.ld.at[0])
+    load("v", R.wv, R.wv_b, R.ld.at[1])
     for i in range(local):
         col = times(c * local + i, DH)
-        load("up", R.wu.at[i], R.wup_b.at[:, pl.ds(col, DH)], R.ld.at[4 + i])
-        load("dn", R.wd.at[i], R.wdn_b.at[:, pl.ds(col, DH)], R.ld.at[4 + local + i])
-    load("o", R.wo, R.wo_b, R.ld.at[3])
+        load("up", R.wu.at[i], R.wup_b.at[:, pl.ds(col, DH)], R.ld.at[2])
+        load("dn", R.wd.at[i], R.wdn_b.at[:, pl.ds(col, DH)], R.ld.at[3])
+    load("o", R.wo, R.wo_b, R.ld.at[4])
     loaded("rt")
     ids = iota((pad_e, C), 0)
     for zz in range(nz):
@@ -525,20 +531,21 @@
     def pass_on(buf, ss, rs, o, right, left):
         @pl.when(right)
         def _():
-            remote(block(buf, o), block(buf, o), ss.at[0, o], rs.at[o], dev(p, z + 1, c)).start()
+            remote(block(buf, o), block(buf, o), ss.at[o], rs.at[o], dev(p, z + 1, c)).start()
 
         @pl.when(left)
         def _():
-            remote(block(buf, o), block(buf, o), ss.at[1, o], rs.at[o], dev(p, z - 1, c)).start()
+            way = jnp.where(o == z, nz, o)
+            remote(block(buf, o), block(buf, o), ss.at[way], rs.at[o], dev(p, z - 1, c)).start()
 
     def passed(buf, ss, o, right, left):
         @pl.when(right)
         def _():
-            sent(block(buf, o), ss.at[0, o])
+            sent(block(buf, o), ss.at[o])
 
         @pl.when(left)
         def _():
-            sent(block(buf, o), ss.at[1, o])
+            sent(block(buf, o), ss.at[jnp.where(o == z, nz, o)])
 
     def gather_own(buf, ss, rs):
         pass_on(buf, ss, rs, z, z < nz - 1, z > 0)
@@ -569,15 +576,11 @@
                 passed(buf, ss, z + k, False, z > 0)
 
     gather_own(R.cotb, R.cot_ss, R.cot_rs)
-    masks = []
     for k in range(1, nz):
         o = line(k)
-        cp = remote(R.mask_s.at[o], R.maskb.at[z], R.mask_ss.at[k], R.mask_rs.at[z], dev(p, o, c))
-        cp.start()
-        masks.append(cp)
-
-    for name in ("tokens", "gain", "het", "wvg", "wog", "wr"):
-        loaded(name)
+        remote(R.mask_s.at[o], R.maskb.at[z], R.tiny_s.at[0], R.tiny_r.at[0], dev(p, o, c)).start()
+
+    loaded("tokens", "gain", "het", "wvg", "wog", "wr")
 
     s_row, s_col = iota((GATE, LANES), 0), iota((GATE, LANES), 1)
     to_v = jnp.where(s_row == s_col, 1.0, 0.0).astype(BF16)
@@ -606,7 +609,7 @@
     R.std_b[...] = standard
     R.normed_b[...] = (standard * R.gain[...]).astype(BF16)
 
-    loaded("qk")
+    landed(R.wqk_b, R.ld.at[0])
     scale = DH ** (-0.5)
     qk = mm(R.normed_b[...], R.wqk_b[:, 0:HD])
     for h in range(H):
@@ -625,16 +628,14 @@
     hit = jnp.concatenate(hit + hit + [jnp.zeros((LANES - 2 * GATE, C), F32)], axis=0)
     R.gate_b[...] = sigmoid(mm(R.tokens[...], R.wg_b[...])) * hit.T
 
-    loaded("up")
-    loaded("dn")
-    wx = []
+    landed(R.wup_b.at[:, core_cols(c)], R.ld.at[2])
+    landed(R.wdn_b.at[:, core_cols(c)], R.ld.at[3])
     for i, buf in enumerate((R.wup_b, R.wdn_b)):
         part = buf.at[:, pl.ds(times(c, HF), HF)]
-        cp = remote(part, part, R.w_ss.at[i], R.w_rs.at[i], dev(p, z, sib))
+        cp = remote(part, part, R.w_s.at[0], R.w_s.at[1], dev(p, z, sib))
         cp.start()
-        wx.append(cp)
-
-    loaded("v")
+
+    landed(R.wv_b, R.ld.at[1])
     gates = R.gate_b[...]
     total = [None] * H
     for x in range(EA):
@@ -660,7 +661,7 @@
             R.mix_b[:, lo : lo + DH] = (
                 column(gates, GATE + x * H + h) * R.att_b[:, h * DH : (h + 1) * DH]
             ).astype(BF16)
-    loaded("o")
+    landed(R.wo_b, R.ld.at[4])
     half_d = D // 2
     for b in range(2):
         cols = slice(b * half_d, (b + 1) * half_d)
@@ -685,7 +686,6 @@
         return sib if dc else c
 
     def send_turned(w0, w1, ss, rs):
-        out = []
         lanes = slice(w0 * LANES, w1 * LANES)
         for k, dc in plane_all:
             to = plane(k)
@@ -694,77 +694,78 @@
             cp = remote(
                 R.lt.at[pl.ds(at, SL), lanes],
                 R.ltr.at[slot, :, lanes],
-                ss.at[slot],
-                rs.at[slot],
+                ss,
+                rs,
                 dev(to, z, side(dc)),
             )
             cp.start()
-            out.append(cp)
         R.ltr[0, :, lanes] = R.lt[pl.ds(times(p * 2 + c, SL), SL), lanes]
-        return out
+
+    def turned_here(w0, w1, ss, rs):
+        there = R.ltr.at[1 : 2 * nd, :, w0 * LANES : w1 * LANES]
+        sent(there, ss)
+        arrived(there, rs)
 
     def rows_at(buf, lanes, slot):
         return buf.at[slot * C : (slot + 1) * C, lanes]
 
-    def send_rows(buf, lanes, ss, rs, ways=(1, 2)):
-        out = []
+    def send_rows(buf, lanes, sem, ways=(1, 2)):
         for k in ways:
-            cp = remote(
+            remote(
                 rows_at(buf, lanes, 0),
                 rows_at(buf, lanes, 2 * k),
-                ss.at[k],
-                rs.at[2 * k],
+                sem.at[0],
+                sem.at[k],
                 dev(plane(k), z, c),
-            )
-            cp.start()
-            out.append(cp)
-        return out + [hand_over(buf, lanes, ss, rs, 0)]
-
-    def hand_over(buf, lanes, ss, rs, k):
-        cp = remote(
+            ).start()
+        hand_over(buf, lanes, sem, 0)
+
+    def hand_over(buf, lanes, sem, k):
+        remote(
             rows_at(buf, lanes, 2 * k),
             rows_at(buf, lanes, 2 * k + 1),
-            ss.at[nd + k],
-            rs.at[2 * k + 1],
+            sem.at[0],
+            sem.at[5 if k == 3 else 4],
             dev(p, z, sib),
-        )
-        cp.start()
-        return cp
-
-    def hand_near(buf, lanes, ss, rs, out, via):
+        ).start()
+
+    def hand_near(buf, lanes, sem, via):
         for k in (via, 3 - via) if via else (1, 2):
-            arrived(rows_at(buf, lanes, 2 * k), rs.at[2 * k])
+            arrived(rows_at(buf, lanes, 2 * k), sem.at[k])
             if k == via:
-                cp = remote(
+                remote(
                     rows_at(buf, lanes, 2 * k),
                     rows_at(buf, lanes, 6),
-                    ss.at[3],
-                    rs.at[6],
+                    sem.at[0],
+                    sem.at[3],
                     dev(plane(3 - via), z, c),
-                )
-                cp.start()
-                out.append(cp)
-            out.append(hand_over(buf, lanes, ss, rs, k))
-
-    def hand_far(buf, lanes, ss, rs, out):
-        arrived(rows_at(buf, lanes, 6), rs.at[6])
-        out.append(hand_over(buf, lanes, ss, rs, 3))
-
-    def rows_here(buf, lanes, rs):
-        for k in range(nd):
-            arrived(rows_at(buf, lanes, 2 * k + 1), rs.at[2 * k + 1])
+                ).start()
+            hand_over(buf, lanes, sem, k)
+
+    def hand_far(buf, lanes, sem):
+        arrived(rows_at(buf, lanes, 6), sem.at[3])
+        hand_over(buf, lanes, sem, 3)
+
+    def near_here(buf, lanes, sem):
+        arrived(buf.at[0 : 3 * C, lanes], sem.at[4])
+
+    def far_here(buf, lanes, sem):
+        arrived(rows_at(buf, lanes, 7), sem.at[5])
+
+    def rows_sent(buf, lanes, sem):
+        sent(buf.at[0 : 7 * C, lanes], sem.at[0])
 
     put_turned(R.tokens[...], 0)
     put_turned(R.normed_b[...], 1)
     put_turned(R.hid_f[...], 2)
-    turned = send_turned(0, 3, R.lt_ss, R.lt_rs)
+    send_turned(0, 3, R.lt_s.at[0], R.lt_s.at[1])
     R.ra[0:C, 0:HD] = R.att_b[...].astype(BF16)
     R.ra[0:C, HD : HD + LANES] = gates.astype(BF16)
     RA = slice(0, HD + LANES)
-    ra_out = send_rows(R.ra, RA, R.ra_ss, R.ra_rs)
-
-    for cp in wx:
-        cp.wait()
+    send_rows(R.ra, RA, R.ra_s)
+
+    sent(R.wup_b, R.w_s.at[0])
+    arrived(R.wup_b, R.w_s.at[1])
 
     least = jnp.minimum(z, nz - 1 - z)
     inner = least > 0
@@ -802,7 +803,9 @@
             def _():
                 arrived(block(R.cotb, o), R.cot_rs.at[o])
 
-            arrived(R.maskb.at[o], R.mask_rs.at[o])
+        @pl.when(k == 1)
+        def _():
+            arrived(R.maskb.at[0 : nz - 1], R.tiny_r.at[0])
 
         hb = R.hidb[rows, :]
         cb = R.cotb[rows, :]
@@ -837,7 +840,7 @@
         @pl.when(k > 0)
         def _():
             remote(
-                R.glog_s.at[o], R.glog_r.at[z], R.gl_ss.at[o], R.gl_rs.at[z], dev(p, o, c)
+                R.glog_s.at[o], R.glog_r.at[z], R.tiny_s.at[1], R.tiny_r.at[1], dev(p, o, c)
             ).start()
 
         @pl.when((k > 0) & (least == 0) & (o != fellow))
@@ -854,7 +857,7 @@
 
         @pl.when(k == 2)
         def _():
-            hand_near(R.ra, RA, R.ra_ss, R.ra_rs, [], 2)
+            hand_near(R.ra, RA, R.ra_s, 2)
 
         @pl.when((k == 2) & (least == 0))
         def _():
@@ -866,106 +869,95 @@
             remote(
                 R.out_s.at[near],
                 R.out_r.at[slot],
-                R.out_ss.at[near],
-                R.out_rs.at[slot],
+                R.out_sem.at[nz + 1],
+                R.out_sem.at[slot],
                 dev(p, near, c),
             ).start()
 
         return carry
 
     def send_back(o):
-        remote(R.gh_s.at[o], R.gh_r.at[z], R.gh_ss.at[o], R.gh_rs.at[z], dev(p, o, c)).start()
+        remote(R.gh_s.at[o], R.gh_r.at[z], R.gh_sem.at[0], R.gh_sem.at[1], dev(p, o, c)).start()
 
     def send_by(o, by, slot):
         remote(
-            R.gh_s.at[o], R.gh_x.at[slot], R.gh_ss.at[o], R.gx_rs.at[slot], dev(p, by, c)
+            R.gh_s.at[o], R.gh_x.at[slot], R.gh_sem.at[0], R.gh_sem.at[2 + slot], dev(p, by, c)
         ).start()
 
     def relay_back(o, slot):
-        arrived(R.gh_x.at[slot], R.gx_rs.at[slot])
+        arrived(R.gh_x.at[slot], R.gh_sem.at[2 + slot])
         R.gh_s[o] = (R.gh_s[o].astype(F32) + R.gh_x[slot].astype(F32)).astype(BF16)
         send_back(o)
 
     lax.fori_loop(0, nz, expert_block, 0)
 
-    pairs = {}
-
     def rows_of(at):
         return pl.ds(times(at, rows_d), rows_d)
 
 
     rows_d = D // nd
-    plane_out = []
-
-    def half(cc):
-        return pl.ds(times(cc, HF), HF)
 
     def grad_at(i, k, cc):
         if i == 0 and k == 3:
-            return R.dg.at[:, half(cc)]
-        return (R.wdn_b, R.wup_b)[i].at[rows_of(plane(k)), half(cc)]
+            return R.dg.at[:, core_cols(cc)]
+        return (R.wdn_b, R.wup_b)[i].at[rows_of(plane(k)), core_cols(cc)]
 
     def expert_grad(i, k):
         left, right = ((R.cotb, R.gact), (R.hidb, R.gra))[i]
         for cc in (sib, c):
-            grad_at(i, k, cc)[...] = tmm(left[:, rows_of(plane(k))], right[:, half(cc)]).astype(BF16)
+            grad_at(i, k, cc)[...] = tmm(left[:, rows_of(plane(k))], right[:, core_cols(cc)]).astype(BF16)
             if cc is sib:
-                cp = remote(
+                remote(
                     grad_at(i, k, sib),
                     R.pair_r.at[i, k],
-                    R.pair_ss.at[i, k],
-                    R.pair_rs.at[i, k],
+                    R.pair_s.at[0],
+                    R.pair_s.at[1 + i if k == 3 else 3],
                     dev(p, z, sib),
-                )
-                cp.start()
-                pairs[i, k] = cp
+                ).start()
 
     def pair_sum(i, k):
-        pairs[i, k].wait()
+        if k == 3:
+            arrived(R.pair_r.at[i, k], R.pair_s.at[1 + i])
         own = grad_at(i, k, c)
         own[...] = (own[...].astype(F32) + R.pair_r[i, k].astype(F32)).astype(BF16)
 
     def part_on(i, k, to, slot):
-        cp = remote(
+        remote(
             grad_at(i, k, c),
             R.eg_r.at[slot, i],
-            R.eg_ss.at[slot, i],
-            R.eg_rs.at[slot, i],
+            R.eg_s.at[0],
+            R.eg_s.at[1 + i if slot == 1 else 3 + i],
             dev(plane(to), z, c),
-        )
-        cp.start()
-        plane_out.append(cp)
+        ).start()
 
     def first_half(i, n):
         first = 1 if i == 0 else 2
         rows = slice(n * rows_d // 2, (n + 1) * rows_d // 2)
-        cp = remote(
+        remote(
             grad_at(i, first, c).at[rows],
             R.eg_r.at[0, i, rows],
-            R.eg_ss.at[3 * n, i],
-            R.eg_rs.at[3 * n, i],
+            R.eg_s.at[0],
+            R.eg_s.at[3 + i],
             dev(plane(first), z, c),
-        )
-        cp.start()
-        plane_out.append(cp)
+        ).start()
 
     def expert_grad_relay(i):
         second = 2 if i == 0 else 1
         first_half(i, 1)
-        arrived(R.eg_r.at[1, i], R.eg_rs.at[1, i])
+        arrived(R.eg_r.at[1, i], R.eg_s.at[1 + i])
         own = grad_at(i, second, c)
         own[...] = (own[...].astype(F32) + R.eg_r[1, i].astype(F32)).astype(BF16)
         part_on(i, second, second, 2)
 
     def to_place(own, got, ss, rs, o):
-        remote(own(o), got(z), ss.at[o], rs.at[z], dev(p, o, c)).start()
+        remote(own(o), got(z), ss, rs, dev(p, o, c)).start()
 
     def run(own, got, ss, rs, k, n):
         def hand(d, slot, to):
             if k > 1:
                 arrived(got(d), rs.at[d])
                 own(d)[...] = (own(d)[...].astype(F32) + got(d)[...].astype(F32)).astype(BF16)
-            remote(own(d), got(slot), ss.at[d], rs.at[slot], dev(p, to, c)).start()
+            remote(own(d), got(slot), ss, rs.at[slot], dev(p, to, c)).start()
 
         @pl.when(z == k - 1)
         def _():
@@ -983,23 +975,23 @@
                 arrived(got(slot), rs.at[slot])
                 total[...] += got(slot)[...].astype(F32)
 
-    out_sum = (lambda d: R.out_s.at[d], lambda d: R.out_r.at[d], R.out_ss, R.out_rs)
+    out_sum = (lambda d: R.out_s.at[d], lambda d: R.out_r.at[d], R.out_sem.at[nz + 1], R.out_sem)
     out_run = functools.partial(run, *out_sum)
 
     def grad_sum(i, lanes):
         return (
             lambda d: R.pb.at[d * S : (d + 1) * S, lanes],
             lambda d: R.pn.at[i, d],
-            R.pn_ss.at[i],
-            R.pn_rs.at[i],
+            R.pn_sem.at[i, nz + 1],
+            R.pn_sem.at[i],
         )
 
     def part_sum(i, lanes):
         return (
             lambda o: R.pb.at[pl.ds(times(o, S), S), lanes],
             lambda o: R.pr.at[o, :, slice(lanes.start - 2 * EV, lanes.stop - 2 * EV)],
-            R.p_ss.at[i],
-            R.p_rs.at[i],
+            R.p_sem.at[0],
+            R.p_sem.at[1 + i],
         )
 
     expert_grad(1, 3)
@@ -1032,21 +1024,20 @@
         expert_grad(0, k)
     R.ghid_f[...] = R.cotb[pl.ds(times(z, C), C), :].astype(F32) + R.gh_s[z].astype(F32)
 
+    arrived(R.gh_r.at[0:2], R.gh_sem.at[1])
+
     def add_back(o):
-        arrived(R.gh_r.at[o], R.gh_rs.at[o])
         R.ghid_f[...] += R.gh_r[o].astype(F32)
 
     add_back(near)
     add_back(jnp.where(inner, fellow, far))
 
-    for k in range(1, nz):
-        o = line(k)
-        arrived(R.glog_r.at[o], R.gl_rs.at[o])
+    arrived(R.glog_r.at[0 : nz - 1], R.tiny_r.at[1])
     out_run(1, 1)
     R.glog_r[z] = R.glog_s[z]
     R.ghid_b[...] = R.ghid_f[...].astype(BF16)
     put_turned(R.ghid_f[...], 3)
-    turned_late = send_turned(3, 4, R.ltl_ss, R.ltl_rs)
+    send_turned(3, 4, R.lt_s.at[2], R.lt_s.at[3])
     out_run(2, 0)
 
     gates = R.gate_b[...]
@@ -1083,7 +1074,7 @@
     R.small_b[...] = small.astype(BF16)
     R.rb[0:C, HD : HD + LANES] = (small + glog.T).astype(BF16)
     RV = slice(0, HD + LANES)
-    rv_out = send_rows(R.rb, RV, R.rv_ss, R.rv_rs, (1, 2, 3))
+    send_rows(R.rb, RV, R.rv_s, (1, 2, 3))
 
     q0 = HD + LANES
     for h in range(H):
@@ -1100,33 +1091,32 @@
             tmm(gs, R.q_b[:, hs])
         ).astype(BF16)
     RQ, RK = slice(q0, q0 + HD), slice(q0 + HD, q0 + 2 * HD)
-    rq_out = send_rows(R.rb, RQ, R.rq_ss, R.rq_rs)
-    rk_out = send_rows(R.rb, RK, R.rk_ss, R.rk_rs)
+    send_rows(R.rb, RQ, R.rq_s)
+    send_rows(R.rb, RK, R.rk_s)
 
     gproj = mm_t(R.rb[0:C, q0 : q0 + 2 * HD], R.wqk_b[...])
     standard = R.std_b[...]
     column_sum = jnp.sum(gproj * standard, axis=0, keepdims=True)
     for b in range(D // LANES):
         R.gp[0, b : b + 1, :] = column_sum[:, b * LANES : (b + 1) * LANES]
-    gain_out = []
     for k, dc in plane_all:
         slot = 2 * k + dc
         cp = remote(
-            R.gp.at[0], R.gp.at[slot], R.gp_ss.at[slot], R.gp_rs.at[slot], dev(plane(k), z, side(dc))
+            R.gp.at[0], R.gp.at[slot], R.tiny_s.at[2], R.tiny_r.at[2], dev(plane(k), z, side(dc))
         )
         cp.start()
-        gain_out.append(cp)
 
     out_run(2, 1)
+    arrived(R.pair_r.at[:, 0:3], R.pair_s.at[3])
     for k in (1, 2, 0):
         pair_sum(1, k)
         pair_sum(0, k)
     first_half(0, 0)
     first_half(1, 0)
-    hand_far(R.ra, RA, R.ra_ss, R.ra_rs, ra_out)
-    for cp in turned:
-        cp.wait()
-    rows_here(R.ra, RA, R.ra_rs)
+    hand_far(R.ra, RA, R.ra_s)
+    turned_here(0, 3, R.lt_s.at[0], R.lt_s.at[1])
+    near_here(R.ra, RA, R.ra_s)
+    far_here(R.ra, RA, R.ra_s)
 
     def turned_of(w):
         return jnp.concatenate(
@@ -1160,15 +1150,14 @@
         slice(2 * EV + 2 * HD, 2 * EV + 2 * HD + LANES),
     )
     gate_rows(R.wo_b, R.ra, GATE, 0, 2 * nd)
-    for cp in turned_late:
-        cp.wait()
+    turned_here(3, 4, R.lt_s.at[2], R.lt_s.at[3])
     gated_grad(3, R.wo_b, 0)
     o_run = functools.partial(run, *grad_sum(0, PO))
     v_run = functools.partial(run, *grad_sum(1, PV))
     o_run(1, 0)
     o_run(1, 1)
     out_run(3, 0)
-    hand_near(R.rb, RV, R.rv_ss, R.rv_rs, rv_out, 0)
+    hand_near(R.rb, RV, R.rv_s, 0)
 
     inputs = R.tokens[...].astype(F32)
     centred = inputs - jnp.mean(inputs, axis=-1, keepdims=True)
@@ -1195,30 +1184,30 @@
     store("gtok")
 
     o_run(2, 0)
-    for k in range(3):
-        arrived(rows_at(R.rb, RV, 2 * k + 1), R.rv_rs.at[2 * k + 1])
+    near_here(R.rb, RV, R.rv_s)
     gate_rows(R.wv_b, R.rb, 0, 0, 6)
     o_run(2, 1)
-    hand_far(R.rb, RV, R.rv_ss, R.rv_rs, rv_out)
-    arrived(rows_at(R.rb, RV, 7), R.rv_rs.at[7])
+    hand_far(R.rb, RV, R.rv_s)
+    far_here(R.rb, RV, R.rv_s)
     gate_rows(R.wv_b, R.rb, 0, 6, 8)
     gated_grad(0, R.wv_b, EV)
     v_run(1, 0)
     v_run(1, 1)
     o_run(1, 2)
-    hand_near(R.rb, RK, R.rk_ss, R.rk_rs, rk_out, 2)
-    hand_near(R.rb, RQ, R.rq_ss, R.rq_rs, rq_out, 1)
+    hand_near(R.rb, RK, R.rk_s, 2)
+    hand_near(R.rb, RQ, R.rq_s, 1)
     expert_grad_relay(0)
     expert_grad_relay(1)
     o_run(3, 0)
     total = R.gp[0]
-    for cp, (k, dc) in zip(gain_out, plane_all):
-        cp.wait()
+    sent(R.gp.at[1:], R.tiny_s.at[2])
+    arrived(R.gp.at[1:], R.tiny_r.at[2])
+    for k, dc in plane_all:
         total = total + R.gp[2 * k + dc]
     R.gz_s[...] = total
     for k in range(1, nz):
         o = line(k)
-        remote(R.gz_s, R.gz.at[z], R.gz_ss.at[o], R.gz_rs.at[z], dev(p, o, c)).start()
+        remote(R.gz_s, R.gz.at[z], R.tiny_s.at[3], R.tiny_r.at[3], dev(p, o, c)).start()
 
     lane_s = iota((SL, LANES), 1)
     small_t = mm(turned_of(0), R.rb[:, HD : HD + LANES])
@@ -1227,10 +1216,11 @@
     send_part(1, PS)
     v_run(2, 0)
     v_run(2, 1)
-    hand_far(R.rb, RQ, R.rq_ss, R.rq_rs, rq_out)
-    hand_far(R.rb, RK, R.rk_ss, R.rk_rs, rk_out)
-    rows_here(R.rb, RQ, R.rq_rs)
-    rows_here(R.rb, RK, R.rk_rs)
+    hand_far(R.rb, RQ, R.rq_s)
+    hand_far(R.rb, RK, R.rk_s)
+    for lanes, sem in ((RQ, R.rq_s), (RK, R.rk_s)):
+        near_here(R.rb, lanes, sem)
+        far_here(R.rb, lanes, sem)
     left = turned_of(1)
     for b in range(2):
         lo = q0 + b * HD
@@ -1242,14 +1232,13 @@
     v_run(3, 0)
 
     R.hid_f[...] += R.out_s[z].astype(F32)
-    run_end(R.hid_f, out_sum[1], R.out_rs)
+    run_end(R.hid_f, out_sum[1], R.out_sem)
     R.mixed[...] = R.hid_f[...].astype(BF16)
     store("mixed")
 
+    arrived(R.gz.at[0 : nz - 1], R.tiny_r.at[3])
     for k in range(1, nz):
-        o = line(k)
-        arrived(R.gz.at[o], R.gz_rs.at[o])
-        total = total + R.gz[o]
+        total = total + R.gz[line(k)]
     first = (p * 2 * nz + z * 2 + c) * S
     pick_row = iota((D // LANES, LANES), 0) == first // LANES
     line_sum = jnp.sum(jnp.where(pick_row, total, 0.0), axis=0, keepdims=True)
@@ -1262,16 +1251,15 @@
 
     def line_total(part, lanes):
         got = R.pb[own_rows, lanes].astype(F32)
+        slots = part_sum(part, lanes)[1]
+        arrived(slots(slice(0, nz - 1)), R.p_sem.at[1 + part])
         for k in range(1, nz):
-            o = line(k)
-            there = part_sum(part, lanes)[1](o)
-            arrived(there, R.p_rs.at[part, o])
-            got = got + there[...].astype(F32)
+            got = got + slots(line(k))[...].astype(F32)
         return got
 
     for i, (dst, lanes) in enumerate(((R.go, PO), (R.gv, PV))):
         dst[...] = R.pb[own_rows, lanes].astype(F32)
-        run_end(dst, grad_sum(i, lanes)[1], R.pn_rs.at[i])
+        run_end(dst, grad_sum(i, lanes)[1], R.pn_sem.at[i])
     store("go", "gv")
     got = line_total(1, PS)
 
@@ -1304,10 +1292,7 @@
     store("gq", "gk")
 
     for i, (buf, dst) in enumerate(((R.wdn_b, R.gdn), (R.wup_b, R.gup))):
-        for n in range(2):
-            rows = slice(n * rows_d // 2, (n + 1) * rows_d // 2)
-            arrived(R.eg_r.at[0, i, rows], R.eg_rs.at[3 * n, i])
-        arrived(R.eg_r.at[2, i], R.eg_rs.at[2, i])
+        arrived(R.eg_r.at[0:2, i], R.eg_s.at[3 + i])
         rows = rows_of(p)
         for x in range(local):
             got = buf[rows, pl.ds(times(c * local + x, DH), DH)].astype(F32)
@@ -1320,30 +1305,29 @@
         cp.wait()
     gather_end(R.cotb, R.cot_ss)
     gather_end(R.hidb, R.hid_ss)
-    for cp in masks + ra_out + rv_out + rq_out + rk_out + plane_out:
-        cp.wait_send()
-    sent(rows_at(R.ra, RA, 4), R.ra_ss.at[3])
-    for k in (1, 2):
-        sent(rows_at(R.ra, RA, 2 * k), R.ra_ss.at[nd + k])
-    for k in range(1, nz):
-        o = line(k)
-        sent(R.gh_s.at[o], R.gh_ss.at[o])
-        sent(R.glog_s.at[o], R.gl_ss.at[o])
-        sent(R.out_s.at[o], R.out_ss.at[o])
-        sent(R.gz_s, R.gz_ss.at[o])
-        for lanes, ss in (
-            (PO, R.pn_ss.at[0]),
-            (PV, R.pn_ss.at[1]),
-            (PQ, R.p_ss.at[0]),
-            (PS, R.p_ss.at[1]),
-        ):
-            sent(R.pb.at[pl.ds(times(o, S), S), lanes], ss.at[o])
+    for buf, lanes, sem in (
+        (R.ra, RA, R.ra_s),
+        (R.rb, RV, R.rv_s),
+        (R.rb, RQ, R.rq_s),
+        (R.rb, RK, R.rk_s),
+    ):
+        rows_sent(buf, lanes, sem)
+    sent(R.maskb.at[0 : nz - 1], R.tiny_s.at[0])
+    sent(R.glog_r.at[0 : nz - 1], R.tiny_s.at[1])
+    sent(R.gz.at[0 : nz - 1], R.tiny_s.at[3])
+    sent(R.gh_r.at[0 : nz - 1], R.gh_sem.at[0])
+    sent(R.out_r.at[0 : nz - 1], R.out_sem.at[nz + 1])
+    sent(R.pair_r, R.pair_s.at[0])
+    sent(R.eg_r, R.eg_s.at[0])
+    sent(R.pr.at[0 : nz - 1], R.p_sem.at[0])
+    for i in range(2):
+        sent(R.pn.at[i, 0 : nz - 1], R.pn_sem.at[i, nz + 1])
 
 
 def settle_kernel(n, *refs):
     src, dst, held, sems = refs[:n], refs[n : 2 * n], refs[2 * n : 3 * n], refs[-1]
-    ins = [pltpu.make_async_copy(src[i], held[i], sems.at[0, i]) for i in range(n)]
-    outs = [pltpu.make_async_copy(held[i], dst[i], sems.at[1, i]) for i in range(n)]
+    ins = [pltpu.make_async_copy(src[i], held[i], sems.at[i]) for i in range(n)]
+    outs = [pltpu.make_async_copy(held[i], dst[i], sems.at[i]) for i in range(n)]
     for cp in ins:
         cp.start()
     for there, back in zip(ins, outs):
@@ -1416,24 +1400,18 @@
     s.vmem("gp", (2 * nd, D // LANES, LANES), F32)
     s.vmem("gz_s", (D // LANES, LANES), F32)
     s.vmem("gz", (nz, D // LANES, LANES), F32)
-    s.sems("ld", 4 + 2 * local)
-    s.sems("gx_rs", 2)
-    s.sems("out_rs", nz + 1)
+    s.sems("ld", 5)
     for name in ("cot_ss", "hid_ss"):
-        s.sems(name, 2, nz)
-    for name in ("cot_rs", "hid_rs", "mask_ss", "mask_rs", "gh_ss", "gh_rs", "gl_ss", "gl_rs", "out_ss", "gz_ss", "gz_rs"):
-        s.sems(name, nz)
-    for name in ("w_ss", "w_rs"):
-        s.sems(name, 2)
-    for name in ("pair_ss", "pair_rs"):
-        s.sems(name, 2, nd)
-    for name in ("lt_ss", "lt_rs", "ltl_ss", "ltl_rs", "gp_ss", "gp_rs", "ra_ss", "ra_rs", "rv_ss", "rv_rs", "rq_ss", "rq_rs", "rk_ss", "rk_rs"):
-        s.sems(name, 2 * nd)
-    for name in ("eg_ss", "eg_rs"):
-        s.sems(name, 4, 2)
-    for name in ("p_ss", "p_rs", "pn_ss"):
-        s.sems(name, 2, nz)
-    s.sems("pn_rs", 2, nz + 1)
+        s.sems(name, nz + 1)
+    for name in ("cot_rs", "hid_rs", "tiny_s", "tiny_r", "lt_s", "gh_sem", "pair_s"):
+        s.sems(name, 4)
+    for name in ("ra_s", "rv_s", "rq_s", "rk_s"):
+        s.sems(name, 6)
+    s.sems("w_s", 2)
+    s.sems("eg_s", 5)
+    s.sems("p_sem", 3)
+    s.sems("out_sem", nz + 2)
+    s.sems("pn_sem", 2, nz + 2)
 
     def out(*shape, dtype=F32):
         return jax.ShapeDtypeStruct(shape, dtype)
@@ -1465,8 +1443,7 @@
     s.vmem("wvg", (EA * H, D), BF16)
     s.vmem("wog", (EA * H, D), BF16)
     s.vmem("wr", (experts, D), BF16)
-    s.sems("ld_in", len(SMALL))
-    s.sems("st", len(OUTPUTS))
+    s.sems("ld_in", len(OUTPUTS))
     outs = pl.pallas_call(
         functools.partial(layer_kernel, names + tuple(s.names), nd, nz, local),
         out_shape=results,
@@ -1500,7 +1477,7 @@
             in_specs=[hbm] * len(outs),
             out_specs=[hbm] * len(outs),
             scratch_shapes=[pltpu.VMEM(x.shape, x.dtype) for x in outs]
-            + [pltpu.SemaphoreType.DMA((2, len(outs)))],
+            + [pltpu.SemaphoreType.DMA((len(outs),))],
             compiler_params=pltpu.CompilerParams(vmem_limit_bytes=VMEM_LIMIT),
         )(*outs)
     )

time: 100 us -> 98.8 us (0.988); the launches traced: 100 us -> 97.9 us
  Pallas kernels: 99.4 us -> 97 us
    pallas_call x1, Pallas kernels: 96.4 us -> 94.1 us  [fused_layer(): pl.pallas_call(functools.partial(layer_kernel, names + tuple(s.names), nd...]
where the time goes in v6:
time: 98.8 us; the launch traced here: 97.9 us
  Pallas kernels  97 us (98%)
    pallas_call x1, Pallas kernels, fused_layer(): pl.pallas_call(functools.partial(layer_kernel, names + tuple(s.names), nd...  94.1 us
    pallas_call x1, Pallas kernels, fused_layer(): pl.pallas_call(functools.partial(settle_kernel, len(outs)), out_shape=res...  2.9 us

profile of v6, /device:TPU:0, one launch (start us, length us, event | category | flops | bytes accessed | tf_op | source)
XLA Modules:
  0.0 97.9 jit_solution(9504076837165266231)
XLA Ops:
  0.7 94.1 %shard_map.238 = (bf16[128,1024]{1,0:T(8,128)(2,1)}, f32[128,1024]{1,0:T(8,128)}, f32[1,32]{1,0:T(1,128)}, f32[32,512]{1,0:T(8,128)}, f32[32,512]{1,0:T(8,128)},...) custom-call(bf16[128,1024]{1,0:T(8,128)(2,1)} %refs_0_.1, ...), custom_call_target="tpu_custom_call" | custom-call | tf_op jit(solution)/shard_map/pallas_call | solution.py:1447
  94.8 2.9 %shard_map.239 = (bf16[128,1024]{1,0:T(8,128)(2,1)}, f32[128,1024]{1,0:T(8,128)}, f32[1,32]{1,0:T(1,128)}, f32[32,512]{1,0:T(8,128)}, f32[32,512]{1,0:T(8,128)},...) custom-call(bf16[128,1024]{1,0:T(8,128)(2,1)} %get-tuple-element.36., ...), custom_call_target="tpu_custom_call" | custom-call | tf_op jit(solution)/shard_map/pallas_call | solution.py:1474

commit v7 on v6

--- a/solution.py
+++ b/solution.py
@@ -480,14 +480,6 @@
 
     for i, name in enumerate(("cot", "lens", "rt", "tokens", "gain", "het", "wvg", "wog", "wr")):
         load(name, r[name + "_h"], r[name], R.ld_in.at[i])
-    stores = []
-
-    def store(*names):
-        for name in names:
-            cp = pltpu.make_async_copy(r[name], r[name + "_h"], R.ld_in.at[OUTPUTS.index(name)])
-            cp.start()
-            stores.append(cp)
-
     loaded("lens")
     l0 = R.lens[0, 0]
     b1 = l0 + R.lens[0, 1]
@@ -943,7 +935,11 @@
 
     def expert_grad_relay(i):
         second = 2 if i == 0 else 1
-        first_half(i, 1)
+
+        @pl.when(least == 0)
+        def _():
+            first_half(i, 1)
+
         arrived(R.eg_r.at[1, i], R.eg_s.at[1 + i])
         own = grad_at(i, second, c)
         own[...] = (own[...].astype(F32) + R.eg_r[1, i].astype(F32)).astype(BF16)
@@ -1022,6 +1018,22 @@
     for k in (1, 2, 0):
         expert_grad(1, k)
         expert_grad(0, k)
+    def sum_pairs():
+        arrived(R.pair_r.at[:, 0:3], R.pair_s.at[3])
+        for k in (1, 2, 0):
+            pair_sum(1, k)
+            pair_sum(0, k)
+
+    @pl.when(inner)
+    def _():
+        sum_pairs()
+        for i in range(2):
+            for n in range(2):
+                first_half(i, n)
+
+    hand_far(R.ra, RA, R.ra_s)
+    turned_here(0, 3, R.lt_s.at[0], R.lt_s.at[1])
+
     R.ghid_f[...] = R.cotb[pl.ds(times(z, C), C), :].astype(F32) + R.gh_s[z].astype(F32)
 
     arrived(R.gh_r.at[0:2], R.gh_sem.at[1])
@@ -1094,6 +1106,47 @@
     send_rows(R.rb, RQ, R.rq_s)
     send_rows(R.rb, RK, R.rk_s)
 
+
+    def turned_of(w):
+        return jnp.concatenate(
+            [R.ltr[s, :, w * LANES : (w + 1) * LANES] for s in range(2 * nd)], axis=1
+        )
+
+    def send_part(part, lanes):
+        for o in (far, fellow, near):
+            to_place(*part_sum(part, lanes), o)
+
+    def gate_rows(dst, rows_of, g0, s0, s1):
+        rows = slice(s0 * C, s1 * C)
+        for x in range(EA):
+            for h in range(H):
+                lo = x * HD + h * DH
+                gx = column(R.ra[rows, HD : HD + LANES], g0 + x * H + h)
+                dst[rows, lo : lo + DH] = gx * rows_of[rows, h * DH : (h + 1) * DH]
+
+    def gated_grad(w, gated, at):
+        left = turned_of(w)
+        for x in range(EA):
+            cols = slice(x * HD, (x + 1) * HD)
+            R.pb[:, at + x * HD : at + (x + 1) * HD] = mm(left, gated[:, cols]).astype(BF16)
+
+    PO, PV, PQ, PS = (
+        slice(0, EV),
+        slice(EV, 2 * EV),
+        slice(2 * EV, 2 * EV + 2 * HD),
+        slice(2 * EV + 2 * HD, 2 * EV + 2 * HD + LANES),
+    )
+    near_here(R.ra, RA, R.ra_s)
+    far_here(R.ra, RA, R.ra_s)
+    gate_rows(R.wo_b, R.ra, GATE, 0, 2 * nd)
+    turned_here(3, 4, R.lt_s.at[2], R.lt_s.at[3])
+    gated_grad(3, R.wo_b, 0)
+    o_run = functools.partial(run, *grad_sum(0, PO))
+    v_run = functools.partial(run, *grad_sum(1, PV))
+    o_run(1, 0)
+    o_run(1, 1)
+    out_run(2, 1)
+    out_run(3, 0)
     gproj = mm_t(R.rb[0:C, q0 : q0 + 2 * HD], R.wqk_b[...])
     standard = R.std_b[...]
     column_sum = jnp.sum(gproj * standard, axis=0, keepdims=True)
@@ -1106,57 +1159,12 @@
         )
         cp.start()
 
-    out_run(2, 1)
-    arrived(R.pair_r.at[:, 0:3], R.pair_s.at[3])
-    for k in (1, 2, 0):
-        pair_sum(1, k)
-        pair_sum(0, k)
-    first_half(0, 0)
-    first_half(1, 0)
-    hand_far(R.ra, RA, R.ra_s)
-    turned_here(0, 3, R.lt_s.at[0], R.lt_s.at[1])
-    near_here(R.ra, RA, R.ra_s)
-    far_here(R.ra, RA, R.ra_s)
-
-    def turned_of(w):
-        return jnp.concatenate(
-            [R.ltr[s, :, w * LANES : (w + 1) * LANES] for s in range(2 * nd)], axis=1
-        )
-
-    def send_part(part, lanes):
-        for o in (far, fellow, near):
-            to_place(*part_sum(part, lanes), o)
-
-    def gate_rows(dst, rows_of, g0, s0, s1):
-        rows = slice(s0 * C, s1 * C)
-        for x in range(EA):
-            for h in range(H):
-                lo = x * HD + h * DH
-                gx = column(R.ra[rows, HD : HD + LANES], g0 + x * H + h).astype(F32)
-                dst[rows, lo : lo + DH] = (
-                    gx * rows_of[rows, h * DH : (h + 1) * DH].astype(F32)
-                ).astype(BF16)
-
-    def gated_grad(w, gated, at):
-        left = turned_of(w)
-        for x in range(EA):
-            cols = slice(x * HD, (x + 1) * HD)
-            R.pb[:, at + x * HD : at + (x + 1) * HD] = mm(left, gated[:, cols]).astype(BF16)
-
-    PO, PV, PQ, PS = (
-        slice(0, EV),
-        slice(EV, 2 * EV),
-        slice(2 * EV, 2 * EV + 2 * HD),
-        slice(2 * EV + 2 * HD, 2 * EV + 2 * HD + LANES),
-    )
-    gate_rows(R.wo_b, R.ra, GATE, 0, 2 * nd)
-    turned_here(3, 4, R.lt_s.at[2], R.lt_s.at[3])
-    gated_grad(3, R.wo_b, 0)
-    o_run = functools.partial(run, *grad_sum(0, PO))
-    v_run = functools.partial(run, *grad_sum(1, PV))
-    o_run(1, 0)
-    o_run(1, 1)
-    out_run(3, 0)
+    @pl.when(least == 0)
+    def _():
+        sum_pairs()
+        first_half(0, 0)
+        first_half(1, 0)
+
     hand_near(R.rb, RV, R.rv_s, 0)
 
     inputs = R.tokens[...].astype(F32)
@@ -1181,7 +1189,6 @@
             R.small_b[...], R.wg_b[cols, :]
         )
 
-    store("gtok")
 
     o_run(2, 0)
     near_here(R.rb, RV, R.rv_s)
@@ -1192,10 +1199,9 @@
     gate_rows(R.wv_b, R.rb, 0, 6, 8)
     gated_grad(0, R.wv_b, EV)
     v_run(1, 0)
-    v_run(1, 1)
-    o_run(1, 2)
     hand_near(R.rb, RK, R.rk_s, 2)
     hand_near(R.rb, RQ, R.rq_s, 1)
+    v_run(1, 1)
     expert_grad_relay(0)
     expert_grad_relay(1)
     o_run(3, 0)
@@ -1214,8 +1220,11 @@
     small_h = mm(turned_of(2), R.rb[:, HD : HD + LANES])
     R.pb[:, PS] = jnp.where(lane_s < 2 * GATE, small_t, small_h).astype(BF16)
     send_part(1, PS)
+    o_run(1, 2)
     v_run(2, 0)
     v_run(2, 1)
+    v_run(3, 0)
+
     hand_far(R.rb, RQ, R.rq_s)
     hand_far(R.rb, RK, R.rk_s)
     for lanes, sem in ((RQ, R.rq_s), (RK, R.rk_s)):
@@ -1229,12 +1238,9 @@
         )
     send_part(0, PQ)
     v_run(1, 2)
-    v_run(3, 0)
-
     R.hid_f[...] += R.out_s[z].astype(F32)
     run_end(R.hid_f, out_sum[1], R.out_sem)
     R.mixed[...] = R.hid_f[...].astype(BF16)
-    store("mixed")
 
     arrived(R.gz.at[0 : nz - 1], R.tiny_r.at[3])
     for k in range(1, nz):
@@ -1245,7 +1251,6 @@
     shift = lax.rem(LANES - lax.rem(first, LANES), LANES)
     line_sum = pltpu.roll(jnp.broadcast_to(line_sum, (8, LANES)), shift, 1)
     R.ggain[...] = line_sum[0:1, 0:S]
-    store("ggain")
 
     own_rows = pl.ds(times(z, S), S)
 
@@ -1260,7 +1265,6 @@
     for i, (dst, lanes) in enumerate(((R.go, PO), (R.gv, PV))):
         dst[...] = R.pb[own_rows, lanes].astype(F32)
         run_end(dst, grad_sum(i, lanes)[1], R.pn_sem.at[i])
-    store("go", "gv")
     got = line_total(1, PS)
 
     def pick(width, source):
@@ -1285,11 +1289,9 @@
     R.gvg[...] = picked(pick(GATE, lambda b: b), got)
     R.gog[...] = picked(pick(GATE, lambda b: b + GATE), got)
     R.gr[...] = picked(got, pick(experts, router_lane))
-    store("gvg", "gog", "gr")
     got = line_total(0, PQ)
     R.gq[...] = got[:, 0:HD]
     R.gk[...] = got[:, HD : 2 * HD]
-    store("gq", "gk")
 
     for i, (buf, dst) in enumerate(((R.wdn_b, R.gdn), (R.wup_b, R.gup))):
         arrived(R.eg_r.at[0:2, i], R.eg_s.at[3 + i])
@@ -1299,10 +1301,7 @@
             for slot in (0, 2):
                 got = got + R.eg_r[slot, i, :, x * DH : (x + 1) * DH].astype(F32)
             dst[x] = got
-        store(("gdn", "gup")[i])
-
-    for cp in stores:
-        cp.wait()
+
     gather_end(R.cotb, R.cot_ss)
     gather_end(R.hidb, R.hid_ss)
     for buf, lanes, sem in (
@@ -1324,16 +1323,12 @@
         sent(R.pn.at[i, 0 : nz - 1], R.pn_sem.at[i, nz + 1])
 
 
-def settle_kernel(n, *refs):
-    src, dst, held, sems = refs[:n], refs[n : 2 * n], refs[2 * n : 3 * n], refs[-1]
-    ins = [pltpu.make_async_copy(src[i], held[i], sems.at[i]) for i in range(n)]
-    outs = [pltpu.make_async_copy(held[i], dst[i], sems.at[i]) for i in range(n)]
-    for cp in ins:
+def settle_kernel(*refs):
+    n = len(refs) // 2
+    copies = [pltpu.make_async_copy(refs[i], refs[n + i], refs[-1].at[i]) for i in range(n)]
+    for cp in copies:
         cp.start()
-    for there, back in zip(ins, outs):
-        there.wait()
-        back.start()
-    for cp in outs:
+    for cp in copies:
         cp.wait()
 
 
@@ -1417,7 +1412,8 @@
         return jax.ShapeDtypeStruct(shape, dtype)
 
     hbm = pl.BlockSpec(memory_space=pl.ANY)
-    names = in_hbm(SMALL) + WEIGHTS + in_hbm(OUTPUTS)
+    vmem = pl.BlockSpec(memory_space=pltpu.VMEM)
+    names = in_hbm(SMALL) + WEIGHTS + OUTPUTS
     results = (
         out(C, D, dtype=BF16),
         out(C, D),
@@ -1432,8 +1428,6 @@
         out(local, D // nd, DH),
         out(local, D // nd, DH),
     )
-    for name, x in zip(OUTPUTS, results):
-        s.vmem(name, x.shape, x.dtype)
     s.vmem("tokens", (C, D), BF16)
     s.vmem("cot", (C, D), BF16)
     s.add("lens", pltpu.SMEM((1, 2), jnp.int32))
@@ -1443,12 +1437,12 @@
     s.vmem("wvg", (EA * H, D), BF16)
     s.vmem("wog", (EA * H, D), BF16)
     s.vmem("wr", (experts, D), BF16)
-    s.sems("ld_in", len(OUTPUTS))
+    s.sems("ld_in", len(SMALL))
     outs = pl.pallas_call(
         functools.partial(layer_kernel, names + tuple(s.names), nd, nz, local),
-        out_shape=results,
+        out_shape=[pltpu.VMEM(x.shape, x.dtype) for x in results],
         in_specs=[hbm] * 15,
-        out_specs=[hbm] * len(OUTPUTS),
+        out_specs=[vmem] * len(OUTPUTS),
         scratch_shapes=s.shapes,
         compiler_params=pltpu.CompilerParams(
             collective_id=0, has_side_effects=True, vmem_limit_bytes=VMEM_LIMIT
@@ -1472,14 +1466,12 @@
     )
     outs = list(
         pl.pallas_call(
-            functools.partial(settle_kernel, len(outs)),
+            settle_kernel,
             out_shape=results,
-            in_specs=[hbm] * len(outs),
+            in_specs=[vmem] * len(outs),
             out_specs=[hbm] * len(outs),
-            scratch_shapes=[pltpu.VMEM(x.shape, x.dtype) for x in outs]
-            + [pltpu.SemaphoreType.DMA((len(outs),))],
-            compiler_params=pltpu.CompilerParams(vmem_limit_bytes=VMEM_LIMIT),
-        )(*outs)
+            scratch_shapes=[pltpu.SemaphoreType.DMA((len(outs),))],
+        )(*[pltpu.with_memory_space_constraint(x, pltpu.VMEM) for x in outs])
     )
     outs[2] = outs[2].reshape(S)
     for i in (7, 8):
@@ -1487,7 +1479,7 @@
     return tuple(outs)
 
 
-VMEM_LIMIT = 62 * 1024 * 1024
+VMEM_LIMIT = 58 * 1024 * 1024
 
 
 def fits(nd, nz, count, experts):

time: 98.8 us -> 97.3 us (0.985)
  Pallas kernels: 97 us -> 95 us
    pallas_call x1, Pallas kernels: 2.9 us -> 1.79 us  [fused_layer(): pl.pallas_call(settle_kernel, out_shape=results, in_specs=[vmem] * len(ou...]
where the time goes in v7:
time: 97.3 us; the launch traced here: 95.9 us
  Pallas kernels  95 us (98%)
    pallas_call x1, Pallas kernels, fused_layer(): pl.pallas_call(functools.partial(layer_kernel, names + tuple(s.names), nd...  93.2 us

profile of v7, /device:TPU:0, one launch (start us, length us, event | category | flops | bytes accessed | tf_op | source)
XLA Modules:
  0.0 95.9 jit_solution(16303798325056313209)
XLA Ops:
  0.7 93.2 %shard_map.238 = (bf16[128,1024]{1,0:T(8,128)(2,1)S(1)}, f32[128,1024]{1,0:T(8,128)S(1)}, f32[1,32]{1,0:T(1,128)S(1)}, f32[32,512]{1,0:T(8,128)S(1)}, f32[32,512...) custom-call(bf16[128,1024]{1,0:T(8,128)(2,1)} %refs_0_.1, ...), custom_call_target="tpu_custom_call" | custom-call | tf_op jit(solution)/shard_map/pallas_call | solution.py:1441
  93.9 1.8 %shard_map.239 = (bf16[128,1024]{1,0:T(8,128)(2,1)}, f32[128,1024]{1,0:T(8,128)}, f32[1,32]{1,0:T(1,128)}, f32[32,512]{1,0:T(8,128)}, f32[32,512]{1,0:T(8,128)},...) custom-call(bf16[128,1024]{1,0:T(8,128)(2,1)S(1)} %get-tuple-element, ...), custom_call_target="tpu_custom_call" | custom-call | tf_op jit(solution)/shard_map/pallas_call | solution.py:1468

commit v8 on v7

--- a/solution.py
+++ b/solution.py
@@ -1013,7 +1013,6 @@
     @pl.when(inner)
     def _():
         relay_back(near, 1)
-        relay_back(fellow, 0)
 
     for k in (1, 2, 0):
         expert_grad(1, k)
@@ -1026,11 +1025,13 @@
 
     @pl.when(inner)
     def _():
+        relay_back(fellow, 0)
         sum_pairs()
         for i in range(2):
             for n in range(2):
                 first_half(i, n)
 
+    out_run(1, 1)
     hand_far(R.ra, RA, R.ra_s)
     turned_here(0, 3, R.lt_s.at[0], R.lt_s.at[1])
 
@@ -1045,7 +1046,6 @@
     add_back(jnp.where(inner, fellow, far))
 
     arrived(R.glog_r.at[0 : nz - 1], R.tiny_r.at[1])
-    out_run(1, 1)
     R.glog_r[z] = R.glog_s[z]
     R.ghid_b[...] = R.ghid_f[...].astype(BF16)
     put_turned(R.ghid_f[...], 3)
@@ -1138,6 +1138,7 @@
     )
     near_here(R.ra, RA, R.ra_s)
     far_here(R.ra, RA, R.ra_s)
+    out_run(2, 1)
     gate_rows(R.wo_b, R.ra, GATE, 0, 2 * nd)
     turned_here(3, 4, R.lt_s.at[2], R.lt_s.at[3])
     gated_grad(3, R.wo_b, 0)
@@ -1145,7 +1146,6 @@
     v_run = functools.partial(run, *grad_sum(1, PV))
     o_run(1, 0)
     o_run(1, 1)
-    out_run(2, 1)
     out_run(3, 0)
     gproj = mm_t(R.rb[0:C, q0 : q0 + 2 * HD], R.wqk_b[...])
     standard = R.std_b[...]
@@ -1202,8 +1202,6 @@
     hand_near(R.rb, RK, R.rk_s, 2)
     hand_near(R.rb, RQ, R.rq_s, 1)
     v_run(1, 1)
-    expert_grad_relay(0)
-    expert_grad_relay(1)
     o_run(3, 0)
     total = R.gp[0]
     sent(R.gp.at[1:], R.tiny_s.at[2])
@@ -1221,6 +1219,8 @@
     R.pb[:, PS] = jnp.where(lane_s < 2 * GATE, small_t, small_h).astype(BF16)
     send_part(1, PS)
     o_run(1, 2)
+    expert_grad_relay(0)
+    expert_grad_relay(1)
     v_run(2, 0)
     v_run(2, 1)
     v_run(3, 0)

time: 97.3 us -> 97.3 us (level)
  no operation moved by 1% of the time
where the time goes in v8:
time: 97.3 us; the launch traced here: 95.9 us
  Pallas kernels  95 us (98%)
    pallas_call x1, Pallas kernels, fused_layer(): pl.pallas_call(functools.partial(layer_kernel, names + tuple(s.names), nd...  93.2 us

profile of v8, /device:TPU:0, one launch (start us, length us, event | category | flops | bytes accessed | tf_op | source)
XLA Modules:
  0.0 95.9 jit_solution(14430722720907869806)
XLA Ops:
  0.7 93.2 %shard_map.238 = (bf16[128,1024]{1,0:T(8,128)(2,1)S(1)}, f32[128,1024]{1,0:T(8,128)S(1)}, f32[1,32]{1,0:T(1,128)S(1)}, f32[32,512]{1,0:T(8,128)S(1)}, f32[32,512...) custom-call(bf16[128,1024]{1,0:T(8,128)(2,1)} %refs_0_.1, ...), custom_call_target="tpu_custom_call" | custom-call | tf_op jit(solution)/shard_map/pallas_call | solution.py:1441
  93.9 1.8 %shard_map.239 = (bf16[128,1024]{1,0:T(8,128)(2,1)}, f32[128,1024]{1,0:T(8,128)}, f32[1,32]{1,0:T(1,128)}, f32[32,512]{1,0:T(8,128)}, f32[32,512]{1,0:T(8,128)},...) custom-call(bf16[128,1024]{1,0:T(8,128)(2,1)S(1)} %get-tuple-element, ...), custom_call_target="tpu_custom_call" | custom-call | tf_op jit(solution)/shard_map/pallas_call | solution.py:1468

commit v9 on v7

--- a/solution.py
+++ b/solution.py
@@ -748,9 +748,11 @@
         sent(buf.at[0 : 7 * C, lanes], sem.at[0])
 
     put_turned(R.tokens[...], 0)
-    put_turned(R.normed_b[...], 1)
-    put_turned(R.hid_f[...], 2)
-    send_turned(0, 3, R.lt_s.at[0], R.lt_s.at[1])
+    put_turned(R.hid_f[...], 1)
+    send_turned(0, 2, R.lt_s.at[0], R.lt_s.at[1])
+    R.nrm[0:C, :] = R.normed_b[...]
+    RN = slice(0, D)
+    send_rows(R.nrm, RN, R.nrm_s)
     R.ra[0:C, 0:HD] = R.att_b[...].astype(BF16)
     R.ra[0:C, HD : HD + LANES] = gates.astype(BF16)
     RA = slice(0, HD + LANES)
@@ -850,8 +852,9 @@
         @pl.when(k == 2)
         def _():
             hand_near(R.ra, RA, R.ra_s, 2)
-
-        @pl.when((k == 2) & (least == 0))
+            hand_near(R.nrm, RN, R.nrm_s, 1)
+
+        @pl.when((k == 1) & (least == 0))
         def _():
             there = pl.ds(times(near, C), C)
             for b in range(2):
@@ -935,11 +938,6 @@
 
     def expert_grad_relay(i):
         second = 2 if i == 0 else 1
-
-        @pl.when(least == 0)
-        def _():
-            first_half(i, 1)
-
         arrived(R.eg_r.at[1, i], R.eg_s.at[1 + i])
         own = grad_at(i, second, c)
         own[...] = (own[...].astype(F32) + R.eg_r[1, i].astype(F32)).astype(BF16)
@@ -975,9 +973,10 @@
     out_run = functools.partial(run, *out_sum)
 
     def grad_sum(i, lanes):
+        held = slice(0, EV) if i == 0 else slice((i - 1) * EV // 2, i * EV // 2)
         return (
             lambda d: R.pb.at[d * S : (d + 1) * S, lanes],
-            lambda d: R.pn.at[i, d],
+            lambda d: R.pn.at[min(i, 1), d, :, held],
             R.pn_sem.at[i, nz + 1],
             R.pn_sem.at[i],
         )
@@ -1032,7 +1031,8 @@
                 first_half(i, n)
 
     hand_far(R.ra, RA, R.ra_s)
-    turned_here(0, 3, R.lt_s.at[0], R.lt_s.at[1])
+    turned_here(0, 2, R.lt_s.at[0], R.lt_s.at[1])
+    hand_far(R.nrm, RN, R.nrm_s)
 
     R.ghid_f[...] = R.cotb[pl.ds(times(z, C), C), :].astype(F32) + R.gh_s[z].astype(F32)
 
@@ -1048,8 +1048,8 @@
     out_run(1, 1)
     R.glog_r[z] = R.glog_s[z]
     R.ghid_b[...] = R.ghid_f[...].astype(BF16)
-    put_turned(R.ghid_f[...], 3)
-    send_turned(3, 4, R.lt_s.at[2], R.lt_s.at[3])
+    put_turned(R.ghid_f[...], 2)
+    send_turned(2, 3, R.lt_s.at[2], R.lt_s.at[3])
     out_run(2, 0)
 
     gates = R.gate_b[...]
@@ -1088,7 +1088,6 @@
     RV = slice(0, HD + LANES)
     send_rows(R.rb, RV, R.rv_s, (1, 2, 3))
 
-    q0 = HD + LANES
     for h in range(H):
         hs = slice(h * DH, (h + 1) * DH)
         low = R.gatt_b[:, hs]
@@ -1096,15 +1095,27 @@
         prob = R.prob_b[h]
         centre = jnp.sum(prob * gsh, axis=-1, keepdims=True)
         gs = (prob * (gsh - centre)).astype(BF16)
-        R.rb[0:C, q0 + h * DH : q0 + (h + 1) * DH] = rot_back(
+        R.qk_b[:, hs] = rot_back(
             mm(gs, R.k_b[:, hs]) * scale
         ).astype(BF16)
-        R.rb[0:C, q0 + HD + h * DH : q0 + HD + (h + 1) * DH] = rot_back(
+        R.qk_b[:, HD + h * DH : HD + (h + 1) * DH] = rot_back(
             tmm(gs, R.q_b[:, hs])
         ).astype(BF16)
-    RQ, RK = slice(q0, q0 + HD), slice(q0 + HD, q0 + 2 * HD)
-    send_rows(R.rb, RQ, R.rq_s)
-    send_rows(R.rb, RK, R.rk_s)
+    place = p * 2 + c
+
+    def columns_of(j):
+        return pl.ds(times(j, LANES), LANES)
+
+    for k, dc in plane_all:
+        slot = 2 * k + dc
+        remote(
+            R.qk_b.at[:, columns_of(plane(k) * 2 + side(dc))],
+            R.qc.at[slot * C : (slot + 1) * C],
+            R.qk_s.at[0],
+            R.qk_s.at[1],
+            dev(plane(k), z, side(dc)),
+        ).start()
+    R.qc[0:C, :] = R.qk_b[:, columns_of(place)]
 
 
     def turned_of(w):
@@ -1130,24 +1141,24 @@
             cols = slice(x * HD, (x + 1) * HD)
             R.pb[:, at + x * HD : at + (x + 1) * HD] = mm(left, gated[:, cols]).astype(BF16)
 
-    PO, PV, PQ, PS = (
-        slice(0, EV),
-        slice(EV, 2 * EV),
-        slice(2 * EV, 2 * EV + 2 * HD),
-        slice(2 * EV + 2 * HD, 2 * EV + 2 * HD + LANES),
-    )
+    PO, PV, PS = slice(0, EV), slice(EV, 2 * EV), slice(2 * EV, 2 * EV + LANES)
     near_here(R.ra, RA, R.ra_s)
     far_here(R.ra, RA, R.ra_s)
     gate_rows(R.wo_b, R.ra, GATE, 0, 2 * nd)
-    turned_here(3, 4, R.lt_s.at[2], R.lt_s.at[3])
-    gated_grad(3, R.wo_b, 0)
+    turned_here(2, 3, R.lt_s.at[2], R.lt_s.at[3])
+    gated_grad(2, R.wo_b, 0)
     o_run = functools.partial(run, *grad_sum(0, PO))
-    v_run = functools.partial(run, *grad_sum(1, PV))
+    halves = (slice(EV, EV + EV // 2), slice(EV + EV // 2, 2 * EV))
+
+    def v_run(k, n):
+        for i, lanes in enumerate(halves):
+            run(*grad_sum(1 + i, lanes), k, n)
+
     o_run(1, 0)
     o_run(1, 1)
     out_run(2, 1)
     out_run(3, 0)
-    gproj = mm_t(R.rb[0:C, q0 : q0 + 2 * HD], R.wqk_b[...])
+    gproj = mm_t(R.qk_b[...], R.wqk_b[...])
     standard = R.std_b[...]
     column_sum = jnp.sum(gproj * standard, axis=0, keepdims=True)
     for b in range(D // LANES):
@@ -1162,9 +1173,12 @@
     @pl.when(least == 0)
     def _():
         sum_pairs()
-        first_half(0, 0)
-        first_half(1, 0)
-
+        for i in range(2):
+            for n in range(2):
+                first_half(i, n)
+
+    expert_grad_relay(0)
+    expert_grad_relay(1)
     hand_near(R.rb, RV, R.rv_s, 0)
 
     inputs = R.tokens[...].astype(F32)
@@ -1199,11 +1213,18 @@
     gate_rows(R.wv_b, R.rb, 0, 6, 8)
     gated_grad(0, R.wv_b, EV)
     v_run(1, 0)
-    hand_near(R.rb, RK, R.rk_s, 2)
-    hand_near(R.rb, RQ, R.rq_s, 1)
+    near_here(R.nrm, RN, R.nrm_s)
+    far_here(R.nrm, RN, R.nrm_s)
+    arrived(R.qc.at[C:], R.qk_s.at[1])
+    turned = tmm(R.qc[...], R.nrm[...])
+    for b in range(D // LANES):
+        t = turned[:, b * LANES : (b + 1) * LANES].T.astype(BF16)
+        for q in range(LANES // S):
+            i = (b * LANES) // S + q
+            pp, zz, cc = i // (2 * nz), (i % (2 * nz)) // 2, i % 2
+            at = (pp * 2 + cc) * S
+            R.qp[zz, at : at + S, :] = t[q * S : (q + 1) * S, :]
     v_run(1, 1)
-    expert_grad_relay(0)
-    expert_grad_relay(1)
     o_run(3, 0)
     total = R.gp[0]
     sent(R.gp.at[1:], R.tiny_s.at[2])
@@ -1217,27 +1238,32 @@
 
     lane_s = iota((SL, LANES), 1)
     small_t = mm(turned_of(0), R.rb[:, HD : HD + LANES])
-    small_h = mm(turned_of(2), R.rb[:, HD : HD + LANES])
+    small_h = mm(turned_of(1), R.rb[:, HD : HD + LANES])
     R.pb[:, PS] = jnp.where(lane_s < 2 * GATE, small_t, small_h).astype(BF16)
-    send_part(1, PS)
+    send_part(0, PS)
+    v_run(2, 0)
+    for o in (far, fellow, near):
+        to_place(lambda d: R.qp.at[d], lambda d: R.qr.at[d], R.qk_s.at[2], R.qk_s.at[3], o)
+    v_run(2, 1)
     o_run(1, 2)
-    v_run(2, 0)
-    v_run(2, 1)
     v_run(3, 0)
 
-    hand_far(R.rb, RQ, R.rq_s)
-    hand_far(R.rb, RK, R.rk_s)
-    for lanes, sem in ((RQ, R.rq_s), (RK, R.rk_s)):
-        near_here(R.rb, lanes, sem)
-        far_here(R.rb, lanes, sem)
-    left = turned_of(1)
-    for b in range(2):
-        lo = q0 + b * HD
-        R.pb[:, 2 * EV + b * HD : 2 * EV + (b + 1) * HD] = mm(left, R.rb[:, lo : lo + HD]).astype(
-            BF16
-        )
-    send_part(0, PQ)
     v_run(1, 2)
+    arrived(R.qr.at[0 : nz - 1], R.qk_s.at[3])
+    got = R.qp[z].astype(F32)
+    for k in range(1, nz):
+        got = got + R.qr[line(k)].astype(F32)
+    R.qs[...] = got
+    for k, dc in plane_all:
+        remote(
+            R.qs.at[pl.ds(times(plane(k) * 2 + side(dc), S), S)],
+            R.qf.at[:, columns_of(place)],
+            R.qk_s.at[4],
+            R.qk_s.at[5],
+            dev(plane(k), z, side(dc)),
+        ).start()
+    R.qf[:, columns_of(place)] = R.qs[pl.ds(times(place, S), S), :]
+
     R.hid_f[...] += R.out_s[z].astype(F32)
     run_end(R.hid_f, out_sum[1], R.out_sem)
     R.mixed[...] = R.hid_f[...].astype(BF16)
@@ -1262,10 +1288,13 @@
             got = got + slots(line(k))[...].astype(F32)
         return got
 
-    for i, (dst, lanes) in enumerate(((R.go, PO), (R.gv, PV))):
-        dst[...] = R.pb[own_rows, lanes].astype(F32)
-        run_end(dst, grad_sum(i, lanes)[1], R.pn_sem.at[i])
-    got = line_total(1, PS)
+    R.go[...] = R.pb[own_rows, PO].astype(F32)
+    run_end(R.go, grad_sum(0, PO)[1], R.pn_sem.at[0])
+    R.gv[...] = R.pb[own_rows, PV].astype(F32)
+    for i, lanes in enumerate(halves):
+        half = R.gv.at[:, lanes.start - EV : lanes.stop - EV]
+        run_end(half, grad_sum(1 + i, lanes)[1], R.pn_sem.at[1 + i])
+    got = line_total(0, PS)
 
     def pick(width, source):
         a, b = iota((width, LANES), 1), iota((width, LANES), 0)
@@ -1289,9 +1318,9 @@
     R.gvg[...] = picked(pick(GATE, lambda b: b), got)
     R.gog[...] = picked(pick(GATE, lambda b: b + GATE), got)
     R.gr[...] = picked(got, pick(experts, router_lane))
-    got = line_total(0, PQ)
-    R.gq[...] = got[:, 0:HD]
-    R.gk[...] = got[:, HD : 2 * HD]
+    arrived(R.qs.at[0 : (2 * nd - 1) * S], R.qk_s.at[5])
+    R.gq[...] = R.qf[:, 0:HD]
+    R.gk[...] = R.qf[:, HD : 2 * HD]
 
     for i, (buf, dst) in enumerate(((R.wdn_b, R.gdn), (R.wup_b, R.gup))):
         arrived(R.eg_r.at[0:2, i], R.eg_s.at[3 + i])
@@ -1307,8 +1336,7 @@
     for buf, lanes, sem in (
         (R.ra, RA, R.ra_s),
         (R.rb, RV, R.rv_s),
-        (R.rb, RQ, R.rq_s),
-        (R.rb, RK, R.rk_s),
+        (R.nrm, RN, R.nrm_s),
     ):
         rows_sent(buf, lanes, sem)
     sent(R.maskb.at[0 : nz - 1], R.tiny_s.at[0])
@@ -1316,11 +1344,15 @@
     sent(R.gz.at[0 : nz - 1], R.tiny_s.at[3])
     sent(R.gh_r.at[0 : nz - 1], R.gh_sem.at[0])
     sent(R.out_r.at[0 : nz - 1], R.out_sem.at[nz + 1])
+    sent(R.qc.at[C:], R.qk_s.at[0])
+    sent(R.qr.at[0 : nz - 1], R.qk_s.at[2])
+    sent(R.qs.at[0 : (2 * nd - 1) * S], R.qk_s.at[4])
     sent(R.pair_r, R.pair_s.at[0])
     sent(R.eg_r, R.eg_s.at[0])
     sent(R.pr.at[0 : nz - 1], R.p_sem.at[0])
+    sent(R.pn.at[0, 0 : nz - 1], R.pn_sem.at[0, nz + 1])
     for i in range(2):
-        sent(R.pn.at[i, 0 : nz - 1], R.pn_sem.at[i, nz + 1])
+        sent(R.pn.at[1, 0 : nz - 1, :, 0 : EV // 2], R.pn_sem.at[1 + i, nz + 1])
 
 
 def settle_kernel(*refs):
@@ -1345,7 +1377,7 @@
     EV = EA * HD
     S = D // (nd * nz * 2)
     SL = S * nz
-    PW = 2 * EV + 2 * HD + LANES
+    PW = 2 * EV + LANES
     s = Scratch()
     s.vmem("wqk_b", (D, 2 * HD), BF16)
     s.vmem("wv_b", (D, EV), BF16)
@@ -1369,10 +1401,17 @@
     s.vmem("att_b", (C, HD), F32)
     s.vmem("mix_b", (C, EV), BF16)
     s.vmem("hid_f", (C, D), F32)
-    s.vmem("lt", (D, 4 * LANES), BF16)
-    s.vmem("ltr", (2 * nd, SL, 4 * LANES), BF16)
+    s.vmem("lt", (D, 3 * LANES), BF16)
+    s.vmem("ltr", (2 * nd, SL, 3 * LANES), BF16)
+    s.vmem("nrm", (2 * nd * C, D), BF16)
+    s.vmem("qk_b", (C, 2 * HD), BF16)
+    s.vmem("qc", (2 * nd * C, LANES), BF16)
+    s.vmem("qp", (nz, D // nz, LANES), BF16)
+    s.vmem("qr", (nz, D // nz, LANES), BF16)
+    s.vmem("qs", (D // nz, LANES), F32)
+    s.vmem("qf", (S, 2 * HD), F32)
     s.vmem("ra", (2 * nd * C, HD + LANES), BF16)
-    s.vmem("rb", (2 * nd * C, 3 * HD + LANES), BF16)
+    s.vmem("rb", (2 * nd * C, HD + LANES), BF16)
     s.vmem("gact", (nz * C, EF), BF16)
     s.vmem("gra", (nz * C, EF), BF16)
     for name in ("gh_s", "gh_r", "out_s"):
@@ -1400,13 +1439,13 @@
         s.sems(name, nz + 1)
     for name in ("cot_rs", "hid_rs", "tiny_s", "tiny_r", "lt_s", "gh_sem", "pair_s"):
         s.sems(name, 4)
-    for name in ("ra_s", "rv_s", "rq_s", "rk_s"):
+    for name in ("ra_s", "rv_s", "nrm_s", "qk_s"):
         s.sems(name, 6)
     s.sems("w_s", 2)
     s.sems("eg_s", 5)
     s.sems("p_sem", 3)
     s.sems("out_sem", nz + 2)
-    s.sems("pn_sem", 2, nz + 2)
+    s.sems("pn_sem", 3, nz + 2)
 
     def out(*shape, dtype=F32):
         return jax.ShapeDtypeStruct(shape, dtype)
@@ -1490,6 +1529,7 @@
         and nz == 4
         and nd == 4
         and own_e % 4 == 0
+        and H * DH == nd * LANES
         and D % (nd * nz * 2 * 16) == 0
         and LANES % (D // (nd * nz * 2)) == 0
         and 2 * EA * H + nz * pad_e <= LANES

time: 97.3 us -> 96 us (0.987)
  no operation moved by 1% of the time
where the time goes in v9:
time: 96 us; the launch traced here: 95.4 us
  Pallas kernels  94.5 us (98%)
    pallas_call x1, Pallas kernels, fused_layer(): pl.pallas_call(functools.partial(layer_kernel, names + tuple(s.names), nd...  92.8 us

profile of v9, /device:TPU:0, one launch (start us, length us, event | category | flops | bytes accessed | tf_op | source)
XLA Modules:
  0.0 95.4 jit_solution(16758235192558631671)
XLA Ops:
  0.7 92.8 %shard_map.238 = (bf16[128,1024]{1,0:T(8,128)(2,1)S(1)}, f32[128,1024]{1,0:T(8,128)S(1)}, f32[1,32]{1,0:T(1,128)S(1)}, f32[32,512]{1,0:T(8,128)S(1)}, f32[32,512...) custom-call(bf16[128,1024]{1,0:T(8,128)(2,1)} %refs_0_.1, ...), custom_call_target="tpu_custom_call" | custom-call | tf_op jit(solution)/shard_map/pallas_call | solution.py:1480
  93.4 1.8 %shard_map.239 = (bf16[128,1024]{1,0:T(8,128)(2,1)}, f32[128,1024]{1,0:T(8,128)}, f32[1,32]{1,0:T(1,128)}, f32[32,512]{1,0:T(8,128)}, f32[32,512]{1,0:T(8,128)},...) custom-call(bf16[128,1024]{1,0:T(8,128)(2,1)S(1)} %get-tuple-element, ...), custom_call_target="tpu_custom_call" | custom-call | tf_op jit(solution)/shard_map/pallas_call | solution.py:1507

commit v10 on v9

--- a/solution.py
+++ b/solution.py
@@ -480,6 +480,8 @@
 
     for i, name in enumerate(("cot", "lens", "rt", "tokens", "gain", "het", "wvg", "wog", "wr")):
         load(name, r[name + "_h"], r[name], R.ld_in.at[i])
+    load("qk", R.wq, R.wqk_b.at[:, 0:HD], R.ld.at[0])
+    load("qk", R.wk, R.wqk_b.at[:, HD : 2 * HD], R.ld.at[0])
     loaded("lens")
     l0 = R.lens[0, 0]
     b1 = l0 + R.lens[0, 1]
@@ -497,8 +499,6 @@
     for b in range(D // LANES):
         cols = slice(b * LANES, (b + 1) * LANES)
         R.cotb[pl.ds(times(z, C), C), cols] = (R.cot[:, cols].astype(F32) * live_f).astype(BF16)
-    load("qk", R.wq, R.wqk_b.at[:, 0:HD], R.ld.at[0])
-    load("qk", R.wk, R.wqk_b.at[:, HD : 2 * HD], R.ld.at[0])
     load("v", R.wv, R.wv_b, R.ld.at[1])
     for i in range(local):
         col = times(c * local + i, DH)
@@ -578,11 +578,6 @@
     to_v = jnp.where(s_row == s_col, 1.0, 0.0).astype(BF16)
     to_o = jnp.where(s_row + GATE == s_col, 1.0, 0.0).astype(BF16)
     R.wg_b[...] = (tmm(R.wvg[...], to_v) + tmm(R.wog[...], to_o)).astype(BF16)
-    experts = R.wr.shape[0]
-    r_row, r_col = iota((experts, LANES), 0), iota((experts, LANES), 1)
-    to_r = jnp.where((r_row == r_col + z * own_e) & (r_col < own_e), 1.0, 0.0).astype(BF16)
-    R.wrl_b[...] = tmm(R.wr[...], to_r).astype(BF16)
-
     half = lax.rem(lane, DH // 2).astype(F32)
     angle = position * jnp.exp(half * (-2.0 / DH * math.log(rope_base)))
     cosine = jnp.cos(angle)
@@ -630,8 +625,10 @@
     landed(R.wv_b, R.ld.at[1])
     gates = R.gate_b[...]
     total = [None] * H
+    for b in range(2):
+        cols = slice(b * EV // 2, (b + 1) * EV // 2)
+        R.val_b[:, cols] = mm(R.tokens[...], R.wv_b[:, cols])
     for x in range(EA):
-        R.val_b[:, x * HD : (x + 1) * HD] = mm(R.tokens[...], R.wv_b[:, x * HD : (x + 1) * HD])
         for h in range(H):
             lo = x * HD + h * DH
             term = column(gates, x * H + h) * R.val_b[:, lo : lo + DH]
@@ -655,13 +652,15 @@
             ).astype(BF16)
     landed(R.wo_b, R.ld.at[4])
     half_d = D // 2
-    for b in range(2):
-        cols = slice(b * half_d, (b + 1) * half_d)
-        hidden = R.tokens[:, cols].astype(F32) + mm_t(R.mix_b[...], R.wo_b[cols, :])
-        R.hid_f[:, cols] = hidden
-        R.hidb[pl.ds(times(z, C), C), cols] = hidden.astype(BF16)
+    hidden = R.tokens[...].astype(F32) + mm_t(R.mix_b[...], R.wo_b[...])
+    R.hid_f[...] = hidden
+    R.hidb[pl.ds(times(z, C), C), :] = hidden.astype(BF16)
     gather_own(R.hidb, R.hid_ss, R.hid_rs)
     gather_step(R.cotb, R.cot_ss, R.cot_rs, 1)
+    experts = R.wr.shape[0]
+    r_row, r_col = iota((experts, LANES), 0), iota((experts, LANES), 1)
+    to_r = jnp.where((r_row == r_col + z * own_e) & (r_col < own_e), 1.0, 0.0).astype(BF16)
+    R.wrl_b[...] = tmm(R.wr[...], to_r).astype(BF16)
 
     def put_turned(x, w):
         for b in range(D // LANES):

time: 96 us -> 95.2 us (level)
  no operation moved by 1% of the time
where the time goes in v10:
time: 95.2 us; the launch traced here: 95 us
  Pallas kernels  94.2 us (99%)
    pallas_call x1, Pallas kernels, fused_layer(): pl.pallas_call(functools.partial(layer_kernel, names + tuple(s.names), nd...  92.4 us

profile of v10, /device:TPU:0, one launch (start us, length us, event | category | flops | bytes accessed | tf_op | source)
XLA Modules:
  0.0 95.0 jit_solution(13053486835711117419)
XLA Ops:
  0.7 92.4 %shard_map.238 = (bf16[128,1024]{1,0:T(8,128)(2,1)S(1)}, f32[128,1024]{1,0:T(8,128)S(1)}, f32[1,32]{1,0:T(1,128)S(1)}, f32[32,512]{1,0:T(8,128)S(1)}, f32[32,512...) custom-call(bf16[128,1024]{1,0:T(8,128)(2,1)} %refs_0_.1, ...), custom_call_target="tpu_custom_call" | custom-call | tf_op jit(solution)/shard_map/pallas_call | solution.py:1479
  93.0 1.8 %shard_map.239 = (bf16[128,1024]{1,0:T(8,128)(2,1)}, f32[128,1024]{1,0:T(8,128)}, f32[1,32]{1,0:T(1,128)}, f32[32,512]{1,0:T(8,128)}, f32[32,512]{1,0:T(8,128)},...) custom-call(bf16[128,1024]{1,0:T(8,128)(2,1)S(1)} %get-tuple-element, ...), custom_call_target="tpu_custom_call" | custom-call | tf_op jit(solution)/shard_map/pallas_call | solution.py:1506
